TPU v7x, 32 devices: a whole 2x2x4 slice. The times are simulated.
32 devices in a mesh: space: 16 (over z, y, x), chan: 2 (over core).
Axes of the slice: x: 2, y: 2, z: 4, core: 2. Of those that a mesh axis runs over, the one named last changes fastest.
Arguments:
- features: bfloat16 [128, 512, 128], P('space', None, 'chan'), may hold values from -6 to 6
- heights: int32 [128, 64], P('space'), may hold values from 0 to 8
- neighbours: int32 [16, 26], P('space'), may hold values from -1 to 15, as said below
- w_conv: bfloat16 [27, 128, 128], replicated, may hold values from -0.109375 to 0.109375
- w_down: bfloat16 [8, 128, 256], replicated, may hold values from -0.1875 to 0.1875
- cotangent: bfloat16 [16, 512, 256], P('space'), may hold values from -12 to 12
Outputs:
- coarse: bfloat16 [16, 512, 256], P('space', None, 'chan')
- grad_conv: float32 [27, 128, 128], P(None, 'chan')
- grad_down: float32 [8, 128, 256], P(None, None, 'chan')
- grad_features: bfloat16 [128, 512, 128], P('space', None, 'chan')
Inputs may be any that keep to these rules, and one draw needn't show every extreme that they name: neighbours[s, k] is the block at offset d_k from block s (the 26 offsets of the finite set (-1,0,1)^3 without the anchor, lexicographic in (x, y, z)), or -1 where no block is there; if neighbours[s, k] = q then neighbours[q, 25 - k] = s; distinct offsets name distinct blocks; blocks lie on a strip two positions wide and two high and are numbered in order of x, then y, then z, so that every neighbour q of s has 1 <= |q - s| <= 7.
All inputs are finite; a program needn't handle non-finite values.
Results may differ from a plain program's by a relative error of at most 0.005.
Values may be sent and summed in bfloat16 or wider, within the bound.
No kernel may reach another device: no remote copies, remote signals or barrier semaphores. Data moves between devices by JAX's collectives and lax.ppermute only.
A program may use at most 320 MiB of HBM per device.

v0:
```python
import jax
import jax.numpy as jnp
from jax import lax
from jax.experimental import pallas as pl
from jax.experimental.pallas import tpu as pltpu
from jax.sharding import PartitionSpec as P

OFFSETS = [
    (along_x, along_y, along_z)
    for along_x in (-1, 0, 1)
    for along_y in (-1, 0, 1)
    for along_z in (-1, 0, 1)
]
DIRECTIONS = [offset for offset in OFFSETS if offset != (0, 0, 0)]
FILL_ORDER = sorted(range(26), key=lambda k: (abs(DIRECTIONS[k][2]), k))
INACTIVE = -1e30
F32 = jnp.float32
BF16 = jnp.bfloat16


def vmem():
    return pl.BlockSpec(memory_space=pltpu.VMEM)


def smem():
    return pl.BlockSpec(memory_space=pltpu.SMEM)


def hbm():
    return pl.BlockSpec(memory_space=pltpu.HBM)


def kernel_call(body, outs, specs, out_specs, scratch=(), flops=0, mib=16):
    call = pl.pallas_call(
        body,
        out_shape=outs,
        in_specs=specs,
        out_specs=out_specs,
        scratch_shapes=list(scratch),
        compiler_params=pltpu.CompilerParams(vmem_limit_bytes=mib * 1024 * 1024),
        cost_estimate=pl.CostEstimate(flops=flops, bytes_accessed=1 << 22, transcendentals=0),
    )

    def run(*operands):
        placed = []
        for spec, operand in zip(specs, operands):
            if spec.memory_space == pltpu.HBM:
                operand = pltpu.with_memory_space_constraint(operand, pltpu.HBM)
            placed.append(operand)
        return call(*placed)

    return run


def start_all(pairs, arrived):
    copies = [
        pltpu.make_async_copy(source, target, arrived.at[i])
        for i, (source, target) in enumerate(pairs)
    ]
    for copy in copies:
        copy.start()
    return copies


def swap_halves(rows):
    return pltpu.roll(rows, 64, 1)


def low_lanes(rows):
    return lax.broadcasted_iota(jnp.int32, rows.shape, 1) < 64


def filled_voxels(heights_ref):
    columns = lax.broadcasted_iota(jnp.int32, (64, 512), 0)
    voxels = lax.broadcasted_iota(jnp.int32, (64, 512), 1)
    spread = (voxels // 8 == columns).astype(F32)
    tall = jnp.dot(heights_ref[...].astype(F32), spread, preferred_element_type=F32)
    level = lax.broadcasted_iota(jnp.int32, tall.shape, 1) % 8
    return (level.astype(F32) < tall).astype(F32)


def fill_slots(rows_ref, near_ref, slots_ref, start=0, faces=True):
    for k, (dx, dy, dz) in enumerate(DIRECTIONS):
        block = near_ref[0, k]
        xh = 7 if dx == 1 else 0
        y = 15 if dy == 1 else 0
        z = 15 if dz == 1 else 0
        if not faces and (dx, dy, dz).count(0) == 2:
            continue

        @pl.when(block >= 0)
        def _(dx=dx, dy=dy, dz=dz, xh=xh, y=y, z=z, block=block):
            zeros = [d == 0 for d in (dx, dy, dz)]
            if zeros == [False, True, True]:
                plane = rows_ref[xh * 256 : xh * 256 + 256, :]
                first, second = plane[:128], plane[128:]
                if dx == -1:
                    second = swap_halves(second)
                else:
                    first = swap_halves(first)
                region = jnp.where(low_lanes(first), first, second)
            elif zeros == [True, False, True]:
                region = jnp.concatenate(
                    [rows_ref[x * 256 + y * 16 : x * 256 + y * 16 + 16, :] for x in range(8)]
                )
            elif zeros == [True, True, False]:
                region = rows_ref[pl.ds(z, 128, stride=16), :]
            elif zeros == [False, False, True]:
                region = rows_ref[xh * 256 + y * 16 : xh * 256 + y * 16 + 16, :]
            elif zeros == [False, True, False]:
                region = rows_ref[pl.ds(xh * 256 + z, 16, stride=16), :]
            elif zeros == [True, False, False]:
                line = rows_ref[pl.ds(y * 16 + z, 8, stride=256), :]
                region = jnp.concatenate([line, line])
            else:
                at = xh * 256 + y * 16 + z
                region = jnp.broadcast_to(rows_ref[at : at + 1, :], (16, 128))
            slots_ref[block, start : start + region.shape[0], :] = region.astype(BF16)


def fill_faces(rows_ref, near_ref, place, faces_ref):
    member, own = place
    for k, (dx, dy, dz) in enumerate(DIRECTIONS):
        if (dx, dy, dz).count(0) != 2:
            continue
        block = near_ref[0, k]
        distance = jnp.where(member == 0, block - own, own - block)
        end = 15 if dx + dy + dz == 1 else 0

        @pl.when((block >= 0) & (distance >= 1))
        def _(dx=dx, dy=dy, end=end, distance=distance):
            if dx:
                region = rows_ref[end * 256 : end * 256 + 256, :]
            elif dy:
                region = jnp.concatenate(
                    [rows_ref[x * 256 + end * 16 : x * 256 + end * 16 + 16, :] for x in range(16)]
                )
            else:
                region = rows_ref[pl.ds(end, 256, stride=16), :]
            faces_ref[distance - 1] = region.astype(BF16)


class Whole:
    def __init__(self, ref):
        self.ref = ref

    def at(self, x, row, height):
        return self.ref, x, row


class Margin:
    def __init__(self, planes_ref, lines_ref):
        self.planes_ref, self.lines_ref = planes_ref, lines_ref

    def at(self, x, row, height):
        if x in (0, 17):
            return self.planes_ref, x // 17, row
        return self.lines_ref, row // 272, (x - 1) * 16


def put_lines(padded, places, rows):
    count = rows.shape[0]
    level = lax.broadcasted_iota(jnp.int32, rows.shape, 0) % 16
    below = jnp.where(level == 0, 0.0, pltpu.roll(rows, 1, 0)).astype(BF16)
    above = jnp.where(level == 15, 0.0, pltpu.roll(rows, count - 1, 0)).astype(BF16)
    here = rows.astype(BF16)
    at = 0
    for x, row, height in places:
        ref, plane, first = padded.at(x, row, height)
        for j, part in enumerate((below, here, above)):
            ref[plane, first : first + height, j * 128 : j * 128 + 128] = part[at : at + height]
        at += height


def put_ends(padded, x, row, rows, dz):
    lines = rows.shape[0]
    j = 0 if dz == -1 else 2
    end = 0 if dz == -1 else 15
    lanes = slice(j * 128, j * 128 + 128)
    ref, plane, first = padded.at(x, row, 16 * lines)
    span = slice(first, first + 16 * lines)
    old = ref[plane, span, lanes].astype(F32).reshape(lines, 16, 128)
    level = lax.broadcasted_iota(jnp.int32, old.shape, 1)
    new = jnp.where(level == end, rows.reshape(lines, 1, 128), old)
    ref[plane, span, lanes] = new.reshape(16 * lines, 128).astype(BF16)


def clear_margin(padded_ref):
    empty = jnp.zeros((288, 384), BF16)
    padded_ref[0] = empty
    padded_ref[17] = empty
    line = jnp.zeros((16, 384), BF16)
    for x in range(1, 17):
        padded_ref[x, 0:16, :] = line
        padded_ref[x, 272:288, :] = line


def put_region(padded, offset, rows):
    dx, dy, dz = offset
    zeros = [d == 0 for d in offset]
    x = 17 if dx == 1 else 0
    y = 17 if dy == 1 else 0
    if zeros == [False, True, True]:
        put_lines(padded, [(x, 16, 256)], rows)
    elif zeros == [True, False, True]:
        put_lines(padded, [(at + 1, y * 16, 16) for at in range(16)], rows)
    elif zeros == [False, False, True]:
        put_lines(padded, [(x, y * 16, 16)], rows)
    elif zeros == [True, True, False]:
        for at in range(16):
            put_ends(padded, at + 1, 16, rows[at * 16 : at * 16 + 16], dz)
    elif zeros == [False, True, False]:
        put_ends(padded, x, 16, rows, dz)
    elif zeros == [True, False, False]:
        for at in range(16):
            put_ends(padded, at + 1, y * 16, rows[at : at + 1], dz)
    else:
        put_ends(padded, x, y * 16, rows[0:1], dz)


def face_source(place, block):
    away = place[1] - block
    return jnp.where(away > 0, 0, 1) == place[0], jnp.clip(jnp.abs(away) - 1, 0, 3)


def fill_margin(padded, near_ref, own_ref, other_ref, start=0, faces=None, z_faces=True):
    for k in FILL_ORDER:
        offset = DIRECTIONS[k]
        block = near_ref[0, k]
        face = offset.count(0) == 2
        if face and offset[2] and not z_faces:
            continue
        if face and faces is not None:
            place, own_faces_ref, other_faces_ref = faces
            here, slot = face_source(place, block)

            @pl.when((block >= 0) & here)
            def _(offset=offset, slot=slot):
                put_region(padded, offset, own_faces_ref[slot].astype(F32))

            @pl.when((block >= 0) & jnp.logical_not(here))
            def _(offset=offset, slot=slot):
                rows = swap_halves(other_faces_ref[slot].astype(F32))
                put_region(padded, offset, rows)

            continue

        @pl.when(block >= 0)
        def _(offset=offset, block=block, face=face):
            height = 128 if face else 16
            own = own_ref[block, start : start + height, :].astype(F32)
            other = other_ref[block, 0:height, :].astype(F32)
            first = jnp.where(low_lanes(own), own, swap_halves(other))
            second = jnp.where(low_lanes(own), swap_halves(own), other)
            if face:
                rows = jnp.concatenate([first, second])
            elif offset[0] == 0:
                rows = jnp.concatenate([first[:8], second[:8]])
            else:
                rows = first if offset[0] == 1 else second
            put_region(padded, offset, rows)


def send_features(
    near_hbm, heights_hbm, features_hbm, slots_ref,
    near_ref, heights_ref, features_ref, rows_ref, arrived
):
    copies = [
        pltpu.make_async_copy(near_hbm, near_ref, arrived.at[8]),
        pltpu.make_async_copy(heights_hbm, heights_ref, arrived.at[9]),
    ]
    order = (0, 1, 2, 3, 4, 5, 6, 7)
    bricks = [
        pltpu.make_async_copy(features_hbm.at[i], features_ref.at[i], arrived.at[i]) for i in order
    ]
    for copy in copies + bricks:
        copy.start()
    copies[1].wait()
    filled = filled_voxels(heights_ref)
    for oz in range(2):
        for oy in range(2):
            pair = []
            for ox in range(2):
                brick = ox + 2 * oy + 4 * oz
                bricks[brick].wait()
                pair.append(features_ref[brick].astype(F32) * filled[brick : brick + 1])
            turned = jnp.concatenate(pair).T
            for vx in range(8):
                for vy in range(8):
                    at = vx * 256 + (8 * oy + vy) * 16 + 8 * oz
                    source = (vx * 8 + vy) * 8
                    rows_ref[at : at + 8, :] = turned[source : source + 8]
    copies[0].wait()
    fill_slots(rows_ref, near_ref, slots_ref)


def own_first_taps(shift, conv_ref, yz):
    taps = []
    for ex in range(3):
        tap = conv_ref[ex * 9 + yz].astype(F32)
        taps.append(pltpu.roll(pltpu.roll(tap, shift, 0), shift, 1))
    return taps


def forward_weights(shift, conv_ref, down_in_ref, cot_in_ref, two_ref, down_ref, cot_ref):
    empty = jnp.zeros((128, 128), BF16)
    for yz in range(9):
        taps = own_first_taps(shift, conv_ref, yz)
        whole = [empty] + [tap.astype(BF16) for tap in taps] + [empty]
        for p in range(4):
            rows = slice((p * 9 + yz) * 128, (p * 9 + yz) * 128 + 128)
            two_ref[rows, 0:128] = whole[p + 1] if p < 3 else empty
            two_ref[rows, 128:256] = whole[p]
    for tap in range(8):
        rows = down_in_ref[tap].astype(F32)
        rows = pltpu.roll(rows, shift, 0)
        down_ref[tap * 128 : tap * 128 + 128, :] = pltpu.roll(rows, 2 * shift, 1).astype(BF16)
    cot_ref[...] = pltpu.roll(cot_in_ref[...].astype(F32), 2 * shift, 1).astype(BF16)


def backward_weights(shift, conv_ref, four_ref):
    empty = jnp.zeros((128, 128), BF16)
    none = jnp.zeros((64, 128), F32)
    for yz in range(9):
        taps = own_first_taps(shift, conv_ref, yz)
        own = [none] + [taps[2 - ex][:64] for ex in range(3)] + [none]
        pairs = [jnp.concatenate([own[i + 1], own[i]]).T.astype(BF16) for i in range(4)]
        for p in range(6):
            at = (p * 9 + 8 - yz) * 128
            four_ref[at : at + 128, 0:128] = pairs[p] if p < 4 else empty
            four_ref[at : at + 128, 128:256] = pairs[p - 2] if p >= 2 else empty


def own_lanes(triple):
    below, here = triple[:, 0:128].astype(F32), triple[:, 128:256].astype(F32)
    both = jnp.where(low_lanes(below), below, swap_halves(here)).astype(BF16)
    return both, triple[:, 256:384]


def prepare(
    core_ref, conv_hbm, down_hbm, cot_hbm, heights_hbm, own_hbm, other_hbm,
    lanes_hbm, active_hbm, slope_hbm, inner_hbm, taps_hbm, down_out_hbm, cot_out_hbm,
    conv_in_ref, down_in_ref, cot_in_ref, heights_ref, own_ref, other_ref,
    two_ref, down_ref, cot_ref, padded_ref, rows_ref, mask_ref, lanes_ref, active_ref,
    slope_ref, inner_ref, slope_wide_ref, arrived, left, left_inner
):
    came = start_all(
        [
            (conv_hbm, conv_in_ref),
            (down_hbm, down_in_ref),
            (cot_hbm, cot_in_ref),
            (heights_hbm, heights_ref),
            (own_hbm, own_ref),
            (other_hbm, other_ref),
        ],
        arrived,
    )
    gone = [
        pltpu.make_async_copy(source, target, left.at[i])
        for i, (source, target) in enumerate(
            [
                (two_ref.at[0:3456, 0:128], taps_hbm),
                (down_ref, down_out_hbm),
                (cot_ref, cot_out_hbm),
                (lanes_ref, lanes_hbm),
                (active_ref, active_hbm),
                (slope_ref, slope_hbm),
            ]
        )
    ]
    for copy in came[:3]:
        copy.wait()
    forward_weights(
        core_ref[0] * 64, conv_in_ref, down_in_ref, cot_in_ref, two_ref, down_ref, cot_ref
    )
    for copy in gone[:3]:
        copy.start()
    for copy in came[3:]:
        copy.wait()
    filled = filled_voxels(heights_ref)
    upright = filled.T
    for brick in range(8):
        ox, oy, oz = brick % 2, brick // 2 % 2, brick // 4
        both = jnp.concatenate([own_ref[brick].astype(F32), other_ref[brick].astype(F32)])
        turned = (both * filled[brick : brick + 1]).T
        mask = jnp.broadcast_to(upright[:, brick : brick + 1], (512, 128))
        for vx in range(8):
            for vy in range(8):
                at = (8 * ox + vx) * 256 + (8 * oy + vy) * 16 + 8 * oz
                source = (vx * 8 + vy) * 8
                rows_ref[at : at + 8, :] = turned[source : source + 8]
                mask_ref[at : at + 8, :] = mask[source : source + 8]
    clear_margin(padded_ref)
    for x in range(16):
        put_lines(Whole(padded_ref), [(x + 1, 16, 256)], rows_ref[x * 256 : x * 256 + 256, :])
        active_ref[x * 256 : x * 256 + 256, :] = mask_ref[x * 256 : x * 256 + 256, :].astype(BF16)
    for x in range(18):
        lanes_ref[x, :, 0:128], lanes_ref[x, :, 128:256] = own_lanes(padded_ref[x])
    gone[3].start()
    gone[4].start()
    for tap in range(8):
        tx, ty, tz = tap // 4, tap // 2 % 2, tap % 2
        part = lax.dot_general(
            cot_ref[...],
            down_ref[tap * 128 : tap * 128 + 128, :],
            (((1,), (1,)), ((), ())),
            preferred_element_type=F32,
        )
        for ux in range(8):
            for uy in range(8):
                at = (2 * ux + tx) * 256 + (2 * uy + ty) * 16 + tz
                source = (ux * 8 + uy) * 8
                rows = pl.ds(at, 8, stride=2)
                slope_wide_ref[rows, :] = part[source : source + 8] * mask_ref[rows, :]
    slope_ref[...] = slope_wide_ref[...].astype(BF16)
    gone[5].start()

    def leave(group):
        rows = pl.ds(pl.multiple_of(group * 1024, 1024), 1024)
        return pltpu.make_async_copy(
            inner_ref.at[rows], inner_hbm.at[rows], left_inner.at[group]
        )


    def step(group, carry):
        lhs = []
        for pair in range(2):
            pieces = []
            for p in range(4):
                for ey in range(3):
                    pieces.append(
                        padded_ref[group * 4 + pair * 2 + p, ey * 16 : ey * 16 + 256, :]
                    )
            lhs.append(jnp.concatenate(pieces, axis=1))
        summed = jnp.dot(jnp.concatenate(lhs), two_ref[...], preferred_element_type=F32)
        for pair in range(2):
            for phase in range(2):
                at = pl.multiple_of((group * 4 + pair * 2 + phase) * 256, 256)
                part = summed[pair * 256 : pair * 256 + 256, phase * 128 : phase * 128 + 128]
                rows = pl.ds(at, 256)
                inner_ref[rows, :] = jnp.where(mask_ref[rows, :] > 0, part, INACTIVE)
        leave(group).start()
        return carry

    lax.fori_loop(0, 4, step, 0)
    for copy in gone:
        copy.wait()
    for group in range(4):
        leave(group).wait()


def tap_rows(taps_ref, taps):
    starts = [((ex * 3 + ey) * 3 + ez) * 128 for ex, ey, ez in taps]
    return jnp.concatenate([taps_ref[at : at + 128, :] for at in starts])


def margin_planes(planes_ref, taps_ref):
    sums = []
    for side, ex in ((0, 0), (1, 2)):
        lhs = jnp.concatenate(
            [planes_ref[side, ey * 16 : ey * 16 + 256, :] for ey in range(3)], axis=1
        )
        rhs = taps_ref[ex * 1152 : ex * 1152 + 1152, :]
        sums.append(jnp.dot(lhs, rhs, preferred_element_type=F32))
    return sums


def margin_lines(lines_ref, taps_ref):
    sums = []
    none = jnp.zeros((16, 384), BF16)
    for side, ey in ((0, 0), (1, 2)):
        lines = lines_ref[side]
        lhs = jnp.concatenate(
            [
                jnp.concatenate([none, lines[:240]]),
                lines,
                jnp.concatenate([lines[16:], none]),
            ],
            axis=1,
        )
        rhs = tap_rows(taps_ref, [(ex, ey, ez) for ex in range(3) for ez in range(3)])
        sums.append(jnp.dot(lhs, rhs, preferred_element_type=F32))
    return sums


def margin_ends(face, ez, taps_ref):
    line = lax.broadcasted_iota(jnp.int32, face.shape, 0) % 16
    shifted = [
        jnp.where(line == 0, 0.0, pltpu.roll(face, 1, 0)),
        face,
        jnp.where(line == 15, 0.0, pltpu.roll(face, 255, 0)),
    ]
    border = jnp.zeros((16, 128), F32)
    lhs = []
    for ex in range(3):
        for part in shifted:
            if ex == 0:
                part = jnp.concatenate([border, part[:240]])
            elif ex == 2:
                part = jnp.concatenate([part[16:], border])
            lhs.append(part.astype(BF16))
    rhs = tap_rows(taps_ref, [(ex, ey, ez) for ex in range(3) for ey in range(3)])
    return jnp.dot(jnp.concatenate(lhs, axis=1), rhs, preferred_element_type=F32)


Z_FACES = ((DIRECTIONS.index((0, 0, -1)), 0), (DIRECTIONS.index((0, 0, 1)), 2))


def joined_face(own_ref, other_ref, block):
    own = own_ref[block].astype(F32)
    other = other_ref[block].astype(F32)
    return jnp.concatenate(
        [
            jnp.where(low_lanes(own), own, swap_halves(other)),
            jnp.where(low_lanes(own), swap_halves(own), other),
        ]
    )


def add_margin(planes_ref, lines_ref, near_ref, own_ref, other_ref, taps_ref, pre_ref):
    for side, added in enumerate(margin_planes(planes_ref, taps_ref)):
        at = side * 15 * 256
        pre_ref[at : at + 256, :] += added
    for side, added in enumerate(margin_lines(lines_ref, taps_ref)):
        for x in range(16):
            at = x * 256 + side * 240
            pre_ref[at : at + 16, :] += added[x * 16 : x * 16 + 16]
    for k, ez in Z_FACES:
        block = near_ref[0, k]

        @pl.when(block >= 0)
        def _(block=block, ez=ez):
            added = margin_ends(joined_face(own_ref, other_ref, block), ez, taps_ref)
            rows = pl.ds(0 if ez == 0 else 15, 256, stride=16)
            pre_ref[rows, :] = pre_ref[rows, :] + added


def put_own_margin(planes_ref, lines_ref, near_ref, own_ref, other_ref, lanes_ref):
    for side in range(2):
        plane = side * 17
        lanes_ref[plane, :, 0:128], lanes_ref[plane, :, 128:256] = own_lanes(planes_ref[side])
        both, above = own_lanes(lines_ref[side])
        rows = slice(side * 272, side * 272 + 16)
        for x in range(16):
            lanes_ref[x + 1, rows, 0:128] = both[x * 16 : x * 16 + 16]
            lanes_ref[x + 1, rows, 128:256] = above[x * 16 : x * 16 + 16]
    for k, ez in Z_FACES:
        block = near_ref[0, k]

        @pl.when(block >= 0)
        def _(block=block, ez=ez):
            face = joined_face(own_ref, other_ref, block)
            lanes = slice(ez * 64, ez * 64 + 128)
            for x in range(16):
                old = lanes_ref[x + 1, 16:272, lanes].astype(F32).reshape(16, 16, 128)
                level = lax.broadcasted_iota(jnp.int32, old.shape, 1)
                lane = lax.broadcasted_iota(jnp.int32, old.shape, 2)
                here = (level == (0 if ez == 0 else 15)) & (lane < 64)
                new = jnp.where(here, face[x * 16 : x * 16 + 16].reshape(16, 1, 128), old)
                lanes_ref[x + 1, 16:272, lanes] = new.reshape(256, 128).astype(BF16)


def forward(
    near_ref, core_ref, at_ref, own_ref, other_ref, taps_ref, inner_ref, slope_ref,
    lanes_hbm, down_hbm, cot_hbm,
    slots_hbm, faces_ref, coarse_hbm, grad_pre_hbm,
    planes_ref, lines_ref, pre_ref, grad_ref, packed_ref, turned_ref, lanes_ref,
    down_ref, cot_ref, coarse_ref, grad_pre_ref, slots_ref, arrived, left, left_slots
):
    came = start_all(
        [(lanes_hbm, lanes_ref), (down_hbm, down_ref), (cot_hbm, cot_ref)], arrived
    )
    pre_ref[...] = inner_ref[...]
    planes_ref[...] = jnp.zeros(planes_ref.shape, BF16)
    lines_ref[...] = jnp.zeros(lines_ref.shape, BF16)
    margin = Margin(planes_ref, lines_ref)
    fill_margin(margin, near_ref, own_ref, other_ref, z_faces=False)
    add_margin(planes_ref, lines_ref, near_ref, own_ref, other_ref, taps_ref, pre_ref)

    turned_ref[:, 0:512] = jnp.zeros((128, 512), BF16)
    turned_ref[:, 4608:5120] = jnp.zeros((128, 512), BF16)
    for x in range(16):
        rows = slice(x * 256, x * 256 + 256)
        pre = pre_ref[rows, :]
        sigmoid = 0.5 + 0.5 * jnp.tanh(0.5 * pre)
        pre_ref[rows, :] = jnp.where(pre > 0.5 * INACTIVE, pre * sigmoid, 0.0)
        grad = slope_ref[rows, :].astype(F32) * sigmoid * (1.0 + pre * (1.0 - sigmoid))
        grad_ref[rows, :] = grad
        grad = grad.astype(BF16)
        grad_pre_ref[rows, :] = grad
        turned_ref[:, 512 + x * 256 : 768 + x * 256] = grad.T

    gone = [
        pltpu.make_async_copy(grad_pre_ref, grad_pre_hbm, left.at[0]),
        pltpu.make_async_copy(coarse_ref, coarse_hbm, left.at[1]),
    ]
    gone[0].start()
    fill_faces(grad_ref, near_ref, (core_ref[0], at_ref[0]), faces_ref)
    share = slots_ref.shape[1] - 16
    for x in range(8):
        low = grad_ref[x * 256 : x * 256 + 256, :]
        high = grad_ref[2048 + x * 256 : 2048 + x * 256 + 256, :]
        packed_ref[x * 256 : x * 256 + 256, :] = jnp.where(
            low_lanes(low), low, swap_halves(high)
        )
    fill_slots(packed_ref, near_ref, slots_ref, share, faces=False)

    def put_terms(at, rows):
        while rows.shape[0]:
            owner, row = at // share, at % share
            count = min(rows.shape[0], share - row)
            slots_ref[owner, row : row + count, :] = rows[:count]
            rows = rows[count:]
            at += count

    ends = [1024 // share] + [(1024 + 576 * i) // share for i in (1, 2)] + [slots_ref.shape[0]]
    leaving = [
        pltpu.make_async_copy(
            slots_ref.at[first:last], slots_hbm.at[first:last], left_slots.at[i]
        )
        for i, (first, last) in enumerate(zip([0] + ends, ends))
    ]

    came[1].wait()
    came[2].wait()
    patches = []
    for tap in range(8):
        tx, ty, tz = tap // 4, tap // 2 % 2, tap % 2
        pieces = []
        for ux in range(8):
            for uy in range(8):
                at = (2 * ux + tx) * 256 + (2 * uy + ty) * 16 + tz
                pieces.append(pre_ref[pl.ds(at, 8, stride=2), :])
        patches.append(jnp.concatenate(pieces).astype(BF16))
    patches = jnp.concatenate(patches, axis=1)
    coarse = jnp.dot(patches, down_ref[...], preferred_element_type=F32)
    coarse_ref[...] = coarse[:, :128].astype(BF16)
    gone[1].start()
    own_cot = cot_ref[:, 0:128].astype(F32).T.astype(BF16)
    grad_down = jnp.dot(own_cot, patches, preferred_element_type=F32)
    for tap in range(8):
        part = grad_down[:, tap * 128 : tap * 128 + 128].T
        put_terms(tap * 128, part.astype(BF16))
    leaving[0].start()

    came[0].wait()
    put_own_margin(planes_ref, lines_ref, near_ref, own_ref, other_ref, lanes_ref)
    lhs = jnp.concatenate(
        [turned_ref[:, (2 - ex) * 256 : (2 - ex) * 256 + 4608] for ex in range(3)]
    )
    for ey in range(3):
        rhs = lanes_ref[:, ey * 16 : ey * 16 + 256, :].reshape(4608, 256)
        summed = jnp.dot(lhs, rhs, preferred_element_type=F32)
        for ex in range(3):
            part = summed[ex * 128 : ex * 128 + 128].T
            put_terms(1024 + (ey * 3 + ex) * 192, part[0:192].astype(BF16))
        leaving[ey + 1].start()
    for copy in gone + leaving:
        copy.wait()


def fetch(taps_hbm, inner_hbm, slope_hbm, taps_ref, inner_ref, slope_ref, arrived):
    for copy in start_all(
        [(taps_hbm, taps_ref), (inner_hbm, inner_ref), (slope_hbm, slope_ref)], arrived
    ):
        copy.wait()


def total(slots_ref, out_ref):
    devices, share, _ = out_ref.shape
    summed = slots_ref[0, 0:share, :].astype(F32)
    for device in range(1, devices):
        summed = summed + slots_ref[device, 0:share, :].astype(F32)
    summed = (summed / devices).astype(BF16)
    for device in range(devices):
        out_ref[device] = summed


def backward(
    near_ref, core_ref, at_ref, own_ref, other_ref, own_faces_ref, other_faces_ref,
    grad_pre_hbm, active_hbm, conv_hbm, out_ref,
    padded_ref, grad_pre_ref, active_ref, conv_ref, back_ref, arrived
):
    came = start_all(
        [(conv_hbm, conv_ref), (grad_pre_hbm, grad_pre_ref), (active_hbm, active_ref)], arrived
    )
    came[0].wait()
    backward_weights(core_ref[0] * 64, conv_ref, back_ref)
    clear_margin(padded_ref)
    came[1].wait()
    for x in range(16):
        rows = grad_pre_ref[x * 256 : x * 256 + 256, :].astype(F32)
        put_lines(Whole(padded_ref), [(x + 1, 16, 256)], rows)
    fill_margin(
        Whole(padded_ref), near_ref, own_ref, other_ref, own_ref.shape[1] - 16,
        ((core_ref[0], at_ref[0]), own_faces_ref, other_faces_ref),
    )
    came[2].wait()
    for half in range(2):
        lhs = []
        for quad in range(2):
            pieces = []
            for p in range(6):
                for ey in range(3):
                    pieces.append(
                        padded_ref[half * 8 + quad * 4 + p, ey * 16 : ey * 16 + 256, :]
                    )
            lhs.append(jnp.concatenate(pieces, axis=1))
        summed = jnp.dot(jnp.concatenate(lhs), back_ref[...], preferred_element_type=F32)
        for quad in range(2):
            for two in range(2):
                part = summed[quad * 256 : quad * 256 + 256, two * 128 : two * 128 + 128]
                x = half * 8 + quad * 4 + two * 2
                even = active_ref[x * 256 : x * 256 + 256, :].astype(F32)
                odd = active_ref[x * 256 + 256 : x * 256 + 512, :].astype(F32)
                part = part * jnp.where(low_lanes(part), even, odd)
                for oy in range(2):
                    rows = [
                        part[(8 * oy + vy) * 16 + 8 * oz : (8 * oy + vy) * 16 + 8 * oz + 8]
                        for oz in range(2)
                        for vy in range(8)
                    ]
                    turned = jnp.concatenate(rows).T
                    first, second = turned[:64], turned[64:]
                    lanes = slice(x % 8 * 64, x % 8 * 64 + 128)
                    brick = half + 2 * oy
                    near = jnp.where(low_lanes(first), first, swap_halves(second))
                    far = jnp.where(low_lanes(first), swap_halves(first), second)
                    out_ref[brick, :, lanes] = near.astype(BF16)
                    out_ref[brick + 4, :, lanes] = far.astype(BF16)


def finish(core_ref, sums_ref, conv_ref, down_ref):
    shift = core_ref[0] * 64
    for tap in range(27):
        ex, ey, ez = tap // 9, tap // 3 % 3, tap % 3
        at = 1024 + ((ey * 3 + ex) * 3 + ez) * 64
        rows = sums_ref[at : at + 64, :].astype(F32)
        conv_ref[tap] = pltpu.roll(rows, shift, 1)
    for tap in range(8):
        rows = sums_ref[tap * 128 : tap * 128 + 128, :].astype(F32)
        down_ref[tap, pl.ds(shift, 64), :] = rows[:64]
        down_ref[tap, pl.ds(64 - shift, 64), :] = rows[64:]


def over_space(block, distance):
    blocks = range(lax.axis_size("space"))
    route = [(2 * i, 2 * (i + distance)) for i in blocks if i + distance in blocks]
    route += [(2 * i + 1, 2 * (i - distance) + 1) for i in blocks if i - distance in blocks]
    return lax.ppermute(block, ("space", "chan"), route)


def over_chan(block):
    return lax.ppermute(block, "chan", [(0, 1), (1, 0)])


def to_all(slots):
    return lax.all_to_all(slots, "space", 0, 0, tiled=True)


def local(features, heights, neighbours, w_conv, w_down, cotangent):
    devices = lax.axis_size("space")
    member = lax.axis_index("chan")

    def out(*shape, dtype=BF16):
        return jax.ShapeDtypeStruct(shape, dtype)

    def held_out(*shape, dtype=BF16):
        return pltpu.HBM(shape, dtype)

    def memory(*shape, dtype=BF16):
        return pltpu.VMEM(shape, dtype)

    def copies(count):
        return pltpu.SemaphoreType.DMA((count,))

    core = member.reshape(1)
    place = (core, lax.axis_index("space").reshape(1))
    turned = features.transpose(0, 2, 1)
    slots = kernel_call(
        send_features,
        out(devices, 128, 128),
        [hbm()] * 3,
        vmem(),
        [
            pltpu.SMEM(neighbours.shape, jnp.int32),
            memory(8, 64, dtype=jnp.int32),
            memory(8, 64, 512),
            memory(2048, 128, dtype=F32),
            copies(10),
        ],
    )(neighbours, heights, turned)
    came = to_all(slots)
    other_turned = over_chan(turned)

    held = [
        held_out(18, 288, 256),
        held_out(4096, 128),
        held_out(4096, 128),
        held_out(4096, 128, dtype=F32),
        held_out(3456, 128),
        held_out(1024, 256),
        held_out(512, 256),
    ]
    lanes, active, slope, inner, taps, down, cot = kernel_call(
        prepare,
        held,
        [smem()] + [hbm()] * 5 + [pl.BlockSpec(memory_space=pl.ANY)],
        [hbm()] * 7,
        [
            memory(27, 128, 128),
            memory(8, 128, 256),
            memory(512, 256),
            memory(8, 64, dtype=jnp.int32),
            memory(8, 64, 512),
            memory(8, 64, 512),
            memory(4608, 256),
            memory(1024, 256),
            memory(512, 256),
            memory(18, 288, 384),
            memory(4096, 128, dtype=F32),
            memory(4096, 128, dtype=F32),
            memory(18, 288, 256),
            memory(4096, 128),
            memory(4096, 128),
            memory(4096, 128, dtype=F32),
            memory(4096, 128, dtype=F32),
            copies(6),
            copies(6),
            copies(4),
        ],
        flops=5 << 30,
        mib=36,
    )(core, w_conv, w_down, cotangent[0], heights, turned, other_turned)
    came, taps, inner, slope = lax.optimization_barrier((came, taps, inner, slope))
    came_other = over_chan(came)
    taps, inner, slope = kernel_call(
        fetch,
        [out(3456, 128), out(4096, 128, dtype=F32), out(4096, 128)],
        [hbm()] * 3,
        [vmem()] * 3,
        [copies(3)],
    )(taps, inner, slope)

    share = -(-2752 // (devices * 16)) * 16
    terms, faces, coarse, grad_pre = kernel_call(
        forward,
        [
            held_out(devices, share + 16, 128),
            out(4, 256, 128),
            held_out(512, 128),
            held_out(4096, 128),
        ],
        [smem()] * 3 + [vmem()] * 5 + [hbm()] * 3,
        [hbm(), vmem(), hbm(), hbm()],
        [
            memory(2, 288, 384),
            memory(2, 256, 384),
            memory(4096, 128, dtype=F32),
            memory(4096, 128, dtype=F32),
            memory(2048, 128, dtype=F32),
            memory(128, 5120),
            memory(18, 288, 256),
            memory(1024, 256),
            memory(512, 256),
            memory(512, 128),
            memory(4096, 128),
            memory(devices, share + 16, 128),
            copies(3),
            copies(2),
            copies(4),
        ],
        flops=5 << 30,
        mib=24,
    )(
        neighbours, *place, came, came_other, taps, inner, slope, lanes, down, cot
    )

    arrived = to_all(terms)
    came_faces = [over_space(faces[i], i + 1) for i in range(4)]
    arrived, *came_faces = lax.optimization_barrier((arrived, *came_faces))
    came_faces = jnp.stack(came_faces)
    other_faces = over_chan(came_faces)
    sums = to_all(
        kernel_call(total, out(devices, share, 128), [vmem()], vmem())(arrived)
    )
    arrived_other = over_chan(arrived[:, share:])
    grad_features = kernel_call(
        backward,
        out(8, 64, 512),
        [smem()] * 3 + [vmem()] * 4 + [hbm()] * 3,
        vmem(),
        [
            memory(18, 288, 384),
            memory(4096, 128),
            memory(4096, 128),
            memory(27, 128, 128),
            memory(6912, 256),
            copies(3),
        ],
        flops=5 << 30,
        mib=24,
    )(
        neighbours, *place, arrived, arrived_other, came_faces, other_faces, grad_pre, active,
        w_conv,
    )

    grad_conv, grad_down = kernel_call(
        finish,
        [out(27, 64, 128, dtype=F32), out(8, 128, 128, dtype=F32)],
        [smem(), vmem()],
        [vmem()] * 2,
    )(core, sums.reshape(-1, 128))
    return coarse[None], grad_conv, grad_down, grad_features.transpose(0, 2, 1)


def solution(mesh):
    placed = (
        P("space", None, "chan"),
        P("space", None),
        P("space", None),
        P(),
        P(),
        P("space", None, None),
    )
    return jax.shard_map(
        local,
        mesh=mesh,
        in_specs=placed,
        out_specs=(
            P("space", None, "chan"),
            P(None, "chan", None),
            P(None, None, "chan"),
            P("space", None, "chan"),
        ),
        check_vma=False,
    )
```

profile of v0, /device:TPU:0, one launch (start us, length us, event | category | flops | bytes accessed | tf_op | source)
XLA Modules:
  0.0 90.8 jit_solution(13393657436218069042)
XLA Ops:
  0.6 0.5 collective-permute-start
  1.1 2.6 %shard_map.93 = bf16[16,128,128]{2,1,0:T(8,128)(2,1)} custom-call(s32[1,26]{1,0:T(1,128)} %near_ref.3, s32[8,64]{1,0:T(8,128)} %heights_hbm.3, bf16[8,64,512]{2,1,0:T(8,128)(2,1)} %bitcast.21), custom_call_target="tpu_custom_call" | custom-call | bytes 4194304 | tf_op jit(solution)/shard_map/pallas_call | solution.py:50
  3.7 8.0 %all-to-all-start = ((bf16[16,128,128]{2,1,0:T(8,128)(2,1)}), bf16[16,128,128]{2,1,0:T(8,128)(2,1)S(1)}, u32[]{:S(2)}, u32[]{:S(2)}) async-start(bf16[16,128,128]{2,1,0:T(8,128)(2,1)} %shard_map.93), calls=%async_computation | async-start | bytes 1048576 | tf_op jit(solution)/shard_map/all_to_all | solution.py:758
  11.7 0.0 collective-permute-done.other_hbm
  11.7 11.6 %shard_map.94 = (bf16[18,288,256]{2,1,0:T(8,128)(2,1)}, bf16[4096,128]{1,0:T(8,128)(2,1)}, bf16[4096,128]{1,0:T(8,128)(2,1)}, f32[4096,128]{1,0:T(8,128)}, bf16[...) custom-call(s32[1]{0:T(128)} %bitcast.core_ref, bf16[27,128,128]{2,1,0:T(8,128)(2,1)} %conv_hbm.3, ...), custom_call_target="tpu_custom_call" | custom-call | flops 5368709120 | bytes 4194304 | tf_op jit(solution)/shard_map/pallas_call | solution.py:50
  23.3 0.0 copy-start
  23.3 3.8 %all-to-all-done.own_ref = bf16[16,128,128]{2,1,0:T(8,128)(2,1)S(1)} async-done(((bf16[16,128,128]{2,1,0:T(8,128)(2,1)}), bf16[16,128,128]{2,1,0:T(8,128)(2,1)S(1)}, u32[]{:S(2)}, u32[]{:S(2)}) %all-to-all-start) | async-done | bytes 524320 | tf_op jit(solution)/shard_map/all_to_all | solution.py:758
  27.1 0.0 collective-permute-start.1
  27.1 2.1 %shard_map.95 = (bf16[3456,128]{1,0:T(8,128)(2,1)S(1)}, f32[4096,128]{1,0:T(8,128)S(1)}, bf16[4096,128]{1,0:T(8,128)(2,1)S(1)}) custom-call(bf16[3456,128]{1,0:T(8,128)(2,1)} %get-tuple-element.33.taps_hbm, f32[4096,128]{1,0:T(8,128)} %get-tuple-element.34.inner_hbm, bf16[4096,128]{1,0:T(8,128)(2,1)} %get-tuple-element.35.slope_hbm), custom_call_target="tpu_custom_call" | custom-call | bytes 4194304 | tf_op jit(solution)/shard_map/pallas_call | solution.py:50
  29.3 0.0 collective-permute-done.1.other_ref
  29.3 0.0 copy-done
  29.3 8.5 %shard_map.96 = (bf16[16,192,128]{2,1,0:T(8,128)(2,1)}, bf16[4,256,128]{2,1,0:T(8,128)(2,1)S(1)}, bf16[512,128]{1,0:T(8,128)(2,1)}, bf16[4096,128]{1,0:T(8,128)(2,1)}) custom-call(s32[1,26]{1,0:T(1,128)S(1)} %copy-done, s32[1]{0:T(128)} %bitcast.core_ref, s32[1]{0:T(128)} %bitcast.1.at_ref, bf16[16,128,128]{2,1,0:T(8,128)(2,1)S(1)} %all-to-all-done.own_ref, ...), custom_call_target="tpu_custom_call" | custom-call | flops 5368709120 | bytes 4194304 | tf_op jit(solution)/shard_map/pallas_call | solution.py:50
  37.8 4.8 %all-to-all-start.1 = ((bf16[16,192,128]{2,1,0:T(8,128)(2,1)}), bf16[16,192,128]{2,1,0:T(8,128)(2,1)S(1)}, u32[]{:S(2)}, u32[]{:S(2)}) async-start(bf16[16,192,128]{2,1,0:T(8,128)(2,1)} %get-tuple-element.43), calls=%async_computation.1 | async-start | bytes 1572864 | tf_op jit(solution)/shard_map/all_to_all | solution.py:758
  42.7 3.8 %collective-permute-start.5 = (bf16[256,128]{1,0:T(8,128)(2,1)S(1)}, bf16[256,128]{1,0:T(8,128)(2,1)S(1)}, u32[]{:S(2)}, u32[]{:S(2)}) collective-permute-start(bf16[256,128]{1,0:T(8,128)(2,1)S(1)} %get-tuple-element.54), channel_id=1, source_target_pairs={{0,8},{2,10},{4,12},{6,14},{8,16},{10,18},{12,20},{14,22},{16,24},... | collective-permute-start | bytes 196616 | tf_op jit(solution)/shard_map/ppermute | solution.py:750
  46.5 4.3 %collective-permute-start.4 = (bf16[256,128]{1,0:T(8,128)(2,1)S(1)}, bf16[256,128]{1,0:T(8,128)(2,1)S(1)}, u32[]{:S(2)}, u32[]{:S(2)}) collective-permute-start(bf16[256,128]{1,0:T(8,128)(2,1)S(1)} %get-tuple-element.55), channel_id=1, source_target_pairs={{0,6},{2,8},{4,10},{6,12},{8,14},{10,16},{12,18},{14,20},{16,22},{... | collective-permute-start | bytes 196616 | tf_op jit(solution)/shard_map/ppermute | solution.py:750
  50.8 3.4 %collective-permute-start.3 = (bf16[256,128]{1,0:T(8,128)(2,1)S(1)}, bf16[256,128]{1,0:T(8,128)(2,1)S(1)}, u32[]{:S(2)}, u32[]{:S(2)}) collective-permute-start(bf16[256,128]{1,0:T(8,128)(2,1)S(1)} %get-tuple-element.56), channel_id=1, source_target_pairs={{0,4},{2,6},{4,8},{6,10},{8,12},{10,14},{12,16},{14,18},{16,20},{1... | collective-permute-start | bytes 196616 | tf_op jit(solution)/shard_map/ppermute | solution.py:750
  54.2 2.5 %collective-permute-start.2 = (bf16[256,128]{1,0:T(8,128)(2,1)S(1)}, bf16[256,128]{1,0:T(8,128)(2,1)S(1)}, u32[]{:S(2)}, u32[]{:S(2)}) collective-permute-start(bf16[256,128]{1,0:T(8,128)(2,1)S(1)} %get-tuple-element.57), channel_id=1, source_target_pairs={{0,2},{2,4},{4,6},{6,8},{8,10},{10,12},{12,14},{14,16},{16,18},{18... | collective-permute-start | bytes 196616 | tf_op jit(solution)/shard_map/ppermute | solution.py:750
  56.7 0.2 collective-permute-done.5
  56.9 0.0 collective-permute-done.4
  56.9 1.4 %collective-permute-done.3 = bf16[256,128]{1,0:T(8,128)(2,1)S(1)} collective-permute-done((bf16[256,128]{1,0:T(8,128)(2,1)S(1)}, bf16[256,128]{1,0:T(8,128)(2,1)S(1)}, u32[]{:S(2)}, u32[]{:S(2)}) %collective-permute-start.3) | collective-permute-done | bytes 65568 | tf_op jit(solution)/shard_map/ppermute | solution.py:750
  58.3 2.1 %collective-permute-done.2 = bf16[256,128]{1,0:T(8,128)(2,1)S(1)} collective-permute-done((bf16[256,128]{1,0:T(8,128)(2,1)S(1)}, bf16[256,128]{1,0:T(8,128)(2,1)S(1)}, u32[]{:S(2)}, u32[]{:S(2)}) %collective-permute-start.2) | collective-permute-done | bytes 65568 | tf_op jit(solution)/shard_map/ppermute | solution.py:750
  60.5 2.3 %all-to-all-done.1.slots_ref.own_ref = bf16[16,192,128]{2,1,0:T(8,128)(2,1)S(1)} async-done(((bf16[16,192,128]{2,1,0:T(8,128)(2,1)}), bf16[16,192,128]{2,1,0:T(8,128)(2,1)S(1)}, u32[]{:S(2)}, u32[]{:S(2)}) %all-to-all-start.1) | async-done | bytes 786464 | tf_op jit(solution)/shard_map/all_to_all | solution.py:758
  62.7 1.0 %shard_map.97 = bf16[16,176,128]{2,1,0:T(8,128)(2,1)} custom-call(bf16[16,192,128]{2,1,0:T(8,128)(2,1)S(1)} %all-to-all-done.1.slots_ref.own_ref), custom_call_target="tpu_custom_call" | custom-call | bytes 4194304 | tf_op jit(solution)/shard_map/pallas_call | solution.py:50
  63.7 7.4 %all-to-all-start.2 = ((bf16[16,176,128]{2,1,0:T(8,128)(2,1)}), bf16[16,176,128]{2,1,0:T(8,128)(2,1)S(1)}, u32[]{:S(2)}, u32[]{:S(2)}) async-start(bf16[16,176,128]{2,1,0:T(8,128)(2,1)} %shard_map.97), calls=%async_computation.2 | async-start | bytes 1441792 | tf_op jit(solution)/shard_map/all_to_all | solution.py:758
  71.1 0.1 collective-permute-start.7
  71.2 0.6 collective-permute-start.6
  71.7 1.0 %collective-permute-done.6.other_ref = bf16[16,16,128]{2,1,0:T(8,128)(2,1)S(1)} collective-permute-done((bf16[16,16,128]{2,1,0:T(8,128)(2,1)S(1)}, bf16[16,16,128]{2,1,0:T(8,128)(2,1)S(1)}, u32[]{:S(2)}, u32[]{:S(2)}) %collective-permute-start.6) | collective-permute-done | bytes 65568 | tf_op jit(solution)/shard_map/ppermute | solution.py:754
  72.8 0.0 collective-permute-done.7.other_faces_ref
  72.8 9.2 %shard_map.99 = bf16[8,64,512]{2,1,0:T(8,128)(2,1)} custom-call(s32[1,26]{1,0:T(1,128)S(1)} %copy-done, s32[1]{0:T(128)} %bitcast.core_ref, s32[1]{0:T(128)} %bitcast.1.at_ref, bf16[16,192,128]{2,1,0:T(8,128)(2,1)S(1)} %all-to-all-done.1.slots_ref.own_ref, bf16[16,16,128]{2,1,0:T(8,128)(2,1)S(1)} %collective-permute-done.6.other_ref, ...), custom_call_target="tpu_custom_call" | custom-call | flops 5368709120 | bytes 4194304 | tf_op jit(solution)/shard_map/pallas_call | solution.py:50
  82.0 7.6 %all-to-all-done.2 = bf16[16,176,128]{2,1,0:T(8,128)(2,1)S(1)} async-done(((bf16[16,176,128]{2,1,0:T(8,128)(2,1)}), bf16[16,176,128]{2,1,0:T(8,128)(2,1)S(1)}, u32[]{:S(2)}, u32[]{:S(2)}) %all-to-all-start.2) | async-done | bytes 720928 | tf_op jit(solution)/shard_map/all_to_all | solution.py:758
  89.6 1.2 %shard_map.98 = (f32[27,64,128]{2,1,0:T(8,128)}, f32[8,128,128]{2,1,0:T(8,128)}) custom-call(s32[1]{0:T(128)} %bitcast.core_ref, bf16[2816,128]{1,0:T(8,128)(2,1)S(1)} %bitcast.19), custom_call_target="tpu_custom_call" | custom-call | bytes 4194304 | tf_op jit(solution)/shard_map/pallas_call | solution.py:50
  (3 shorter events, 0.1 us)
Async XLA Ops:
  0.6 11.1 %collective-permute-start = (bf16[8,64,512]{2,1,0:T(8,128)(2,1)}, bf16[8,64,512]{2,1,0:T(8,128)(2,1)S(1)}, u32[]{:S(2)}, u32[]{:S(2)}) collective-permute-start(bf16[8,64,512]{2,1,0:T(8,128)(2,1)} %bitcast.20), channel_id=1, source_target_pairs={{0,1},{1,0},{2,3},{3,2},{4,5},{5,4},{6,7},{7,6},{8,9},{9,8},{10,11... | collective-permute-start | bytes 1572872 | tf_op jit(solution)/shard_map/ppermute | solution.py:754
  3.7 23.4 %all-to-all-start = ((bf16[16,128,128]{2,1,0:T(8,128)(2,1)}), bf16[16,128,128]{2,1,0:T(8,128)(2,1)S(1)}, u32[]{:S(2)}, u32[]{:S(2)}) async-start(bf16[16,128,128]{2,1,0:T(8,128)(2,1)} %shard_map.93), calls=%async_computation | async-start | bytes 1048576 | tf_op jit(solution)/shard_map/all_to_all | solution.py:758
  23.3 6.0 %copy-start = (s32[1,26]{1,0:T(1,128)S(1)}, s32[1,26]{1,0:T(1,128)}, u32[]{:S(2)}) copy-start(s32[1,26]{1,0:T(1,128)} %near_ref.3) | copy-start | bytes 316
  27.1 2.2 %collective-permute-start.1 = (bf16[16,128,128]{2,1,0:T(8,128)(2,1)S(1)}, bf16[16,128,128]{2,1,0:T(8,128)(2,1)S(1)}, u32[]{:S(2)}, u32[]{:S(2)}) collective-permute-start(bf16[16,128,128]{2,1,0:T(8,128)(2,1)S(1)} %all-to-all-done.own_ref), channel_id=1, source_target_pairs={{0,1},{1,0},{2,3},{3,2},{4,5},{5,4},{6,7},{7,6},{8,9},{9,8},{10,11... | collective-permute-start | bytes 1572872 | tf_op jit(solution)/shard_map/ppermute | solution.py:754
  37.8 24.9 %all-to-all-start.1 = ((bf16[16,192,128]{2,1,0:T(8,128)(2,1)}), bf16[16,192,128]{2,1,0:T(8,128)(2,1)S(1)}, u32[]{:S(2)}, u32[]{:S(2)}) async-start(bf16[16,192,128]{2,1,0:T(8,128)(2,1)} %get-tuple-element.43), calls=%async_computation.1 | async-start | bytes 1572864 | tf_op jit(solution)/shard_map/all_to_all | solution.py:758
  42.7 14.2 %collective-permute-start.5 = (bf16[256,128]{1,0:T(8,128)(2,1)S(1)}, bf16[256,128]{1,0:T(8,128)(2,1)S(1)}, u32[]{:S(2)}, u32[]{:S(2)}) collective-permute-start(bf16[256,128]{1,0:T(8,128)(2,1)S(1)} %get-tuple-element.54), channel_id=1, source_target_pairs={{0,8},{2,10},{4,12},{6,14},{8,16},{10,18},{12,20},{14,22},{16,24},... | collective-permute-start | bytes 196616 | tf_op jit(solution)/shard_map/ppermute | solution.py:750
  46.5 10.4 %collective-permute-start.4 = (bf16[256,128]{1,0:T(8,128)(2,1)S(1)}, bf16[256,128]{1,0:T(8,128)(2,1)S(1)}, u32[]{:S(2)}, u32[]{:S(2)}) collective-permute-start(bf16[256,128]{1,0:T(8,128)(2,1)S(1)} %get-tuple-element.55), channel_id=1, source_target_pairs={{0,6},{2,8},{4,10},{6,12},{8,14},{10,16},{12,18},{14,20},{16,22},{... | collective-permute-start | bytes 196616 | tf_op jit(solution)/shard_map/ppermute | solution.py:750
  50.8 7.5 %collective-permute-start.3 = (bf16[256,128]{1,0:T(8,128)(2,1)S(1)}, bf16[256,128]{1,0:T(8,128)(2,1)S(1)}, u32[]{:S(2)}, u32[]{:S(2)}) collective-permute-start(bf16[256,128]{1,0:T(8,128)(2,1)S(1)} %get-tuple-element.56), channel_id=1, source_target_pairs={{0,4},{2,6},{4,8},{6,10},{8,12},{10,14},{12,16},{14,18},{16,20},{1... | collective-permute-start | bytes 196616 | tf_op jit(solution)/shard_map/ppermute | solution.py:750
  54.2 6.3 %collective-permute-start.2 = (bf16[256,128]{1,0:T(8,128)(2,1)S(1)}, bf16[256,128]{1,0:T(8,128)(2,1)S(1)}, u32[]{:S(2)}, u32[]{:S(2)}) collective-permute-start(bf16[256,128]{1,0:T(8,128)(2,1)S(1)} %get-tuple-element.57), channel_id=1, source_target_pairs={{0,2},{2,4},{4,6},{6,8},{8,10},{10,12},{12,14},{14,16},{16,18},{18... | collective-permute-start | bytes 196616 | tf_op jit(solution)/shard_map/ppermute | solution.py:750
  63.7 25.9 %all-to-all-start.2 = ((bf16[16,176,128]{2,1,0:T(8,128)(2,1)}), bf16[16,176,128]{2,1,0:T(8,128)(2,1)S(1)}, u32[]{:S(2)}, u32[]{:S(2)}) async-start(bf16[16,176,128]{2,1,0:T(8,128)(2,1)} %shard_map.97), calls=%async_computation.2 | async-start | bytes 1441792 | tf_op jit(solution)/shard_map/all_to_all | solution.py:758
  71.1 1.7 %collective-permute-start.7 = (bf16[4,256,128]{2,1,0:T(8,128)(2,1)S(1)}, bf16[4,256,128]{2,1,0:T(8,128)(2,1)S(1)}, u32[]{:S(2)}, u32[]{:S(2)}) collective-permute-start(bf16[4,256,128]{2,1,0:T(8,128)(2,1)S(1)} %pad_maximum_fusion.own_faces_ref), channel_id=1, source_target_pairs={{0,1},{1,0},{2,3},{3,2},{4,5},{5,4},{6,7},{7,6},{8,9},{9,8},{10,11... | collective-permute-start | bytes 786440 | tf_op jit(solution)/shard_map/ppermute | solution.py:754
  71.2 1.6 %collective-permute-start.6 = (bf16[16,16,128]{2,1,0:T(8,128)(2,1)S(1)}, bf16[16,16,128]{2,1,0:T(8,128)(2,1)S(1)}, u32[]{:S(2)}, u32[]{:S(2)}) collective-permute-start(bf16[16,16,128]{2,1,0:T(8,128)(2,1)S(1)} %slice.19), channel_id=1, source_target_pairs={{0,1},{1,0},{2,3},{3,2},{4,5},{5,4},{6,7},{7,6},{8,9},{9,8},{10,11... | collective-permute-start | bytes 196616 | tf_op jit(solution)/shard_map/ppermute | solution.py:754
where the time goes:
time: 91.2 us; the launch traced here: 90.8 us
  Pallas kernels  36.3 us (40%)
  starting transfers between devices  35.2 us (39%)
  waiting for transfers between devices  18.5 us (20%)
    pallas_call x7, Pallas kernels, run(): return call(*placed)  36.3 us
    all_to_all x3, starting transfers between devices, to_all(): return lax.all_to_all(slots, 'space', 0, 0, tiled=True)  20.1 us
    ppermute x4, starting transfers between devices, over_space(): return lax.ppermute(block, ('space', 'chan'), route)  13.9 us
    all_to_all x3, waiting for transfers between devices, to_all(): return lax.all_to_all(slots, 'space', 0, 0, tiled=True)  13.6 us
    ppermute x4, waiting for transfers between devices, over_space(): return lax.ppermute(block, ('space', 'chan'), route)  3.79 us
  transfers between devices with their start and end apart: 11, of which 7 were waited for; matrix products, arithmetic and copies ran while one was open for 0% of the time, Pallas kernels for 28%

commit v1 on v0

--- a/solution.py
+++ b/solution.py
@@ -1,3 +1,5 @@
+import functools
+
 import jax
 import jax.numpy as jnp
 from jax import lax
@@ -14,6 +16,8 @@
 DIRECTIONS = [offset for offset in OFFSETS if offset != (0, 0, 0)]
 FILL_ORDER = sorted(range(26), key=lambda k: (abs(DIRECTIONS[k][2]), k))
 INACTIVE = -1e30
+NEAR, FAR = 4, 7
+INNER = 4
 F32 = jnp.float32
 BF16 = jnp.bfloat16
 
@@ -79,14 +83,12 @@
     return (level.astype(F32) < tall).astype(F32)
 
 
-def fill_slots(rows_ref, near_ref, slots_ref, start=0, faces=True):
+def fill_slots(rows_ref, near_ref, slots_ref):
     for k, (dx, dy, dz) in enumerate(DIRECTIONS):
         block = near_ref[0, k]
         xh = 7 if dx == 1 else 0
         y = 15 if dy == 1 else 0
         z = 15 if dz == 1 else 0
-        if not faces and (dx, dy, dz).count(0) == 2:
-            continue
 
         @pl.when(block >= 0)
         def _(dx=dx, dy=dy, dz=dz, xh=xh, y=y, z=z, block=block):
@@ -115,29 +117,48 @@
             else:
                 at = xh * 256 + y * 16 + z
                 region = jnp.broadcast_to(rows_ref[at : at + 1, :], (16, 128))
-            slots_ref[block, start : start + region.shape[0], :] = region.astype(BF16)
-
-
-def fill_faces(rows_ref, near_ref, place, faces_ref):
+            slots_ref[block, 0 : region.shape[0], :] = region.astype(BF16)
+
+
+def fill_regions(rows_ref, near_ref, place, near_out_ref, far_out_ref):
     member, own = place
     for k, (dx, dy, dz) in enumerate(DIRECTIONS):
-        if (dx, dy, dz).count(0) != 2:
-            continue
         block = near_ref[0, k]
         distance = jnp.where(member == 0, block - own, own - block)
-        end = 15 if dx + dy + dz == 1 else 0
-
-        @pl.when((block >= 0) & (distance >= 1))
-        def _(dx=dx, dy=dy, end=end, distance=distance):
-            if dx:
-                region = rows_ref[end * 256 : end * 256 + 256, :]
-            elif dy:
-                region = jnp.concatenate(
-                    [rows_ref[x * 256 + end * 16 : x * 256 + end * 16 + 16, :] for x in range(16)]
+        face = (dx, dy, dz).count(0) == 2
+        x, y, z = (15 if d == 1 else 0 for d in (dx, dy, dz))
+        wanted = (block >= 0) & (distance >= 1)
+
+        def region(dx=dx, dy=dy, dz=dz, x=x, y=y, z=z):
+            zeros = [d == 0 for d in (dx, dy, dz)]
+            if zeros == [False, True, True]:
+                rows = rows_ref[x * 256 : x * 256 + 256, :]
+            elif zeros == [True, False, True]:
+                rows = jnp.concatenate(
+                    [rows_ref[at * 256 + y * 16 : at * 256 + y * 16 + 16, :] for at in range(16)]
                 )
+            elif zeros == [True, True, False]:
+                rows = rows_ref[pl.ds(z, 256, stride=16), :]
+            elif zeros == [False, False, True]:
+                rows = rows_ref[x * 256 + y * 16 : x * 256 + y * 16 + 16, :]
+            elif zeros == [False, True, False]:
+                rows = rows_ref[pl.ds(x * 256 + z, 16, stride=16), :]
+            elif zeros == [True, False, False]:
+                rows = rows_ref[pl.ds(y * 16 + z, 16, stride=256), :]
             else:
-                region = rows_ref[pl.ds(end, 256, stride=16), :]
-            faces_ref[distance - 1] = region.astype(BF16)
+                at = x * 256 + y * 16 + z
+                rows = jnp.broadcast_to(rows_ref[at : at + 1, :], (16, 128))
+            return rows.astype(BF16)
+
+        @pl.when(wanted & (distance <= NEAR))
+        def _(region=region, distance=distance, height=256 if face else 16):
+            near_out_ref[distance - 1, 0:height, :] = region()
+
+        if not face:
+
+            @pl.when(wanted & (distance > NEAR))
+            def _(region=region, distance=distance):
+                far_out_ref[distance - 1 - NEAR] = region()
 
 
 class Whole:
@@ -218,37 +239,39 @@
         put_ends(padded, x, y * 16, rows[0:1], dz)
 
 
-def face_source(place, block):
-    away = place[1] - block
-    return jnp.where(away > 0, 0, 1) == place[0], jnp.clip(jnp.abs(away) - 1, 0, 3)
-
-
-def fill_margin(padded, near_ref, own_ref, other_ref, start=0, faces=None, z_faces=True):
+def fill_grad_margin(padded, near_ref, place, own_ref, other_ref):
+    for k in FILL_ORDER:
+        offset = DIRECTIONS[k]
+        block = near_ref[0, k]
+        height = 256 if offset.count(0) == 2 else 16
+        away = place[1] - block
+        distance = jnp.abs(away)
+        here = jnp.where(away > 0, 0, 1) == place[0]
+        far = NEAR * 256 + (distance - 1 - NEAR) * 16
+        start = (distance - 1) * 256 if height == 256 else jnp.where(
+            distance <= NEAR, (distance - 1) * 256, far
+        )
+
+        @pl.when(block >= 0)
+        def _(offset=offset, here=here, start=start, height=height):
+            span = pl.ds(pl.multiple_of(start, 16), height)
+            own = own_ref[span, :].astype(F32)
+            other = swap_halves(other_ref[span, :].astype(F32))
+            put_region(padded, offset, jnp.where(here, own, other))
+
+
+def fill_margin(padded, near_ref, own_ref, other_ref):
     for k in FILL_ORDER:
         offset = DIRECTIONS[k]
         block = near_ref[0, k]
         face = offset.count(0) == 2
-        if face and offset[2] and not z_faces:
-            continue
-        if face and faces is not None:
-            place, own_faces_ref, other_faces_ref = faces
-            here, slot = face_source(place, block)
-
-            @pl.when((block >= 0) & here)
-            def _(offset=offset, slot=slot):
-                put_region(padded, offset, own_faces_ref[slot].astype(F32))
-
-            @pl.when((block >= 0) & jnp.logical_not(here))
-            def _(offset=offset, slot=slot):
-                rows = swap_halves(other_faces_ref[slot].astype(F32))
-                put_region(padded, offset, rows)
-
+        if face and offset[2]:
             continue
 
         @pl.when(block >= 0)
         def _(offset=offset, block=block, face=face):
             height = 128 if face else 16
-            own = own_ref[block, start : start + height, :].astype(F32)
+            own = own_ref[block, 0:height, :].astype(F32)
             other = other_ref[block, 0:height, :].astype(F32)
             first = jnp.where(low_lanes(own), own, swap_halves(other))
             second = jnp.where(low_lanes(own), swap_halves(own), other)
@@ -342,7 +365,7 @@
     lanes_hbm, active_hbm, slope_hbm, inner_hbm, taps_hbm, down_out_hbm, cot_out_hbm,
     conv_in_ref, down_in_ref, cot_in_ref, heights_ref, own_ref, other_ref,
     two_ref, down_ref, cot_ref, padded_ref, rows_ref, mask_ref, lanes_ref, active_ref,
-    slope_ref, inner_ref, slope_wide_ref, arrived, left, left_inner
+    slope_ref, inner_ref, arrived, left, left_inner
 ):
     came = start_all(
         [
@@ -411,8 +434,7 @@
                 at = (2 * ux + tx) * 256 + (2 * uy + ty) * 16 + tz
                 source = (ux * 8 + uy) * 8
                 rows = pl.ds(at, 8, stride=2)
-                slope_wide_ref[rows, :] = part[source : source + 8] * mask_ref[rows, :]
-    slope_ref[...] = slope_wide_ref[...].astype(BF16)
+                slope_ref[rows, :] = part[source : source + 8] * mask_ref[rows, :]
     gone[5].start()
 
     def leave(group):
@@ -563,9 +585,9 @@
 def forward(
     near_ref, core_ref, at_ref, own_ref, other_ref, taps_ref, inner_ref, slope_ref,
     lanes_hbm, down_hbm, cot_hbm,
-    slots_hbm, faces_ref, coarse_hbm, grad_pre_hbm,
-    planes_ref, lines_ref, pre_ref, grad_ref, packed_ref, turned_ref, lanes_ref,
-    down_ref, cot_ref, coarse_ref, grad_pre_ref, slots_ref, arrived, left, left_slots
+    terms_hbm, near_out_ref, far_out_ref, coarse_hbm, grad_pre_hbm,
+    planes_ref, lines_ref, pre_ref, grad_ref, turned_ref, lanes_ref,
+    down_ref, cot_ref, coarse_ref, grad_pre_ref, terms_ref, arrived, left, left_terms
 ):
     came = start_all(
         [(lanes_hbm, lanes_ref), (down_hbm, down_ref), (cot_hbm, cot_ref)], arrived
@@ -574,7 +596,7 @@
     planes_ref[...] = jnp.zeros(planes_ref.shape, BF16)
     lines_ref[...] = jnp.zeros(lines_ref.shape, BF16)
     margin = Margin(planes_ref, lines_ref)
-    fill_margin(margin, near_ref, own_ref, other_ref, z_faces=False)
+    fill_margin(margin, near_ref, own_ref, other_ref)
     add_margin(planes_ref, lines_ref, near_ref, own_ref, other_ref, taps_ref, pre_ref)
 
     turned_ref[:, 0:512] = jnp.zeros((128, 512), BF16)
@@ -584,7 +606,7 @@
         pre = pre_ref[rows, :]
         sigmoid = 0.5 + 0.5 * jnp.tanh(0.5 * pre)
         pre_ref[rows, :] = jnp.where(pre > 0.5 * INACTIVE, pre * sigmoid, 0.0)
-        grad = slope_ref[rows, :].astype(F32) * sigmoid * (1.0 + pre * (1.0 - sigmoid))
+        grad = slope_ref[rows, :] * sigmoid * (1.0 + pre * (1.0 - sigmoid))
         grad_ref[rows, :] = grad
         grad = grad.astype(BF16)
         grad_pre_ref[rows, :] = grad
@@ -595,31 +617,15 @@
         pltpu.make_async_copy(coarse_ref, coarse_hbm, left.at[1]),
     ]
     gone[0].start()
-    fill_faces(grad_ref, near_ref, (core_ref[0], at_ref[0]), faces_ref)
-    share = slots_ref.shape[1] - 16
-    for x in range(8):
-        low = grad_ref[x * 256 : x * 256 + 256, :]
-        high = grad_ref[2048 + x * 256 : 2048 + x * 256 + 256, :]
-        packed_ref[x * 256 : x * 256 + 256, :] = jnp.where(
-            low_lanes(low), low, swap_halves(high)
+    fill_regions(grad_ref, near_ref, (core_ref[0], at_ref[0]), near_out_ref, far_out_ref)
+
+    def leave(i, first, last):
+        return pltpu.make_async_copy(
+            terms_ref.at[first:last], terms_hbm.at[first:last], left_terms.at[i]
         )
-    fill_slots(packed_ref, near_ref, slots_ref, share, faces=False)
-
-    def put_terms(at, rows):
-        while rows.shape[0]:
-            owner, row = at // share, at % share
-            count = min(rows.shape[0], share - row)
-            slots_ref[owner, row : row + count, :] = rows[:count]
-            rows = rows[count:]
-            at += count
-
-    ends = [1024 // share] + [(1024 + 576 * i) // share for i in (1, 2)] + [slots_ref.shape[0]]
-    leaving = [
-        pltpu.make_async_copy(
-            slots_ref.at[first:last], slots_hbm.at[first:last], left_slots.at[i]
-        )
-        for i, (first, last) in enumerate(zip([0] + ends, ends))
-    ]
+
+    ends = [1024, 1600, 2176, terms_ref.shape[0]]
+    leaving = [leave(i, first, last) for i, (first, last) in enumerate(zip([0] + ends, ends))]
 
     came[1].wait()
     came[2].wait()
@@ -640,7 +646,7 @@
     grad_down = jnp.dot(own_cot, patches, preferred_element_type=F32)
     for tap in range(8):
         part = grad_down[:, tap * 128 : tap * 128 + 128].T
-        put_terms(tap * 128, part.astype(BF16))
+        terms_ref[tap * 128 : tap * 128 + 128, :] = part.astype(BF16)
     leaving[0].start()
 
     came[0].wait()
@@ -653,7 +659,8 @@
         summed = jnp.dot(lhs, rhs, preferred_element_type=F32)
         for ex in range(3):
             part = summed[ex * 128 : ex * 128 + 128].T
-            put_terms(1024 + (ey * 3 + ex) * 192, part[0:192].astype(BF16))
+            at = 1024 + (ey * 3 + ex) * 192
+            terms_ref[at : at + 192, :] = part[0:192].astype(BF16)
         leaving[ey + 1].start()
     for copy in gone + leaving:
         copy.wait()
@@ -666,18 +673,27 @@
         copy.wait()
 
 
-def total(slots_ref, out_ref):
-    devices, share, _ = out_ref.shape
-    summed = slots_ref[0, 0:share, :].astype(F32)
-    for device in range(1, devices):
-        summed = summed + slots_ref[device, 0:share, :].astype(F32)
-    summed = (summed / devices).astype(BF16)
-    for device in range(devices):
-        out_ref[device] = summed
+def total(scale, parts_ref, out_hbm, sum_ref, left):
+    summed = parts_ref[0].astype(F32)
+    for part in range(1, parts_ref.shape[0]):
+        summed = summed + parts_ref[part].astype(F32)
+    sum_ref[...] = (summed * scale).astype(BF16)
+    repeat(sum_ref, out_hbm, left)
+
+
+def repeat(rows_ref, out_hbm, left):
+    copies = [
+        pltpu.make_async_copy(rows_ref, out_hbm.at[i], left.at[i])
+        for i in range(out_hbm.shape[0])
+    ]
+    for copy in copies:
+        copy.start()
+    for copy in copies:
+        copy.wait()
 
 
 def backward(
-    near_ref, core_ref, at_ref, own_ref, other_ref, own_faces_ref, other_faces_ref,
+    near_ref, core_ref, at_ref, own_ref, other_ref,
     grad_pre_hbm, active_hbm, conv_hbm, out_ref,
     padded_ref, grad_pre_ref, active_ref, conv_ref, back_ref, arrived
 ):
@@ -691,10 +707,8 @@
     for x in range(16):
         rows = grad_pre_ref[x * 256 : x * 256 + 256, :].astype(F32)
         put_lines(Whole(padded_ref), [(x + 1, 16, 256)], rows)
-    fill_margin(
-        Whole(padded_ref), near_ref, own_ref, other_ref, own_ref.shape[1] - 16,
-        ((core_ref[0], at_ref[0]), own_faces_ref, other_faces_ref),
-    )
+    place = (core_ref[0], at_ref[0])
+    fill_grad_margin(Whole(padded_ref), near_ref, place, own_ref, other_ref)
     came[2].wait()
     for half in range(2):
         lhs = []
@@ -758,6 +772,15 @@
     return lax.all_to_all(slots, "space", 0, 0, tiled=True)
 
 
+def to_group(slots, inner):
+    devices = lax.axis_size("space")
+    if inner:
+        groups = [[i + j for j in range(INNER)] for i in range(0, devices, INNER)]
+    else:
+        groups = [[i + j for j in range(0, devices, INNER)] for i in range(INNER)]
+    return lax.all_to_all(slots, "space", 0, 0, axis_index_groups=groups, tiled=True)
+
+
 def local(features, heights, neighbours, w_conv, w_down, cotangent):
     devices = lax.axis_size("space")
     member = lax.axis_index("chan")
@@ -796,7 +819,7 @@
     held = [
         held_out(18, 288, 256),
         held_out(4096, 128),
-        held_out(4096, 128),
+        held_out(4096, 128, dtype=F32),
         held_out(4096, 128, dtype=F32),
         held_out(3456, 128),
         held_out(1024, 256),
@@ -822,7 +845,6 @@
             memory(4096, 128, dtype=F32),
             memory(18, 288, 256),
             memory(4096, 128),
-            memory(4096, 128),
             memory(4096, 128, dtype=F32),
             memory(4096, 128, dtype=F32),
             copies(6),
@@ -836,36 +858,38 @@
     came_other = over_chan(came)
     taps, inner, slope = kernel_call(
         fetch,
-        [out(3456, 128), out(4096, 128, dtype=F32), out(4096, 128)],
+        [out(3456, 128), out(4096, 128, dtype=F32), out(4096, 128, dtype=F32)],
         [hbm()] * 3,
         [vmem()] * 3,
         [copies(3)],
     )(taps, inner, slope)
 
+    outer = devices // INNER
     share = -(-2752 // (devices * 16)) * 16
-    terms, faces, coarse, grad_pre = kernel_call(
+    height = share * outer
+    terms, near_out, far_out, coarse, grad_pre = kernel_call(
         forward,
         [
-            held_out(devices, share + 16, 128),
-            out(4, 256, 128),
+            held_out(INNER * height, 128),
+            out(NEAR, 256, 128),
+            out(FAR - NEAR, 16, 128),
             held_out(512, 128),
             held_out(4096, 128),
         ],
         [smem()] * 3 + [vmem()] * 5 + [hbm()] * 3,
-        [hbm(), vmem(), hbm(), hbm()],
+        [hbm(), vmem(), vmem(), hbm(), hbm()],
         [
             memory(2, 288, 384),
             memory(2, 256, 384),
             memory(4096, 128, dtype=F32),
             memory(4096, 128, dtype=F32),
-            memory(2048, 128, dtype=F32),
             memory(128, 5120),
             memory(18, 288, 256),
             memory(1024, 256),
             memory(512, 256),
             memory(512, 128),
             memory(4096, 128),
-            memory(devices, share + 16, 128),
+            memory(INNER * height, 128),
             copies(3),
             copies(2),
             copies(4),
@@ -876,19 +900,39 @@
         neighbours, *place, came, came_other, taps, inner, slope, lanes, down, cot
     )
 
-    arrived = to_all(terms)
-    came_faces = [over_space(faces[i], i + 1) for i in range(4)]
-    arrived, *came_faces = lax.optimization_barrier((arrived, *came_faces))
-    came_faces = jnp.stack(came_faces)
-    other_faces = over_chan(came_faces)
-    sums = to_all(
-        kernel_call(total, out(devices, share, 128), [vmem()], vmem())(arrived)
-    )
-    arrived_other = over_chan(arrived[:, share:])
+    def sum_of(parts, times, scale):
+        rows = parts.shape[1]
+        return kernel_call(
+            functools.partial(total, scale),
+            held_out(times, rows, 128),
+            [vmem()],
+            hbm(),
+            [memory(rows, 128), copies(times)],
+        )(parts)
+
+    arrived = to_group(terms.reshape(INNER, height, 128), True)
+    near_came = [over_space(near_out[i], i + 1) for i in range(NEAR)]
+    arrived, *near_came = lax.optimization_barrier((arrived, *near_came))
+    part = sum_of(arrived, 1, 1.0).reshape(outer, share, 128)
+    arrived = to_group(part, False)
+    far_came = [over_space(far_out[i], NEAR + i + 1) for i in range(FAR - NEAR)]
+    arrived, *far_came = lax.optimization_barrier((arrived, *far_came))
+    whole = to_group(sum_of(arrived, outer, 1.0 / devices), False)
+    own_regions = jnp.concatenate(near_came + far_came)
+    other_regions = over_chan(own_regions)
+    whole, own_regions, other_regions = lax.optimization_barrier(
+        (whole, own_regions, other_regions)
+    )
+    sums = to_group(
+        kernel_call(
+            repeat, held_out(INNER, height, 128), [vmem()], hbm(), [copies(INNER)]
+        )(whole.reshape(height, 128)),
+        True,
+    )
     grad_features = kernel_call(
         backward,
         out(8, 64, 512),
-        [smem()] * 3 + [vmem()] * 4 + [hbm()] * 3,
+        [smem()] * 3 + [vmem()] * 2 + [hbm()] * 3,
         vmem(),
         [
             memory(18, 288, 384),
@@ -900,10 +944,7 @@
         ],
         flops=5 << 30,
         mib=24,
-    )(
-        neighbours, *place, arrived, arrived_other, came_faces, other_faces, grad_pre, active,
-        w_conv,
-    )
+    )(neighbours, *place, own_regions, other_regions, grad_pre, active, w_conv)
 
     grad_conv, grad_down = kernel_call(
         finish,

time: 91.2 us -> 101 us (1.11)
  blocking collectives: 0 us -> 11.4 us
  waiting for transfers between devices: 18.5 us -> 9.99 us
  starting transfers between devices: 35.2 us -> 39.2 us
  Pallas kernels: 36.3 us -> 38.5 us
    all_to_all x3 -> x1, starting transfers between devices: 20.1 us -> 7.89 us  [to_all(): return lax.all_to_all(slots, 'space', 0, 0, tiled=True)]
    all_to_all x0 -> x1, blocking collectives: none -> 11.4 us  [to_group(): lax.all_to_all(slots, 'space', 0, 0, axis_index_groups=groups, tiled=True)]
    all_to_all x0 -> x3, starting transfers between devices: none -> 10.4 us  [to_group(): lax.all_to_all(slots, 'space', 0, 0, axis_index_groups=groups, tiled=True)]
    all_to_all x3 -> x1, waiting for transfers between devices: 13.6 us -> 3.98 us  [to_all(): return lax.all_to_all(slots, 'space', 0, 0, tiled=True)]
    ppermute x4 -> x7, starting transfers between devices: 13.9 us -> 20.3 us  [over_space(): return lax.ppermute(block, ('space', 'chan'), route)]
    all_to_all x0 -> x3, waiting for transfers between devices: none -> 5.98 us  [to_group(): lax.all_to_all(slots, 'space', 0, 0, axis_index_groups=groups, tiled=True)]
    ppermute x4 -> x7, waiting for transfers between devices: 3.79 us -> 0.02 us  [over_space(): return lax.ppermute(block, ('space', 'chan'), route)]
    pallas_call x7 -> x9, Pallas kernels: 36.3 us -> 38.5 us  [run(): return call(*placed)]
  transfers between devices with their start and end apart: 11 -> 14, of which waited for: 7 -> 2; matrix products, arithmetic and copies ran while one was open for 0% -> 0% of each run, Pallas kernels for 28% -> 27%
where the time goes in v1:
time: 101 us; the launch traced here: 100 us
  starting transfers between devices  39.2 us (39%)
  Pallas kernels  38.5 us (38%)
  blocking collectives  11.4 us (11%)
  waiting for transfers between devices  9.99 us (10%)
    pallas_call x9, Pallas kernels, run(): return call(*placed)  38.5 us
    ppermute x7, starting transfers between devices, over_space(): return lax.ppermute(block, ('space', 'chan'), route)  20.3 us
    all_to_all x1, blocking collectives, to_group(): lax.all_to_all(slots, 'space', 0, 0, axis_index_groups=groups, tiled=True)  11.4 us
    all_to_all x3, starting transfers between devices, to_group(): lax.all_to_all(slots, 'space', 0, 0, axis_index_groups=groups, tiled=True)  10.4 us
    all_to_all x1, starting transfers between devices, to_all(): return lax.all_to_all(slots, 'space', 0, 0, tiled=True)  7.89 us
    all_to_all x3, waiting for transfers between devices, to_group(): lax.all_to_all(slots, 'space', 0, 0, axis_index_groups=groups, tiled=True)  5.98 us
    all_to_all x1, waiting for transfers between devices, to_all(): return lax.all_to_all(slots, 'space', 0, 0, tiled=True)  3.98 us
  transfers between devices with their start and end apart: 14, of which 2 were waited for; matrix products, arithmetic and copies ran while one was open for 0% of the time, Pallas kernels for 27%

profile of v1, /device:TPU:0, one launch (start us, length us, event | category | flops | bytes accessed | tf_op | source)
XLA Modules:
  0.0 100.1 jit_solution(10212357387690307030)
XLA Ops:
  0.6 0.5 collective-permute-start
  1.1 2.6 %shard_map.93 = bf16[16,128,128]{2,1,0:T(8,128)(2,1)} custom-call(s32[1,26]{1,0:T(1,128)} %near_ref.3, s32[8,64]{1,0:T(8,128)} %heights_hbm.3, bf16[8,64,512]{2,1,0:T(8,128)(2,1)} %bitcast.29), custom_call_target="tpu_custom_call" | custom-call | bytes 4194304 | tf_op jit(solution)/shard_map/pallas_call | solution.py:54
  3.7 7.9 %all-to-all-start = ((bf16[16,128,128]{2,1,0:T(8,128)(2,1)}), bf16[16,128,128]{2,1,0:T(8,128)(2,1)S(1)}, u32[]{:S(2)}, u32[]{:S(2)}) async-start(bf16[16,128,128]{2,1,0:T(8,128)(2,1)} %shard_map.93), calls=%async_computation | async-start | bytes 1048576 | tf_op jit(solution)/shard_map/all_to_all | solution.py:772
  11.6 0.0 collective-permute-done.other_hbm
  11.7 11.5 %shard_map.94 = (bf16[18,288,256]{2,1,0:T(8,128)(2,1)}, bf16[4096,128]{1,0:T(8,128)(2,1)}, f32[4096,128]{1,0:T(8,128)}, f32[4096,128]{1,0:T(8,128)}, bf16[3456,1...) custom-call(s32[1]{0:T(128)} %bitcast.core_ref, bf16[27,128,128]{2,1,0:T(8,128)(2,1)} %conv_hbm.3, ...), custom_call_target="tpu_custom_call" | custom-call | flops 5368709120 | bytes 4194304 | tf_op jit(solution)/shard_map/pallas_call | solution.py:54
  23.1 4.0 %all-to-all-done.own_ref = bf16[16,128,128]{2,1,0:T(8,128)(2,1)S(1)} async-done(((bf16[16,128,128]{2,1,0:T(8,128)(2,1)}), bf16[16,128,128]{2,1,0:T(8,128)(2,1)S(1)}, u32[]{:S(2)}, u32[]{:S(2)}) %all-to-all-start) | async-done | bytes 524320 | tf_op jit(solution)/shard_map/all_to_all | solution.py:772
  27.1 0.0 collective-permute-start.1
  27.1 0.0 copy-start
  27.1 2.5 %shard_map.95 = (bf16[3456,128]{1,0:T(8,128)(2,1)S(1)}, f32[4096,128]{1,0:T(8,128)S(1)}, f32[4096,128]{1,0:T(8,128)S(1)}) custom-call(bf16[3456,128]{1,0:T(8,128)(2,1)} %get-tuple-element.41.taps_hbm, f32[4096,128]{1,0:T(8,128)} %get-tuple-element.42.inner_hbm, f32[4096,128]{1,0:T(8,128)} %get-tuple-element.43.slope_hbm), custom_call_target="tpu_custom_call" | custom-call | bytes 4194304 | tf_op jit(solution)/shard_map/pallas_call | solution.py:54
  29.7 0.0 collective-permute-done.1.other_ref
  29.7 0.0 copy-done
  29.7 8.9 %shard_map.96 = (bf16[2816,128]{1,0:T(8,128)(2,1)}, bf16[4,256,128]{2,1,0:T(8,128)(2,1)S(1)}, bf16[3,16,128]{2,1,0:T(8,128)(2,1)S(1)}, bf16[512,128]{1,0:T(8,128)(2,1)}, bf16[4096,128]{1,0:T(8,128)(2,1)}) custom-call(s32[1,26]{1,0:T(1,128)S(1)} %copy-done, s32[1]{0:T(128)} %bitcast.core_ref, s32[1]{0:T(128)} %bitcast.1.at_ref, ...), custom_call_target="tpu_custom_call" | custom-call | flops 5368709120 | bytes 4194304 | tf_op jit(solution)/shard_map/pallas_call | solution.py:54
  38.6 3.5 %all-to-all-start.1 = ((bf16[4,704,128]{2,1,0:T(8,128)(2,1)}), bf16[4,704,128]{2,1,0:T(8,128)(2,1)S(1)}, u32[]{:S(2)}, u32[]{:S(2)}) async-start(bf16[4,704,128]{2,1,0:T(8,128)(2,1)} %bitcast.27), calls=%async_computation.1 | async-start | bytes 1441792 | tf_op jit(solution)/shard_map/all_to_all | solution.py:781
  42.1 3.0 %collective-permute-start.5 = (bf16[256,128]{1,0:T(8,128)(2,1)S(1)}, bf16[256,128]{1,0:T(8,128)(2,1)S(1)}, u32[]{:S(2)}, u32[]{:S(2)}) collective-permute-start(bf16[256,128]{1,0:T(8,128)(2,1)S(1)} %get-tuple-element.70), channel_id=1, source_target_pairs={{0,8},{2,10},{4,12},{6,14},{8,16},{10,18},{12,20},{14,22},{16,24},... | collective-permute-start | bytes 196616 | tf_op jit(solution)/shard_map/ppermute | solution.py:764
  45.1 4.8 %collective-permute-start.4 = (bf16[256,128]{1,0:T(8,128)(2,1)S(1)}, bf16[256,128]{1,0:T(8,128)(2,1)S(1)}, u32[]{:S(2)}, u32[]{:S(2)}) collective-permute-start(bf16[256,128]{1,0:T(8,128)(2,1)S(1)} %get-tuple-element.71), channel_id=1, source_target_pairs={{0,6},{2,8},{4,10},{6,12},{8,14},{10,16},{12,18},{14,20},{16,22},{... | collective-permute-start | bytes 196616 | tf_op jit(solution)/shard_map/ppermute | solution.py:764
  49.9 2.6 %collective-permute-start.3 = (bf16[256,128]{1,0:T(8,128)(2,1)S(1)}, bf16[256,128]{1,0:T(8,128)(2,1)S(1)}, u32[]{:S(2)}, u32[]{:S(2)}) collective-permute-start(bf16[256,128]{1,0:T(8,128)(2,1)S(1)} %get-tuple-element.72), channel_id=1, source_target_pairs={{0,4},{2,6},{4,8},{6,10},{8,12},{10,14},{12,16},{14,18},{16,20},{1... | collective-permute-start | bytes 196616 | tf_op jit(solution)/shard_map/ppermute | solution.py:764
  52.5 2.5 %collective-permute-start.2 = (bf16[256,128]{1,0:T(8,128)(2,1)S(1)}, bf16[256,128]{1,0:T(8,128)(2,1)S(1)}, u32[]{:S(2)}, u32[]{:S(2)}) collective-permute-start(bf16[256,128]{1,0:T(8,128)(2,1)S(1)} %get-tuple-element.73), channel_id=1, source_target_pairs={{0,2},{2,4},{4,6},{6,8},{8,10},{10,12},{12,14},{14,16},{16,18},{18... | collective-permute-start | bytes 196616 | tf_op jit(solution)/shard_map/ppermute | solution.py:764
  55.0 4.4 %collective-permute-start.8 = (bf16[16,128]{1,0:T(8,128)(2,1)S(1)}, bf16[16,128]{1,0:T(8,128)(2,1)S(1)}, u32[]{:S(2)}, u32[]{:S(2)}) collective-permute-start(bf16[16,128]{1,0:T(8,128)(2,1)S(1)} %get-tuple-element.74), channel_id=1, source_target_pairs={{0,14},{2,16},{4,18},{6,20},{8,22},{10,24},{12,26},{14,28},{16,30}... | collective-permute-start | bytes 12296 | tf_op jit(solution)/shard_map/ppermute | solution.py:764
  59.4 0.0 collective-permute-done.5
  59.4 1.3 %collective-permute-start.7 = (bf16[16,128]{1,0:T(8,128)(2,1)S(1)}, bf16[16,128]{1,0:T(8,128)(2,1)S(1)}, u32[]{:S(2)}, u32[]{:S(2)}) collective-permute-start(bf16[16,128]{1,0:T(8,128)(2,1)S(1)} %get-tuple-element.75), channel_id=1, source_target_pairs={{0,12},{2,14},{4,16},{6,18},{8,20},{10,22},{12,24},{14,26},{16,28}... | collective-permute-start | bytes 12296 | tf_op jit(solution)/shard_map/ppermute | solution.py:764
  60.7 0.0 collective-permute-done.4
  60.7 1.8 %collective-permute-start.6 = (bf16[16,128]{1,0:T(8,128)(2,1)S(1)}, bf16[16,128]{1,0:T(8,128)(2,1)S(1)}, u32[]{:S(2)}, u32[]{:S(2)}) collective-permute-start(bf16[16,128]{1,0:T(8,128)(2,1)S(1)} %get-tuple-element.76), channel_id=1, source_target_pairs={{0,10},{2,12},{4,14},{6,16},{8,18},{10,20},{12,22},{14,24},{16,26}... | collective-permute-start | bytes 12296 | tf_op jit(solution)/shard_map/ppermute | solution.py:764
  62.5 0.0 collective-permute-done.3
  62.5 0.0 collective-permute-done.2
  62.5 0.0 all-to-all-done.1.parts_ref
  62.6 0.8 shard_map.97
  63.3 3.4 %all-to-all-start.2 = ((bf16[4,176,128]{2,1,0:T(8,128)(2,1)}), bf16[4,176,128]{2,1,0:T(8,128)(2,1)S(1)}, u32[]{:S(2)}, u32[]{:S(2)}) async-start(bf16[4,176,128]{2,1,0:T(8,128)(2,1)} %bitcast.26), calls=%async_computation.2 | async-start | bytes 360448 | tf_op jit(solution)/shard_map/all_to_all | solution.py:781
  66.8 0.0 collective-permute-done.8
  66.8 0.0 collective-permute-done.7
  66.8 0.0 collective-permute-done.6
  66.8 6.0 %all-to-all-done.2.parts_ref = bf16[4,176,128]{2,1,0:T(8,128)(2,1)S(1)} async-done(((bf16[4,176,128]{2,1,0:T(8,128)(2,1)}), bf16[4,176,128]{2,1,0:T(8,128)(2,1)S(1)}, u32[]{:S(2)}, u32[]{:S(2)}) %all-to-all-start.2) | async-done | bytes 180256 | tf_op jit(solution)/shard_map/all_to_all | solution.py:781
  72.8 0.1 collective-permute-start.9
  72.9 0.7 shard_map.98
  73.6 11.4 %all_to_all.25 = bf16[4,176,128]{2,1,0:T(8,128)(2,1)S(1)} all-to-all(bf16[4,176,128]{2,1,0:T(8,128)(2,1)} %shard_map.98), channel_id=1, replica_groups={{0,8,16,24},{2,10,18,26},{4,12,20,28},{6,14,22,30},{1,9,17,25},{3,11,19..., dimensions={0} | all-to-all | bytes 360448 | tf_op jit(solution)/shard_map/all_to_all | solution.py:781
  85.0 0.0 collective-permute-done.9.other_ref
  85.0 0.9 shard_map.99
  85.9 3.5 %all-to-all-start.4 = ((bf16[4,704,128]{2,1,0:T(8,128)(2,1)}), bf16[4,704,128]{2,1,0:T(8,128)(2,1)S(1)}, u32[]{:S(2)}, u32[]{:S(2)}) async-start(bf16[4,704,128]{2,1,0:T(8,128)(2,1)} %shard_map.99), calls=%async_computation.4 | async-start | bytes 1441792 | tf_op jit(solution)/shard_map/all_to_all | solution.py:781
  89.4 9.4 %shard_map.101 = bf16[8,64,512]{2,1,0:T(8,128)(2,1)} custom-call(s32[1,26]{1,0:T(1,128)S(1)} %copy-done, s32[1]{0:T(128)} %bitcast.core_ref, s32[1]{0:T(128)} %bitcast.1.at_ref, bf16[1072,128]{1,0:T(8,128)(2,1)S(1)} %constant_dynamic-update-slice_fusion.own_ref, bf16[1072,128]{1,0:T(8,128)(2,1)S(1)} %collective-permute-done.9.other_ref, ...), custom_call_target="tpu_custom_call" | custom-call | flops 5368709120 | bytes 4194304 | tf_op jit(solution)/shard_map/pallas_call | solution.py:54
  98.8 0.0 all-to-all-done.4
  98.8 1.2 %shard_map.100 = (f32[27,64,128]{2,1,0:T(8,128)}, f32[8,128,128]{2,1,0:T(8,128)}) custom-call(s32[1]{0:T(128)} %bitcast.core_ref, bf16[2816,128]{1,0:T(8,128)(2,1)S(1)} %bitcast.24), custom_call_target="tpu_custom_call" | custom-call | bytes 4194304 | tf_op jit(solution)/shard_map/pallas_call | solution.py:54
  (9 shorter events, 0.1 us)
Async XLA Ops:
  0.6 11.0 %collective-permute-start = (bf16[8,64,512]{2,1,0:T(8,128)(2,1)}, bf16[8,64,512]{2,1,0:T(8,128)(2,1)S(1)}, u32[]{:S(2)}, u32[]{:S(2)}) collective-permute-start(bf16[8,64,512]{2,1,0:T(8,128)(2,1)} %bitcast.28), channel_id=1, source_target_pairs={{0,1},{1,0},{2,3},{3,2},{4,5},{5,4},{6,7},{7,6},{8,9},{9,8},{10,11... | collective-permute-start | bytes 1572872 | tf_op jit(solution)/shard_map/ppermute | solution.py:768
  3.7 23.4 %all-to-all-start = ((bf16[16,128,128]{2,1,0:T(8,128)(2,1)}), bf16[16,128,128]{2,1,0:T(8,128)(2,1)S(1)}, u32[]{:S(2)}, u32[]{:S(2)}) async-start(bf16[16,128,128]{2,1,0:T(8,128)(2,1)} %shard_map.93), calls=%async_computation | async-start | bytes 1048576 | tf_op jit(solution)/shard_map/all_to_all | solution.py:772
  27.1 2.6 %collective-permute-start.1 = (bf16[16,128,128]{2,1,0:T(8,128)(2,1)S(1)}, bf16[16,128,128]{2,1,0:T(8,128)(2,1)S(1)}, u32[]{:S(2)}, u32[]{:S(2)}) collective-permute-start(bf16[16,128,128]{2,1,0:T(8,128)(2,1)S(1)} %all-to-all-done.own_ref), channel_id=1, source_target_pairs={{0,1},{1,0},{2,3},{3,2},{4,5},{5,4},{6,7},{7,6},{8,9},{9,8},{10,11... | collective-permute-start | bytes 1572872 | tf_op jit(solution)/shard_map/ppermute | solution.py:768
  27.1 2.6 %copy-start = (s32[1,26]{1,0:T(1,128)S(1)}, s32[1,26]{1,0:T(1,128)}, u32[]{:S(2)}) copy-start(s32[1,26]{1,0:T(1,128)} %near_ref.3) | copy-start | bytes 316
  38.6 24.0 %all-to-all-start.1 = ((bf16[4,704,128]{2,1,0:T(8,128)(2,1)}), bf16[4,704,128]{2,1,0:T(8,128)(2,1)S(1)}, u32[]{:S(2)}, u32[]{:S(2)}) async-start(bf16[4,704,128]{2,1,0:T(8,128)(2,1)} %bitcast.27), calls=%async_computation.1 | async-start | bytes 1441792 | tf_op jit(solution)/shard_map/all_to_all | solution.py:781
  42.1 17.2 %collective-permute-start.5 = (bf16[256,128]{1,0:T(8,128)(2,1)S(1)}, bf16[256,128]{1,0:T(8,128)(2,1)S(1)}, u32[]{:S(2)}, u32[]{:S(2)}) collective-permute-start(bf16[256,128]{1,0:T(8,128)(2,1)S(1)} %get-tuple-element.70), channel_id=1, source_target_pairs={{0,8},{2,10},{4,12},{6,14},{8,16},{10,18},{12,20},{14,22},{16,24},... | collective-permute-start | bytes 196616 | tf_op jit(solution)/shard_map/ppermute | solution.py:764
  45.1 15.6 %collective-permute-start.4 = (bf16[256,128]{1,0:T(8,128)(2,1)S(1)}, bf16[256,128]{1,0:T(8,128)(2,1)S(1)}, u32[]{:S(2)}, u32[]{:S(2)}) collective-permute-start(bf16[256,128]{1,0:T(8,128)(2,1)S(1)} %get-tuple-element.71), channel_id=1, source_target_pairs={{0,6},{2,8},{4,10},{6,12},{8,14},{10,16},{12,18},{14,20},{16,22},{... | collective-permute-start | bytes 196616 | tf_op jit(solution)/shard_map/ppermute | solution.py:764
  49.9 12.6 %collective-permute-start.3 = (bf16[256,128]{1,0:T(8,128)(2,1)S(1)}, bf16[256,128]{1,0:T(8,128)(2,1)S(1)}, u32[]{:S(2)}, u32[]{:S(2)}) collective-permute-start(bf16[256,128]{1,0:T(8,128)(2,1)S(1)} %get-tuple-element.72), channel_id=1, source_target_pairs={{0,4},{2,6},{4,8},{6,10},{8,12},{10,14},{12,16},{14,18},{16,20},{1... | collective-permute-start | bytes 196616 | tf_op jit(solution)/shard_map/ppermute | solution.py:764
  52.5 10.1 %collective-permute-start.2 = (bf16[256,128]{1,0:T(8,128)(2,1)S(1)}, bf16[256,128]{1,0:T(8,128)(2,1)S(1)}, u32[]{:S(2)}, u32[]{:S(2)}) collective-permute-start(bf16[256,128]{1,0:T(8,128)(2,1)S(1)} %get-tuple-element.73), channel_id=1, source_target_pairs={{0,2},{2,4},{4,6},{6,8},{8,10},{10,12},{12,14},{14,16},{16,18},{18... | collective-permute-start | bytes 196616 | tf_op jit(solution)/shard_map/ppermute | solution.py:764
  55.0 11.8 %collective-permute-start.8 = (bf16[16,128]{1,0:T(8,128)(2,1)S(1)}, bf16[16,128]{1,0:T(8,128)(2,1)S(1)}, u32[]{:S(2)}, u32[]{:S(2)}) collective-permute-start(bf16[16,128]{1,0:T(8,128)(2,1)S(1)} %get-tuple-element.74), channel_id=1, source_target_pairs={{0,14},{2,16},{4,18},{6,20},{8,22},{10,24},{12,26},{14,28},{16,30}... | collective-permute-start | bytes 12296 | tf_op jit(solution)/shard_map/ppermute | solution.py:764
  59.4 7.4 %collective-permute-start.7 = (bf16[16,128]{1,0:T(8,128)(2,1)S(1)}, bf16[16,128]{1,0:T(8,128)(2,1)S(1)}, u32[]{:S(2)}, u32[]{:S(2)}) collective-permute-start(bf16[16,128]{1,0:T(8,128)(2,1)S(1)} %get-tuple-element.75), channel_id=1, source_target_pairs={{0,12},{2,14},{4,16},{6,18},{8,20},{10,22},{12,24},{14,26},{16,28}... | collective-permute-start | bytes 12296 | tf_op jit(solution)/shard_map/ppermute | solution.py:764
  60.7 6.1 %collective-permute-start.6 = (bf16[16,128]{1,0:T(8,128)(2,1)S(1)}, bf16[16,128]{1,0:T(8,128)(2,1)S(1)}, u32[]{:S(2)}, u32[]{:S(2)}) collective-permute-start(bf16[16,128]{1,0:T(8,128)(2,1)S(1)} %get-tuple-element.76), channel_id=1, source_target_pairs={{0,10},{2,12},{4,14},{6,16},{8,18},{10,20},{12,22},{14,24},{16,26}... | collective-permute-start | bytes 12296 | tf_op jit(solution)/shard_map/ppermute | solution.py:764
  63.3 9.5 %all-to-all-start.2 = ((bf16[4,176,128]{2,1,0:T(8,128)(2,1)}), bf16[4,176,128]{2,1,0:T(8,128)(2,1)S(1)}, u32[]{:S(2)}, u32[]{:S(2)}) async-start(bf16[4,176,128]{2,1,0:T(8,128)(2,1)} %bitcast.26), calls=%async_computation.2 | async-start | bytes 360448 | tf_op jit(solution)/shard_map/all_to_all | solution.py:781
  72.8 12.2 %collective-permute-start.9 = (bf16[1072,128]{1,0:T(8,128)(2,1)S(1)}, bf16[1072,128]{1,0:T(8,128)(2,1)S(1)}, u32[]{:S(2)}, u32[]{:S(2)}) collective-permute-start(bf16[1072,128]{1,0:T(8,128)(2,1)S(1)} %constant_dynamic-update-slice_fusion.own_ref), channel_id=1, source_target_pairs={{0,1},{1,0},{2,3},{3,2},{4,5},{5,4},{6,7},{7,6},{8,9},{9,8},{10,11... | collective-permute-start | bytes 823304 | tf_op jit(solution)/shard_map/ppermute | solution.py:768
  85.9 12.9 %all-to-all-start.4 = ((bf16[4,704,128]{2,1,0:T(8,128)(2,1)}), bf16[4,704,128]{2,1,0:T(8,128)(2,1)S(1)}, u32[]{:S(2)}, u32[]{:S(2)}) async-start(bf16[4,704,128]{2,1,0:T(8,128)(2,1)} %shard_map.99), calls=%async_computation.4 | async-start | bytes 1441792 | tf_op jit(solution)/shard_map/all_to_all | solution.py:781

commit v2 on v0

--- a/solution.py
+++ b/solution.py
@@ -79,14 +79,12 @@
     return (level.astype(F32) < tall).astype(F32)
 
 
-def fill_slots(rows_ref, near_ref, slots_ref, start=0, faces=True):
+def fill_slots(rows_ref, near_ref, slots_ref):
     for k, (dx, dy, dz) in enumerate(DIRECTIONS):
         block = near_ref[0, k]
         xh = 7 if dx == 1 else 0
         y = 15 if dy == 1 else 0
         z = 15 if dz == 1 else 0
-        if not faces and (dx, dy, dz).count(0) == 2:
-            continue
 
         @pl.when(block >= 0)
         def _(dx=dx, dy=dy, dz=dz, xh=xh, y=y, z=z, block=block):
@@ -115,7 +113,33 @@
             else:
                 at = xh * 256 + y * 16 + z
                 region = jnp.broadcast_to(rows_ref[at : at + 1, :], (16, 128))
-            slots_ref[block, start : start + region.shape[0], :] = region.astype(BF16)
+            slots_ref[block, 0 : region.shape[0], :] = region.astype(BF16)
+
+
+def fill_edges(rows_ref, near_ref, slots_ref, start):
+    for k, (dx, dy, dz) in enumerate(DIRECTIONS):
+        if (dx, dy, dz).count(0) == 2:
+            continue
+        block = near_ref[0, k]
+        x, y, z = (15 if d == 1 else 0 for d in (dx, dy, dz))
+
+        @pl.when(block >= 0)
+        def _(dx=dx, dy=dy, dz=dz, x=x, y=y, z=z, block=block):
+            if dx == 0:
+                line = rows_ref[pl.ds(y * 16 + z, 16, stride=256), :]
+                low, high = line[:8], swap_halves(line[8:])
+                line = jnp.where(low_lanes(low), low, high)
+                rows = jnp.concatenate([line, line])
+            elif dz == 0:
+                rows = rows_ref[x * 256 + y * 16 : x * 256 + y * 16 + 16, :]
+            elif dy == 0:
+                rows = rows_ref[pl.ds(x * 256 + z, 16, stride=16), :]
+            else:
+                at = x * 256 + y * 16 + z
+                rows = jnp.broadcast_to(rows_ref[at : at + 1, :], (16, 128))
+            if dx == 1:
+                rows = swap_halves(rows)
+            slots_ref[block, start : start + 16, :] = rows.astype(BF16)
 
 
 def fill_faces(rows_ref, near_ref, place, faces_ref):
@@ -342,7 +366,7 @@
     lanes_hbm, active_hbm, slope_hbm, inner_hbm, taps_hbm, down_out_hbm, cot_out_hbm,
     conv_in_ref, down_in_ref, cot_in_ref, heights_ref, own_ref, other_ref,
     two_ref, down_ref, cot_ref, padded_ref, rows_ref, mask_ref, lanes_ref, active_ref,
-    slope_ref, inner_ref, slope_wide_ref, arrived, left, left_inner
+    slope_ref, inner_ref, arrived, left, left_inner
 ):
     came = start_all(
         [
@@ -411,8 +435,7 @@
                 at = (2 * ux + tx) * 256 + (2 * uy + ty) * 16 + tz
                 source = (ux * 8 + uy) * 8
                 rows = pl.ds(at, 8, stride=2)
-                slope_wide_ref[rows, :] = part[source : source + 8] * mask_ref[rows, :]
-    slope_ref[...] = slope_wide_ref[...].astype(BF16)
+                slope_ref[rows, :] = part[source : source + 8] * mask_ref[rows, :]
     gone[5].start()
 
     def leave(group):
@@ -561,14 +584,20 @@
 
 
 def forward(
-    near_ref, core_ref, at_ref, own_ref, other_ref, taps_ref, inner_ref, slope_ref,
-    lanes_hbm, down_hbm, cot_hbm,
+    near_ref, core_ref, at_ref, own_ref, other_ref, taps_ref, inner_ref,
+    slope_hbm, lanes_hbm, down_hbm, cot_hbm,
     slots_hbm, faces_ref, coarse_hbm, grad_pre_hbm,
-    planes_ref, lines_ref, pre_ref, grad_ref, packed_ref, turned_ref, lanes_ref,
+    planes_ref, lines_ref, pre_ref, grad_ref, turned_ref, slope_ref, lanes_ref,
     down_ref, cot_ref, coarse_ref, grad_pre_ref, slots_ref, arrived, left, left_slots
 ):
     came = start_all(
-        [(lanes_hbm, lanes_ref), (down_hbm, down_ref), (cot_hbm, cot_ref)], arrived
+        [
+            (slope_hbm, slope_ref),
+            (lanes_hbm, lanes_ref),
+            (down_hbm, down_ref),
+            (cot_hbm, cot_ref),
+        ],
+        arrived,
     )
     pre_ref[...] = inner_ref[...]
     planes_ref[...] = jnp.zeros(planes_ref.shape, BF16)
@@ -576,6 +605,7 @@
     margin = Margin(planes_ref, lines_ref)
     fill_margin(margin, near_ref, own_ref, other_ref, z_faces=False)
     add_margin(planes_ref, lines_ref, near_ref, own_ref, other_ref, taps_ref, pre_ref)
+    came[0].wait()
 
     turned_ref[:, 0:512] = jnp.zeros((128, 512), BF16)
     turned_ref[:, 4608:5120] = jnp.zeros((128, 512), BF16)
@@ -584,7 +614,7 @@
         pre = pre_ref[rows, :]
         sigmoid = 0.5 + 0.5 * jnp.tanh(0.5 * pre)
         pre_ref[rows, :] = jnp.where(pre > 0.5 * INACTIVE, pre * sigmoid, 0.0)
-        grad = slope_ref[rows, :].astype(F32) * sigmoid * (1.0 + pre * (1.0 - sigmoid))
+        grad = slope_ref[rows, :] * sigmoid * (1.0 + pre * (1.0 - sigmoid))
         grad_ref[rows, :] = grad
         grad = grad.astype(BF16)
         grad_pre_ref[rows, :] = grad
@@ -597,13 +627,7 @@
     gone[0].start()
     fill_faces(grad_ref, near_ref, (core_ref[0], at_ref[0]), faces_ref)
     share = slots_ref.shape[1] - 16
-    for x in range(8):
-        low = grad_ref[x * 256 : x * 256 + 256, :]
-        high = grad_ref[2048 + x * 256 : 2048 + x * 256 + 256, :]
-        packed_ref[x * 256 : x * 256 + 256, :] = jnp.where(
-            low_lanes(low), low, swap_halves(high)
-        )
-    fill_slots(packed_ref, near_ref, slots_ref, share, faces=False)
+    fill_edges(grad_ref, near_ref, slots_ref, share)
 
     def put_terms(at, rows):
         while rows.shape[0]:
@@ -621,8 +645,8 @@
         for i, (first, last) in enumerate(zip([0] + ends, ends))
     ]
 
-    came[1].wait()
     came[2].wait()
+    came[3].wait()
     patches = []
     for tap in range(8):
         tx, ty, tz = tap // 4, tap // 2 % 2, tap % 2
@@ -643,7 +667,7 @@
         put_terms(tap * 128, part.astype(BF16))
     leaving[0].start()
 
-    came[0].wait()
+    came[1].wait()
     put_own_margin(planes_ref, lines_ref, near_ref, own_ref, other_ref, lanes_ref)
     lhs = jnp.concatenate(
         [turned_ref[:, (2 - ex) * 256 : (2 - ex) * 256 + 4608] for ex in range(3)]
@@ -659,21 +683,24 @@
         copy.wait()
 
 
-def fetch(taps_hbm, inner_hbm, slope_hbm, taps_ref, inner_ref, slope_ref, arrived):
-    for copy in start_all(
-        [(taps_hbm, taps_ref), (inner_hbm, inner_ref), (slope_hbm, slope_ref)], arrived
-    ):
+def fetch(taps_hbm, inner_hbm, taps_ref, inner_ref, arrived):
+    for copy in start_all([(taps_hbm, taps_ref), (inner_hbm, inner_ref)], arrived):
         copy.wait()
 
 
-def total(slots_ref, out_ref):
-    devices, share, _ = out_ref.shape
+def total(slots_ref, out_hbm, sum_ref, left):
+    devices, share, _ = out_hbm.shape
     summed = slots_ref[0, 0:share, :].astype(F32)
     for device in range(1, devices):
         summed = summed + slots_ref[device, 0:share, :].astype(F32)
-    summed = (summed / devices).astype(BF16)
-    for device in range(devices):
-        out_ref[device] = summed
+    sum_ref[...] = (summed / devices).astype(BF16)
+    copies = [
+        pltpu.make_async_copy(sum_ref, out_hbm.at[i], left.at[i]) for i in range(devices)
+    ]
+    for copy in copies:
+        copy.start()
+    for copy in copies:
+        copy.wait()
 
 
 def backward(
@@ -796,7 +823,7 @@
     held = [
         held_out(18, 288, 256),
         held_out(4096, 128),
-        held_out(4096, 128),
+        held_out(4096, 128, dtype=F32),
         held_out(4096, 128, dtype=F32),
         held_out(3456, 128),
         held_out(1024, 256),
@@ -822,7 +849,6 @@
             memory(4096, 128, dtype=F32),
             memory(18, 288, 256),
             memory(4096, 128),
-            memory(4096, 128),
             memory(4096, 128, dtype=F32),
             memory(4096, 128, dtype=F32),
             copies(6),
@@ -832,15 +858,15 @@
         flops=5 << 30,
         mib=36,
     )(core, w_conv, w_down, cotangent[0], heights, turned, other_turned)
-    came, taps, inner, slope = lax.optimization_barrier((came, taps, inner, slope))
+    came, taps, inner = lax.optimization_barrier((came, taps, inner))
     came_other = over_chan(came)
-    taps, inner, slope = kernel_call(
+    taps, inner = kernel_call(
         fetch,
-        [out(3456, 128), out(4096, 128, dtype=F32), out(4096, 128)],
-        [hbm()] * 3,
-        [vmem()] * 3,
-        [copies(3)],
-    )(taps, inner, slope)
+        [out(3456, 128), out(4096, 128, dtype=F32)],
+        [hbm()] * 2,
+        [vmem()] * 2,
+        [copies(2)],
+    )(taps, inner)
 
     share = -(-2752 // (devices * 16)) * 16
     terms, faces, coarse, grad_pre = kernel_call(
@@ -851,22 +877,22 @@
             held_out(512, 128),
             held_out(4096, 128),
         ],
-        [smem()] * 3 + [vmem()] * 5 + [hbm()] * 3,
+        [smem()] * 3 + [vmem()] * 4 + [hbm()] * 4,
         [hbm(), vmem(), hbm(), hbm()],
         [
             memory(2, 288, 384),
             memory(2, 256, 384),
             memory(4096, 128, dtype=F32),
             memory(4096, 128, dtype=F32),
-            memory(2048, 128, dtype=F32),
             memory(128, 5120),
+            memory(4096, 128, dtype=F32),
             memory(18, 288, 256),
             memory(1024, 256),
             memory(512, 256),
             memory(512, 128),
             memory(4096, 128),
             memory(devices, share + 16, 128),
-            copies(3),
+            copies(4),
             copies(2),
             copies(4),
         ],
@@ -882,7 +908,13 @@
     came_faces = jnp.stack(came_faces)
     other_faces = over_chan(came_faces)
     sums = to_all(
-        kernel_call(total, out(devices, share, 128), [vmem()], vmem())(arrived)
+        kernel_call(
+            total,
+            held_out(devices, share, 128),
+            [vmem()],
+            hbm(),
+            [memory(share, 128), copies(devices)],
+        )(arrived)
     )
     arrived_other = over_chan(arrived[:, share:])
     grad_features = kernel_call(

time: 91.2 us -> 90.8 us (level)
  no operation moved by 1% of the time
where the time goes in v2:
time: 90.8 us; the launch traced here: 90.4 us
  Pallas kernels  35.7 us (39%)
  starting transfers between devices  35.2 us (39%)
  waiting for transfers between devices  18.7 us (21%)
    pallas_call x7, Pallas kernels, run(): return call(*placed)  35.7 us
    all_to_all x3, starting transfers between devices, to_all(): return lax.all_to_all(slots, 'space', 0, 0, tiled=True)  20.1 us
    ppermute x4, starting transfers between devices, over_space(): return lax.ppermute(block, ('space', 'chan'), route)  13.9 us
    all_to_all x3, waiting for transfers between devices, to_all(): return lax.all_to_all(slots, 'space', 0, 0, tiled=True)  13.8 us
    ppermute x4, waiting for transfers between devices, over_space(): return lax.ppermute(block, ('space', 'chan'), route)  3.8 us
  transfers between devices with their start and end apart: 11, of which 7 were waited for; matrix products, arithmetic and copies ran while one was open for 0% of the time, Pallas kernels for 28%

profile of v2, /device:TPU:0, one launch (start us, length us, event | category | flops | bytes accessed | tf_op | source)
XLA Modules:
  0.0 90.4 jit_solution(18132489348329635065)
XLA Ops:
  0.6 0.5 collective-permute-start
  1.1 2.6 %shard_map.93 = bf16[16,128,128]{2,1,0:T(8,128)(2,1)} custom-call(s32[1,26]{1,0:T(1,128)} %near_ref.3, s32[8,64]{1,0:T(8,128)} %heights_hbm.3, bf16[8,64,512]{2,1,0:T(8,128)(2,1)} %bitcast.21), custom_call_target="tpu_custom_call" | custom-call | bytes 4194304 | tf_op jit(solution)/shard_map/pallas_call | solution.py:50
  3.8 7.9 %all-to-all-start = ((bf16[16,128,128]{2,1,0:T(8,128)(2,1)}), bf16[16,128,128]{2,1,0:T(8,128)(2,1)S(1)}, u32[]{:S(2)}, u32[]{:S(2)}) async-start(bf16[16,128,128]{2,1,0:T(8,128)(2,1)} %shard_map.93), calls=%async_computation | async-start | bytes 1048576 | tf_op jit(solution)/shard_map/all_to_all | solution.py:785
  11.7 0.0 collective-permute-done.other_hbm
  11.7 11.5 %shard_map.94 = (bf16[18,288,256]{2,1,0:T(8,128)(2,1)}, bf16[4096,128]{1,0:T(8,128)(2,1)}, f32[4096,128]{1,0:T(8,128)}, f32[4096,128]{1,0:T(8,128)}, bf16[3456,1...) custom-call(s32[1]{0:T(128)} %bitcast.core_ref, bf16[27,128,128]{2,1,0:T(8,128)(2,1)} %conv_hbm.3, ...), custom_call_target="tpu_custom_call" | custom-call | flops 5368709120 | bytes 4194304 | tf_op jit(solution)/shard_map/pallas_call | solution.py:50
  23.2 0.0 copy-start
  23.2 3.9 %all-to-all-done.own_ref = bf16[16,128,128]{2,1,0:T(8,128)(2,1)S(1)} async-done(((bf16[16,128,128]{2,1,0:T(8,128)(2,1)}), bf16[16,128,128]{2,1,0:T(8,128)(2,1)S(1)}, u32[]{:S(2)}, u32[]{:S(2)}) %all-to-all-start) | async-done | bytes 524320 | tf_op jit(solution)/shard_map/all_to_all | solution.py:785
  27.1 0.0 collective-permute-start.1
  27.1 1.9 %shard_map.95 = (bf16[3456,128]{1,0:T(8,128)(2,1)S(1)}, f32[4096,128]{1,0:T(8,128)S(1)}) custom-call(bf16[3456,128]{1,0:T(8,128)(2,1)} %get-tuple-element.30.taps_hbm, f32[4096,128]{1,0:T(8,128)} %get-tuple-element.31.inner_hbm), custom_call_target="tpu_custom_call" | custom-call | bytes 4194304 | tf_op jit(solution)/shard_map/pallas_call | solution.py:50
  29.0 0.0 collective-permute-done.1.other_ref
  29.1 0.0 copy-done
  29.1 8.3 %shard_map.96 = (bf16[16,192,128]{2,1,0:T(8,128)(2,1)}, bf16[4,256,128]{2,1,0:T(8,128)(2,1)S(1)}, bf16[512,128]{1,0:T(8,128)(2,1)}, bf16[4096,128]{1,0:T(8,128)(2,1)}) custom-call(s32[1,26]{1,0:T(1,128)S(1)} %copy-done, s32[1]{0:T(128)} %bitcast.core_ref, s32[1]{0:T(128)} %bitcast.1.at_ref, bf16[16,128,128]{2,1,0:T(8,128)(2,1)S(1)} %all-to-all-done.own_ref, ...), custom_call_target="tpu_custom_call" | custom-call | flops 5368709120 | bytes 4194304 | tf_op jit(solution)/shard_map/pallas_call | solution.py:50
  37.3 4.8 %all-to-all-start.1 = ((bf16[16,192,128]{2,1,0:T(8,128)(2,1)}), bf16[16,192,128]{2,1,0:T(8,128)(2,1)S(1)}, u32[]{:S(2)}, u32[]{:S(2)}) async-start(bf16[16,192,128]{2,1,0:T(8,128)(2,1)} %get-tuple-element.39), calls=%async_computation.1 | async-start | bytes 1572864 | tf_op jit(solution)/shard_map/all_to_all | solution.py:785
  42.2 3.8 %collective-permute-start.5 = (bf16[256,128]{1,0:T(8,128)(2,1)S(1)}, bf16[256,128]{1,0:T(8,128)(2,1)S(1)}, u32[]{:S(2)}, u32[]{:S(2)}) collective-permute-start(bf16[256,128]{1,0:T(8,128)(2,1)S(1)} %get-tuple-element.50), channel_id=1, source_target_pairs={{0,8},{2,10},{4,12},{6,14},{8,16},{10,18},{12,20},{14,22},{16,24},... | collective-permute-start | bytes 196616 | tf_op jit(solution)/shard_map/ppermute | solution.py:777
  46.0 4.3 %collective-permute-start.4 = (bf16[256,128]{1,0:T(8,128)(2,1)S(1)}, bf16[256,128]{1,0:T(8,128)(2,1)S(1)}, u32[]{:S(2)}, u32[]{:S(2)}) collective-permute-start(bf16[256,128]{1,0:T(8,128)(2,1)S(1)} %get-tuple-element.51), channel_id=1, source_target_pairs={{0,6},{2,8},{4,10},{6,12},{8,14},{10,16},{12,18},{14,20},{16,22},{... | collective-permute-start | bytes 196616 | tf_op jit(solution)/shard_map/ppermute | solution.py:777
  50.3 3.4 %collective-permute-start.3 = (bf16[256,128]{1,0:T(8,128)(2,1)S(1)}, bf16[256,128]{1,0:T(8,128)(2,1)S(1)}, u32[]{:S(2)}, u32[]{:S(2)}) collective-permute-start(bf16[256,128]{1,0:T(8,128)(2,1)S(1)} %get-tuple-element.52), channel_id=1, source_target_pairs={{0,4},{2,6},{4,8},{6,10},{8,12},{10,14},{12,16},{14,18},{16,20},{1... | collective-permute-start | bytes 196616 | tf_op jit(solution)/shard_map/ppermute | solution.py:777
  53.7 2.5 %collective-permute-start.2 = (bf16[256,128]{1,0:T(8,128)(2,1)S(1)}, bf16[256,128]{1,0:T(8,128)(2,1)S(1)}, u32[]{:S(2)}, u32[]{:S(2)}) collective-permute-start(bf16[256,128]{1,0:T(8,128)(2,1)S(1)} %get-tuple-element.53), channel_id=1, source_target_pairs={{0,2},{2,4},{4,6},{6,8},{8,10},{10,12},{12,14},{14,16},{16,18},{18... | collective-permute-start | bytes 196616 | tf_op jit(solution)/shard_map/ppermute | solution.py:777
  56.1 0.2 collective-permute-done.5
  56.4 0.0 collective-permute-done.4
  56.4 1.4 %collective-permute-done.3 = bf16[256,128]{1,0:T(8,128)(2,1)S(1)} collective-permute-done((bf16[256,128]{1,0:T(8,128)(2,1)S(1)}, bf16[256,128]{1,0:T(8,128)(2,1)S(1)}, u32[]{:S(2)}, u32[]{:S(2)}) %collective-permute-start.3) | collective-permute-done | bytes 65568 | tf_op jit(solution)/shard_map/ppermute | solution.py:777
  57.8 2.1 %collective-permute-done.2 = bf16[256,128]{1,0:T(8,128)(2,1)S(1)} collective-permute-done((bf16[256,128]{1,0:T(8,128)(2,1)S(1)}, bf16[256,128]{1,0:T(8,128)(2,1)S(1)}, u32[]{:S(2)}, u32[]{:S(2)}) %collective-permute-start.2) | collective-permute-done | bytes 65568 | tf_op jit(solution)/shard_map/ppermute | solution.py:777
  59.9 2.3 %all-to-all-done.1.slots_ref.own_ref = bf16[16,192,128]{2,1,0:T(8,128)(2,1)S(1)} async-done(((bf16[16,192,128]{2,1,0:T(8,128)(2,1)}), bf16[16,192,128]{2,1,0:T(8,128)(2,1)S(1)}, u32[]{:S(2)}, u32[]{:S(2)}) %all-to-all-start.1) | async-done | bytes 786464 | tf_op jit(solution)/shard_map/all_to_all | solution.py:785
  62.2 1.1 %shard_map.97 = bf16[16,176,128]{2,1,0:T(8,128)(2,1)} custom-call(bf16[16,192,128]{2,1,0:T(8,128)(2,1)S(1)} %all-to-all-done.1.slots_ref.own_ref), custom_call_target="tpu_custom_call" | custom-call | bytes 4194304 | tf_op jit(solution)/shard_map/pallas_call | solution.py:50
  63.3 7.4 %all-to-all-start.2 = ((bf16[16,176,128]{2,1,0:T(8,128)(2,1)}), bf16[16,176,128]{2,1,0:T(8,128)(2,1)S(1)}, u32[]{:S(2)}, u32[]{:S(2)}) async-start(bf16[16,176,128]{2,1,0:T(8,128)(2,1)} %shard_map.97), calls=%async_computation.2 | async-start | bytes 1441792 | tf_op jit(solution)/shard_map/all_to_all | solution.py:785
  70.7 0.1 collective-permute-start.7
  70.8 0.6 collective-permute-start.6
  71.4 1.0 %collective-permute-done.6.other_ref = bf16[16,16,128]{2,1,0:T(8,128)(2,1)S(1)} collective-permute-done((bf16[16,16,128]{2,1,0:T(8,128)(2,1)S(1)}, bf16[16,16,128]{2,1,0:T(8,128)(2,1)S(1)}, u32[]{:S(2)}, u32[]{:S(2)}) %collective-permute-start.6) | collective-permute-done | bytes 65568 | tf_op jit(solution)/shard_map/ppermute | solution.py:781
  72.4 0.0 collective-permute-done.7.other_faces_ref
  72.4 9.1 %shard_map.99 = bf16[8,64,512]{2,1,0:T(8,128)(2,1)} custom-call(s32[1,26]{1,0:T(1,128)S(1)} %copy-done, s32[1]{0:T(128)} %bitcast.core_ref, s32[1]{0:T(128)} %bitcast.1.at_ref, bf16[16,192,128]{2,1,0:T(8,128)(2,1)S(1)} %all-to-all-done.1.slots_ref.own_ref, bf16[16,16,128]{2,1,0:T(8,128)(2,1)S(1)} %collective-permute-done.6.other_ref, ...), custom_call_target="tpu_custom_call" | custom-call | flops 5368709120 | bytes 4194304 | tf_op jit(solution)/shard_map/pallas_call | solution.py:50
  81.5 7.7 %all-to-all-done.2 = bf16[16,176,128]{2,1,0:T(8,128)(2,1)S(1)} async-done(((bf16[16,176,128]{2,1,0:T(8,128)(2,1)}), bf16[16,176,128]{2,1,0:T(8,128)(2,1)S(1)}, u32[]{:S(2)}, u32[]{:S(2)}) %all-to-all-start.2) | async-done | bytes 720928 | tf_op jit(solution)/shard_map/all_to_all | solution.py:785
  89.2 1.2 %shard_map.98 = (f32[27,64,128]{2,1,0:T(8,128)}, f32[8,128,128]{2,1,0:T(8,128)}) custom-call(s32[1]{0:T(128)} %bitcast.core_ref, bf16[2816,128]{1,0:T(8,128)(2,1)S(1)} %bitcast.19), custom_call_target="tpu_custom_call" | custom-call | bytes 4194304 | tf_op jit(solution)/shard_map/pallas_call | solution.py:50
  (3 shorter events, 0.1 us)
Async XLA Ops:
  0.6 11.1 %collective-permute-start = (bf16[8,64,512]{2,1,0:T(8,128)(2,1)}, bf16[8,64,512]{2,1,0:T(8,128)(2,1)S(1)}, u32[]{:S(2)}, u32[]{:S(2)}) collective-permute-start(bf16[8,64,512]{2,1,0:T(8,128)(2,1)} %bitcast.20), channel_id=1, source_target_pairs={{0,1},{1,0},{2,3},{3,2},{4,5},{5,4},{6,7},{7,6},{8,9},{9,8},{10,11... | collective-permute-start | bytes 1572872 | tf_op jit(solution)/shard_map/ppermute | solution.py:781
  3.8 23.4 %all-to-all-start = ((bf16[16,128,128]{2,1,0:T(8,128)(2,1)}), bf16[16,128,128]{2,1,0:T(8,128)(2,1)S(1)}, u32[]{:S(2)}, u32[]{:S(2)}) async-start(bf16[16,128,128]{2,1,0:T(8,128)(2,1)} %shard_map.93), calls=%async_computation | async-start | bytes 1048576 | tf_op jit(solution)/shard_map/all_to_all | solution.py:785
  23.2 5.9 %copy-start = (s32[1,26]{1,0:T(1,128)S(1)}, s32[1,26]{1,0:T(1,128)}, u32[]{:S(2)}) copy-start(s32[1,26]{1,0:T(1,128)} %near_ref.3) | copy-start | bytes 316
  27.1 1.9 %collective-permute-start.1 = (bf16[16,128,128]{2,1,0:T(8,128)(2,1)S(1)}, bf16[16,128,128]{2,1,0:T(8,128)(2,1)S(1)}, u32[]{:S(2)}, u32[]{:S(2)}) collective-permute-start(bf16[16,128,128]{2,1,0:T(8,128)(2,1)S(1)} %all-to-all-done.own_ref), channel_id=1, source_target_pairs={{0,1},{1,0},{2,3},{3,2},{4,5},{5,4},{6,7},{7,6},{8,9},{9,8},{10,11... | collective-permute-start | bytes 1572872 | tf_op jit(solution)/shard_map/ppermute | solution.py:781
  37.3 24.9 %all-to-all-start.1 = ((bf16[16,192,128]{2,1,0:T(8,128)(2,1)}), bf16[16,192,128]{2,1,0:T(8,128)(2,1)S(1)}, u32[]{:S(2)}, u32[]{:S(2)}) async-start(bf16[16,192,128]{2,1,0:T(8,128)(2,1)} %get-tuple-element.39), calls=%async_computation.1 | async-start | bytes 1572864 | tf_op jit(solution)/shard_map/all_to_all | solution.py:785
  42.2 14.2 %collective-permute-start.5 = (bf16[256,128]{1,0:T(8,128)(2,1)S(1)}, bf16[256,128]{1,0:T(8,128)(2,1)S(1)}, u32[]{:S(2)}, u32[]{:S(2)}) collective-permute-start(bf16[256,128]{1,0:T(8,128)(2,1)S(1)} %get-tuple-element.50), channel_id=1, source_target_pairs={{0,8},{2,10},{4,12},{6,14},{8,16},{10,18},{12,20},{14,22},{16,24},... | collective-permute-start | bytes 196616 | tf_op jit(solution)/shard_map/ppermute | solution.py:777
  46.0 10.4 %collective-permute-start.4 = (bf16[256,128]{1,0:T(8,128)(2,1)S(1)}, bf16[256,128]{1,0:T(8,128)(2,1)S(1)}, u32[]{:S(2)}, u32[]{:S(2)}) collective-permute-start(bf16[256,128]{1,0:T(8,128)(2,1)S(1)} %get-tuple-element.51), channel_id=1, source_target_pairs={{0,6},{2,8},{4,10},{6,12},{8,14},{10,16},{12,18},{14,20},{16,22},{... | collective-permute-start | bytes 196616 | tf_op jit(solution)/shard_map/ppermute | solution.py:777
  50.3 7.5 %collective-permute-start.3 = (bf16[256,128]{1,0:T(8,128)(2,1)S(1)}, bf16[256,128]{1,0:T(8,128)(2,1)S(1)}, u32[]{:S(2)}, u32[]{:S(2)}) collective-permute-start(bf16[256,128]{1,0:T(8,128)(2,1)S(1)} %get-tuple-element.52), channel_id=1, source_target_pairs={{0,4},{2,6},{4,8},{6,10},{8,12},{10,14},{12,16},{14,18},{16,20},{1... | collective-permute-start | bytes 196616 | tf_op jit(solution)/shard_map/ppermute | solution.py:777
  53.7 6.3 %collective-permute-start.2 = (bf16[256,128]{1,0:T(8,128)(2,1)S(1)}, bf16[256,128]{1,0:T(8,128)(2,1)S(1)}, u32[]{:S(2)}, u32[]{:S(2)}) collective-permute-start(bf16[256,128]{1,0:T(8,128)(2,1)S(1)} %get-tuple-element.53), channel_id=1, source_target_pairs={{0,2},{2,4},{4,6},{6,8},{8,10},{10,12},{12,14},{14,16},{16,18},{18... | collective-permute-start | bytes 196616 | tf_op jit(solution)/shard_map/ppermute | solution.py:777
  63.3 25.9 %all-to-all-start.2 = ((bf16[16,176,128]{2,1,0:T(8,128)(2,1)}), bf16[16,176,128]{2,1,0:T(8,128)(2,1)S(1)}, u32[]{:S(2)}, u32[]{:S(2)}) async-start(bf16[16,176,128]{2,1,0:T(8,128)(2,1)} %shard_map.97), calls=%async_computation.2 | async-start | bytes 1441792 | tf_op jit(solution)/shard_map/all_to_all | solution.py:785
  70.7 1.7 %collective-permute-start.7 = (bf16[4,256,128]{2,1,0:T(8,128)(2,1)S(1)}, bf16[4,256,128]{2,1,0:T(8,128)(2,1)S(1)}, u32[]{:S(2)}, u32[]{:S(2)}) collective-permute-start(bf16[4,256,128]{2,1,0:T(8,128)(2,1)S(1)} %pad_maximum_fusion.own_faces_ref), channel_id=1, source_target_pairs={{0,1},{1,0},{2,3},{3,2},{4,5},{5,4},{6,7},{7,6},{8,9},{9,8},{10,11... | collective-permute-start | bytes 786440 | tf_op jit(solution)/shard_map/ppermute | solution.py:781
  70.8 1.6 %collective-permute-start.6 = (bf16[16,16,128]{2,1,0:T(8,128)(2,1)S(1)}, bf16[16,16,128]{2,1,0:T(8,128)(2,1)S(1)}, u32[]{:S(2)}, u32[]{:S(2)}) collective-permute-start(bf16[16,16,128]{2,1,0:T(8,128)(2,1)S(1)} %slice.19), channel_id=1, source_target_pairs={{0,1},{1,0},{2,3},{3,2},{4,5},{5,4},{6,7},{7,6},{8,9},{9,8},{10,11... | collective-permute-start | bytes 196616 | tf_op jit(solution)/shard_map/ppermute | solution.py:781

commit v3 on v2

--- a/solution.py
+++ b/solution.py
@@ -1,3 +1,5 @@
+import functools
+
 import jax
 import jax.numpy as jnp
 from jax import lax
@@ -300,15 +302,15 @@
     for copy in copies + bricks:
         copy.start()
     copies[1].wait()
-    filled = filled_voxels(heights_ref)
+    filled = filled_voxels(heights_ref).astype(BF16)
     for oz in range(2):
         for oy in range(2):
             pair = []
             for ox in range(2):
                 brick = ox + 2 * oy + 4 * oz
                 bricks[brick].wait()
-                pair.append(features_ref[brick].astype(F32) * filled[brick : brick + 1])
-            turned = jnp.concatenate(pair).T
+                pair.append(features_ref[brick] * filled[brick : brick + 1])
+            turned = jnp.concatenate(pair).T.astype(F32)
             for vx in range(8):
                 for vy in range(8):
                     at = vx * 256 + (8 * oy + vy) * 16 + 8 * oz
@@ -365,7 +367,7 @@
     core_ref, conv_hbm, down_hbm, cot_hbm, heights_hbm, own_hbm, other_hbm,
     lanes_hbm, active_hbm, slope_hbm, inner_hbm, taps_hbm, down_out_hbm, cot_out_hbm,
     conv_in_ref, down_in_ref, cot_in_ref, heights_ref, own_ref, other_ref,
-    two_ref, down_ref, cot_ref, padded_ref, rows_ref, mask_ref, lanes_ref, active_ref,
+    two_ref, down_ref, cot_ref, own_cot_ref, padded_ref, rows_ref, mask_ref, lanes_ref, active_ref,
     slope_ref, inner_ref, arrived, left, left_inner
 ):
     came = start_all(
@@ -385,7 +387,7 @@
             [
                 (two_ref.at[0:3456, 0:128], taps_hbm),
                 (down_ref, down_out_hbm),
-                (cot_ref, cot_out_hbm),
+                (own_cot_ref, cot_out_hbm),
                 (lanes_ref, lanes_hbm),
                 (active_ref, active_hbm),
                 (slope_ref, slope_hbm),
@@ -397,6 +399,7 @@
     forward_weights(
         core_ref[0] * 64, conv_in_ref, down_in_ref, cot_in_ref, two_ref, down_ref, cot_ref
     )
+    own_cot_ref[...] = cot_ref[:, 0:128].T
     for copy in gone[:3]:
         copy.start()
     for copy in came[3:]:
@@ -477,33 +480,32 @@
     return jnp.concatenate([taps_ref[at : at + 128, :] for at in starts])
 
 
-def margin_planes(planes_ref, taps_ref):
-    sums = []
-    for side, ex in ((0, 0), (1, 2)):
-        lhs = jnp.concatenate(
-            [planes_ref[side, ey * 16 : ey * 16 + 256, :] for ey in range(3)], axis=1
-        )
-        rhs = taps_ref[ex * 1152 : ex * 1152 + 1152, :]
-        sums.append(jnp.dot(lhs, rhs, preferred_element_type=F32))
-    return sums
-
-
-def margin_lines(lines_ref, taps_ref):
-    sums = []
+def any_block(near_ref, axis, step):
+    found = [near_ref[0, k] >= 0 for k, offset in enumerate(DIRECTIONS) if offset[axis] == step]
+    return functools.reduce(jnp.logical_or, found)
+
+
+def margin_plane(planes_ref, taps_ref, side):
+    lhs = jnp.concatenate(
+        [planes_ref[side, ey * 16 : ey * 16 + 256, :] for ey in range(3)], axis=1
+    )
+    rhs = taps_ref[side * 2304 : side * 2304 + 1152, :]
+    return jnp.dot(lhs, rhs, preferred_element_type=F32)
+
+
+def margin_lines(lines_ref, taps_ref, side):
     none = jnp.zeros((16, 384), BF16)
-    for side, ey in ((0, 0), (1, 2)):
-        lines = lines_ref[side]
-        lhs = jnp.concatenate(
-            [
-                jnp.concatenate([none, lines[:240]]),
-                lines,
-                jnp.concatenate([lines[16:], none]),
-            ],
-            axis=1,
-        )
-        rhs = tap_rows(taps_ref, [(ex, ey, ez) for ex in range(3) for ez in range(3)])
-        sums.append(jnp.dot(lhs, rhs, preferred_element_type=F32))
-    return sums
+    lines = lines_ref[side]
+    lhs = jnp.concatenate(
+        [
+            jnp.concatenate([none, lines[:240]]),
+            lines,
+            jnp.concatenate([lines[16:], none]),
+        ],
+        axis=1,
+    )
+    rhs = tap_rows(taps_ref, [(ex, 2 * side, ez) for ex in range(3) for ez in range(3)])
+    return jnp.dot(lhs, rhs, preferred_element_type=F32)
 
 
 def margin_ends(face, ez, taps_ref):
@@ -541,13 +543,20 @@
 
 
 def add_margin(planes_ref, lines_ref, near_ref, own_ref, other_ref, taps_ref, pre_ref):
-    for side, added in enumerate(margin_planes(planes_ref, taps_ref)):
-        at = side * 15 * 256
-        pre_ref[at : at + 256, :] += added
-    for side, added in enumerate(margin_lines(lines_ref, taps_ref)):
-        for x in range(16):
-            at = x * 256 + side * 240
-            pre_ref[at : at + 16, :] += added[x * 16 : x * 16 + 16]
+    for side in range(2):
+
+        @pl.when(any_block(near_ref, 0, 2 * side - 1))
+        def _(side=side):
+            at = side * 15 * 256
+            pre_ref[at : at + 256, :] += margin_plane(planes_ref, taps_ref, side)
+
+        @pl.when(any_block(near_ref, 1, 2 * side - 1))
+        def _(side=side):
+            added = margin_lines(lines_ref, taps_ref, side)
+            for x in range(16):
+                at = x * 256 + side * 240
+                pre_ref[at : at + 16, :] += added[x * 16 : x * 16 + 16]
+
     for k, ez in Z_FACES:
         block = near_ref[0, k]
 
@@ -584,28 +593,27 @@
 
 
 def forward(
-    near_ref, core_ref, at_ref, own_ref, other_ref, taps_ref, inner_ref,
-    slope_hbm, lanes_hbm, down_hbm, cot_hbm,
+    near_ref, core_ref, at_ref, own_ref, other_ref, taps_ref, slope_ref,
+    inner_hbm, lanes_hbm, down_hbm, cot_hbm,
     slots_hbm, faces_ref, coarse_hbm, grad_pre_hbm,
-    planes_ref, lines_ref, pre_ref, grad_ref, turned_ref, slope_ref, lanes_ref,
+    planes_ref, lines_ref, pre_ref, grad_ref, turned_ref, lanes_ref,
     down_ref, cot_ref, coarse_ref, grad_pre_ref, slots_ref, arrived, left, left_slots
 ):
     came = start_all(
         [
-            (slope_hbm, slope_ref),
+            (inner_hbm, pre_ref),
             (lanes_hbm, lanes_ref),
             (down_hbm, down_ref),
             (cot_hbm, cot_ref),
         ],
         arrived,
     )
-    pre_ref[...] = inner_ref[...]
     planes_ref[...] = jnp.zeros(planes_ref.shape, BF16)
     lines_ref[...] = jnp.zeros(lines_ref.shape, BF16)
     margin = Margin(planes_ref, lines_ref)
     fill_margin(margin, near_ref, own_ref, other_ref, z_faces=False)
+    came[0].wait()
     add_margin(planes_ref, lines_ref, near_ref, own_ref, other_ref, taps_ref, pre_ref)
-    came[0].wait()
 
     turned_ref[:, 0:512] = jnp.zeros((128, 512), BF16)
     turned_ref[:, 4608:5120] = jnp.zeros((128, 512), BF16)
@@ -660,11 +668,9 @@
     coarse = jnp.dot(patches, down_ref[...], preferred_element_type=F32)
     coarse_ref[...] = coarse[:, :128].astype(BF16)
     gone[1].start()
-    own_cot = cot_ref[:, 0:128].astype(F32).T.astype(BF16)
-    grad_down = jnp.dot(own_cot, patches, preferred_element_type=F32)
+    grad_down = jnp.dot(cot_ref[...], patches, preferred_element_type=F32).astype(BF16)
     for tap in range(8):
-        part = grad_down[:, tap * 128 : tap * 128 + 128].T
-        put_terms(tap * 128, part.astype(BF16))
+        put_terms(tap * 128, grad_down[:, tap * 128 : tap * 128 + 128].T)
     leaving[0].start()
 
     came[1].wait()
@@ -676,31 +682,26 @@
         rhs = lanes_ref[:, ey * 16 : ey * 16 + 256, :].reshape(4608, 256)
         summed = jnp.dot(lhs, rhs, preferred_element_type=F32)
         for ex in range(3):
-            part = summed[ex * 128 : ex * 128 + 128].T
-            put_terms(1024 + (ey * 3 + ex) * 192, part[0:192].astype(BF16))
+            part = summed[ex * 128 : ex * 128 + 128].astype(BF16).T
+            put_terms(1024 + (ey * 3 + ex) * 192, part[0:192])
         leaving[ey + 1].start()
     for copy in gone + leaving:
         copy.wait()
 
 
-def fetch(taps_hbm, inner_hbm, taps_ref, inner_ref, arrived):
-    for copy in start_all([(taps_hbm, taps_ref), (inner_hbm, inner_ref)], arrived):
+def fetch(taps_hbm, slope_hbm, taps_ref, slope_ref, arrived):
+    for copy in start_all([(taps_hbm, taps_ref), (slope_hbm, slope_ref)], arrived):
         copy.wait()
 
 
-def total(slots_ref, out_hbm, sum_ref, left):
-    devices, share, _ = out_hbm.shape
+def total(slots_ref, out_ref):
+    devices, share, _ = out_ref.shape
     summed = slots_ref[0, 0:share, :].astype(F32)
     for device in range(1, devices):
         summed = summed + slots_ref[device, 0:share, :].astype(F32)
-    sum_ref[...] = (summed / devices).astype(BF16)
-    copies = [
-        pltpu.make_async_copy(sum_ref, out_hbm.at[i], left.at[i]) for i in range(devices)
-    ]
-    for copy in copies:
-        copy.start()
-    for copy in copies:
-        copy.wait()
+    summed = (summed / devices).astype(BF16)
+    for device in range(devices):
+        out_ref[device] = summed
 
 
 def backward(
@@ -827,7 +828,7 @@
         held_out(4096, 128, dtype=F32),
         held_out(3456, 128),
         held_out(1024, 256),
-        held_out(512, 256),
+        held_out(128, 512),
     ]
     lanes, active, slope, inner, taps, down, cot = kernel_call(
         prepare,
@@ -844,6 +845,7 @@
             memory(4608, 256),
             memory(1024, 256),
             memory(512, 256),
+            memory(128, 512),
             memory(18, 288, 384),
             memory(4096, 128, dtype=F32),
             memory(4096, 128, dtype=F32),
@@ -858,15 +860,15 @@
         flops=5 << 30,
         mib=36,
     )(core, w_conv, w_down, cotangent[0], heights, turned, other_turned)
-    came, taps, inner = lax.optimization_barrier((came, taps, inner))
+    came, taps, slope, inner = lax.optimization_barrier((came, taps, slope, inner))
     came_other = over_chan(came)
-    taps, inner = kernel_call(
+    taps, slope = kernel_call(
         fetch,
         [out(3456, 128), out(4096, 128, dtype=F32)],
         [hbm()] * 2,
         [vmem()] * 2,
         [copies(2)],
-    )(taps, inner)
+    )(taps, slope)
 
     share = -(-2752 // (devices * 16)) * 16
     terms, faces, coarse, grad_pre = kernel_call(
@@ -885,10 +887,9 @@
             memory(4096, 128, dtype=F32),
             memory(4096, 128, dtype=F32),
             memory(128, 5120),
-            memory(4096, 128, dtype=F32),
             memory(18, 288, 256),
             memory(1024, 256),
-            memory(512, 256),
+            memory(128, 512),
             memory(512, 128),
             memory(4096, 128),
             memory(devices, share + 16, 128),
@@ -899,7 +900,7 @@
         flops=5 << 30,
         mib=24,
     )(
-        neighbours, *place, came, came_other, taps, inner, slope, lanes, down, cot
+        neighbours, *place, came, came_other, taps, slope, inner, lanes, down, cot
     )
 
     arrived = to_all(terms)
@@ -908,13 +909,7 @@
     came_faces = jnp.stack(came_faces)
     other_faces = over_chan(came_faces)
     sums = to_all(
-        kernel_call(
-            total,
-            held_out(devices, share, 128),
-            [vmem()],
-            hbm(),
-            [memory(share, 128), copies(devices)],
-        )(arrived)
+        kernel_call(total, out(devices, share, 128), [vmem()], vmem())(arrived)
     )
     arrived_other = over_chan(arrived[:, share:])
     grad_features = kernel_call(

time: 90.8 us -> 91.5 us (level)
  Pallas kernels: 35.7 us -> 37.2 us
    pallas_call x7, Pallas kernels: 35.7 us -> 37.2 us  [run(): return call(*placed)]
where the time goes in v3:
time: 91.5 us; the launch traced here: 90.9 us
  Pallas kernels  37.2 us (41%)
  starting transfers between devices  34.3 us (37%)
  waiting for transfers between devices  18.4 us (20%)
    pallas_call x7, Pallas kernels, run(): return call(*placed)  37.2 us
    all_to_all x3, starting transfers between devices, to_all(): return lax.all_to_all(slots, 'space', 0, 0, tiled=True)  19.2 us
    ppermute x4, starting transfers between devices, over_space(): return lax.ppermute(block, ('space', 'chan'), route)  13.9 us
    all_to_all x3, waiting for transfers between devices, to_all(): return lax.all_to_all(slots, 'space', 0, 0, tiled=True)  13.7 us
    ppermute x4, waiting for transfers between devices, over_space(): return lax.ppermute(block, ('space', 'chan'), route)  3.65 us
  transfers between devices with their start and end apart: 11, of which 7 were waited for; matrix products, arithmetic and copies ran while one was open for 0% of the time, Pallas kernels for 28%

profile of v3, /device:TPU:0, one launch (start us, length us, event | category | flops | bytes accessed | tf_op | source)
XLA Modules:
  0.0 90.9 jit_solution(10048629192156665884)
XLA Ops:
  0.6 0.5 collective-permute-start
  1.1 2.4 %shard_map.93 = bf16[16,128,128]{2,1,0:T(8,128)(2,1)} custom-call(s32[1,26]{1,0:T(1,128)} %near_ref.3, s32[8,64]{1,0:T(8,128)} %heights_hbm.3, bf16[8,64,512]{2,1,0:T(8,128)(2,1)} %bitcast.21), custom_call_target="tpu_custom_call" | custom-call | bytes 4194304 | tf_op jit(solution)/shard_map/pallas_call | solution.py:52
  3.6 7.9 %all-to-all-start = ((bf16[16,128,128]{2,1,0:T(8,128)(2,1)}), bf16[16,128,128]{2,1,0:T(8,128)(2,1)S(1)}, u32[]{:S(2)}, u32[]{:S(2)}) async-start(bf16[16,128,128]{2,1,0:T(8,128)(2,1)} %shard_map.93), calls=%async_computation | async-start | bytes 1048576 | tf_op jit(solution)/shard_map/all_to_all | solution.py:786
  11.5 0.0 collective-permute-done.other_hbm
  11.5 11.6 %shard_map.94 = (bf16[18,288,256]{2,1,0:T(8,128)(2,1)}, bf16[4096,128]{1,0:T(8,128)(2,1)}, f32[4096,128]{1,0:T(8,128)}, f32[4096,128]{1,0:T(8,128)}, bf16[3456,1...) custom-call(s32[1]{0:T(128)} %bitcast.core_ref, bf16[27,128,128]{2,1,0:T(8,128)(2,1)} %conv_hbm.3, ...), custom_call_target="tpu_custom_call" | custom-call | flops 5368709120 | bytes 4194304 | tf_op jit(solution)/shard_map/pallas_call | solution.py:52
  23.0 0.0 copy-start
  23.0 3.9 %all-to-all-done.own_ref = bf16[16,128,128]{2,1,0:T(8,128)(2,1)S(1)} async-done(((bf16[16,128,128]{2,1,0:T(8,128)(2,1)}), bf16[16,128,128]{2,1,0:T(8,128)(2,1)S(1)}, u32[]{:S(2)}, u32[]{:S(2)}) %all-to-all-start) | async-done | bytes 524320 | tf_op jit(solution)/shard_map/all_to_all | solution.py:786
  26.9 0.0 collective-permute-start.1
  26.9 1.9 %shard_map.95 = (bf16[3456,128]{1,0:T(8,128)(2,1)S(1)}, f32[4096,128]{1,0:T(8,128)S(1)}) custom-call(bf16[3456,128]{1,0:T(8,128)(2,1)} %get-tuple-element.32.taps_hbm, f32[4096,128]{1,0:T(8,128)} %get-tuple-element.33.slope_hbm), custom_call_target="tpu_custom_call" | custom-call | bytes 4194304 | tf_op jit(solution)/shard_map/pallas_call | solution.py:52
  28.8 0.0 collective-permute-done.1.other_ref
  28.8 0.0 copy-done
  28.8 9.8 %shard_map.96 = (bf16[16,192,128]{2,1,0:T(8,128)(2,1)}, bf16[4,256,128]{2,1,0:T(8,128)(2,1)S(1)}, bf16[512,128]{1,0:T(8,128)(2,1)}, bf16[4096,128]{1,0:T(8,128)(2,1)}) custom-call(s32[1,26]{1,0:T(1,128)S(1)} %copy-done, s32[1]{0:T(128)} %bitcast.core_ref, s32[1]{0:T(128)} %bitcast.1.at_ref, bf16[16,128,128]{2,1,0:T(8,128)(2,1)S(1)} %all-to-all-done.own_ref, ...), custom_call_target="tpu_custom_call" | custom-call | flops 5368709120 | bytes 4194304 | tf_op jit(solution)/shard_map/pallas_call | solution.py:52
  38.6 4.2 %all-to-all-start.1 = ((bf16[16,192,128]{2,1,0:T(8,128)(2,1)}), bf16[16,192,128]{2,1,0:T(8,128)(2,1)S(1)}, u32[]{:S(2)}, u32[]{:S(2)}) async-start(bf16[16,192,128]{2,1,0:T(8,128)(2,1)} %get-tuple-element.41), calls=%async_computation.1 | async-start | bytes 1572864 | tf_op jit(solution)/shard_map/all_to_all | solution.py:786
  42.8 3.8 %collective-permute-start.5 = (bf16[256,128]{1,0:T(8,128)(2,1)S(1)}, bf16[256,128]{1,0:T(8,128)(2,1)S(1)}, u32[]{:S(2)}, u32[]{:S(2)}) collective-permute-start(bf16[256,128]{1,0:T(8,128)(2,1)S(1)} %get-tuple-element.52), channel_id=1, source_target_pairs={{0,8},{2,10},{4,12},{6,14},{8,16},{10,18},{12,20},{14,22},{16,24},... | collective-permute-start | bytes 196616 | tf_op jit(solution)/shard_map/ppermute | solution.py:778
  46.7 4.3 %collective-permute-start.4 = (bf16[256,128]{1,0:T(8,128)(2,1)S(1)}, bf16[256,128]{1,0:T(8,128)(2,1)S(1)}, u32[]{:S(2)}, u32[]{:S(2)}) collective-permute-start(bf16[256,128]{1,0:T(8,128)(2,1)S(1)} %get-tuple-element.53), channel_id=1, source_target_pairs={{0,6},{2,8},{4,10},{6,12},{8,14},{10,16},{12,18},{14,20},{16,22},{... | collective-permute-start | bytes 196616 | tf_op jit(solution)/shard_map/ppermute | solution.py:778
  50.9 3.4 %collective-permute-start.3 = (bf16[256,128]{1,0:T(8,128)(2,1)S(1)}, bf16[256,128]{1,0:T(8,128)(2,1)S(1)}, u32[]{:S(2)}, u32[]{:S(2)}) collective-permute-start(bf16[256,128]{1,0:T(8,128)(2,1)S(1)} %get-tuple-element.54), channel_id=1, source_target_pairs={{0,4},{2,6},{4,8},{6,10},{8,12},{10,14},{12,16},{14,18},{16,20},{1... | collective-permute-start | bytes 196616 | tf_op jit(solution)/shard_map/ppermute | solution.py:778
  54.3 2.5 %collective-permute-start.2 = (bf16[256,128]{1,0:T(8,128)(2,1)S(1)}, bf16[256,128]{1,0:T(8,128)(2,1)S(1)}, u32[]{:S(2)}, u32[]{:S(2)}) collective-permute-start(bf16[256,128]{1,0:T(8,128)(2,1)S(1)} %get-tuple-element.55), channel_id=1, source_target_pairs={{0,2},{2,4},{4,6},{6,8},{8,10},{10,12},{12,14},{14,16},{16,18},{18... | collective-permute-start | bytes 196616 | tf_op jit(solution)/shard_map/ppermute | solution.py:778
  56.8 0.2 collective-permute-done.5
  56.9 0.0 collective-permute-done.4
  56.9 1.5 %collective-permute-done.3 = bf16[256,128]{1,0:T(8,128)(2,1)S(1)} collective-permute-done((bf16[256,128]{1,0:T(8,128)(2,1)S(1)}, bf16[256,128]{1,0:T(8,128)(2,1)S(1)}, u32[]{:S(2)}, u32[]{:S(2)}) %collective-permute-start.3) | collective-permute-done | bytes 65568 | tf_op jit(solution)/shard_map/ppermute | solution.py:778
  58.4 2.0 %collective-permute-done.2 = bf16[256,128]{1,0:T(8,128)(2,1)S(1)} collective-permute-done((bf16[256,128]{1,0:T(8,128)(2,1)S(1)}, bf16[256,128]{1,0:T(8,128)(2,1)S(1)}, u32[]{:S(2)}, u32[]{:S(2)}) %collective-permute-start.2) | collective-permute-done | bytes 65568 | tf_op jit(solution)/shard_map/ppermute | solution.py:778
  60.4 2.4 %all-to-all-done.1.slots_ref.own_ref = bf16[16,192,128]{2,1,0:T(8,128)(2,1)S(1)} async-done(((bf16[16,192,128]{2,1,0:T(8,128)(2,1)}), bf16[16,192,128]{2,1,0:T(8,128)(2,1)S(1)}, u32[]{:S(2)}, u32[]{:S(2)}) %all-to-all-start.1) | async-done | bytes 786464 | tf_op jit(solution)/shard_map/all_to_all | solution.py:786
  62.9 1.0 %shard_map.97 = bf16[16,176,128]{2,1,0:T(8,128)(2,1)} custom-call(bf16[16,192,128]{2,1,0:T(8,128)(2,1)S(1)} %all-to-all-done.1.slots_ref.own_ref), custom_call_target="tpu_custom_call" | custom-call | bytes 4194304 | tf_op jit(solution)/shard_map/pallas_call | solution.py:52
  63.8 7.2 %all-to-all-start.2 = ((bf16[16,176,128]{2,1,0:T(8,128)(2,1)}), bf16[16,176,128]{2,1,0:T(8,128)(2,1)S(1)}, u32[]{:S(2)}, u32[]{:S(2)}) async-start(bf16[16,176,128]{2,1,0:T(8,128)(2,1)} %shard_map.97), calls=%async_computation.2 | async-start | bytes 1441792 | tf_op jit(solution)/shard_map/all_to_all | solution.py:786
  71.0 0.1 collective-permute-start.7
  71.1 0.6 collective-permute-start.6
  71.7 1.0 %collective-permute-done.6.other_ref = bf16[16,16,128]{2,1,0:T(8,128)(2,1)S(1)} collective-permute-done((bf16[16,16,128]{2,1,0:T(8,128)(2,1)S(1)}, bf16[16,16,128]{2,1,0:T(8,128)(2,1)S(1)}, u32[]{:S(2)}, u32[]{:S(2)}) %collective-permute-start.6) | collective-permute-done | bytes 65568 | tf_op jit(solution)/shard_map/ppermute | solution.py:782
  72.7 0.0 collective-permute-done.7.other_faces_ref
  72.7 9.4 %shard_map.99 = bf16[8,64,512]{2,1,0:T(8,128)(2,1)} custom-call(s32[1,26]{1,0:T(1,128)S(1)} %copy-done, s32[1]{0:T(128)} %bitcast.core_ref, s32[1]{0:T(128)} %bitcast.1.at_ref, bf16[16,192,128]{2,1,0:T(8,128)(2,1)S(1)} %all-to-all-done.1.slots_ref.own_ref, bf16[16,16,128]{2,1,0:T(8,128)(2,1)S(1)} %collective-permute-done.6.other_ref, ...), custom_call_target="tpu_custom_call" | custom-call | flops 5368709120 | bytes 4194304 | tf_op jit(solution)/shard_map/pallas_call | solution.py:52
  82.2 7.5 %all-to-all-done.2 = bf16[16,176,128]{2,1,0:T(8,128)(2,1)S(1)} async-done(((bf16[16,176,128]{2,1,0:T(8,128)(2,1)}), bf16[16,176,128]{2,1,0:T(8,128)(2,1)S(1)}, u32[]{:S(2)}, u32[]{:S(2)}) %all-to-all-start.2) | async-done | bytes 720928 | tf_op jit(solution)/shard_map/all_to_all | solution.py:786
  89.6 1.2 %shard_map.98 = (f32[27,64,128]{2,1,0:T(8,128)}, f32[8,128,128]{2,1,0:T(8,128)}) custom-call(s32[1]{0:T(128)} %bitcast.core_ref, bf16[2816,128]{1,0:T(8,128)(2,1)S(1)} %bitcast.19), custom_call_target="tpu_custom_call" | custom-call | bytes 4194304 | tf_op jit(solution)/shard_map/pallas_call | solution.py:52
  (3 shorter events, 0.1 us)
Async XLA Ops:
  0.6 10.8 %collective-permute-start = (bf16[8,64,512]{2,1,0:T(8,128)(2,1)}, bf16[8,64,512]{2,1,0:T(8,128)(2,1)S(1)}, u32[]{:S(2)}, u32[]{:S(2)}) collective-permute-start(bf16[8,64,512]{2,1,0:T(8,128)(2,1)} %bitcast.20), channel_id=1, source_target_pairs={{0,1},{1,0},{2,3},{3,2},{4,5},{5,4},{6,7},{7,6},{8,9},{9,8},{10,11... | collective-permute-start | bytes 1572872 | tf_op jit(solution)/shard_map/ppermute | solution.py:782
  3.6 23.4 %all-to-all-start = ((bf16[16,128,128]{2,1,0:T(8,128)(2,1)}), bf16[16,128,128]{2,1,0:T(8,128)(2,1)S(1)}, u32[]{:S(2)}, u32[]{:S(2)}) async-start(bf16[16,128,128]{2,1,0:T(8,128)(2,1)} %shard_map.93), calls=%async_computation | async-start | bytes 1048576 | tf_op jit(solution)/shard_map/all_to_all | solution.py:786
  23.0 5.8 %copy-start = (s32[1,26]{1,0:T(1,128)S(1)}, s32[1,26]{1,0:T(1,128)}, u32[]{:S(2)}) copy-start(s32[1,26]{1,0:T(1,128)} %near_ref.3) | copy-start | bytes 316
  26.9 1.9 %collective-permute-start.1 = (bf16[16,128,128]{2,1,0:T(8,128)(2,1)S(1)}, bf16[16,128,128]{2,1,0:T(8,128)(2,1)S(1)}, u32[]{:S(2)}, u32[]{:S(2)}) collective-permute-start(bf16[16,128,128]{2,1,0:T(8,128)(2,1)S(1)} %all-to-all-done.own_ref), channel_id=1, source_target_pairs={{0,1},{1,0},{2,3},{3,2},{4,5},{5,4},{6,7},{7,6},{8,9},{9,8},{10,11... | collective-permute-start | bytes 1572872 | tf_op jit(solution)/shard_map/ppermute | solution.py:782
  38.6 24.2 %all-to-all-start.1 = ((bf16[16,192,128]{2,1,0:T(8,128)(2,1)}), bf16[16,192,128]{2,1,0:T(8,128)(2,1)S(1)}, u32[]{:S(2)}, u32[]{:S(2)}) async-start(bf16[16,192,128]{2,1,0:T(8,128)(2,1)} %get-tuple-element.41), calls=%async_computation.1 | async-start | bytes 1572864 | tf_op jit(solution)/shard_map/all_to_all | solution.py:786
  42.8 14.1 %collective-permute-start.5 = (bf16[256,128]{1,0:T(8,128)(2,1)S(1)}, bf16[256,128]{1,0:T(8,128)(2,1)S(1)}, u32[]{:S(2)}, u32[]{:S(2)}) collective-permute-start(bf16[256,128]{1,0:T(8,128)(2,1)S(1)} %get-tuple-element.52), channel_id=1, source_target_pairs={{0,8},{2,10},{4,12},{6,14},{8,16},{10,18},{12,20},{14,22},{16,24},... | collective-permute-start | bytes 196616 | tf_op jit(solution)/shard_map/ppermute | solution.py:778
  46.7 10.3 %collective-permute-start.4 = (bf16[256,128]{1,0:T(8,128)(2,1)S(1)}, bf16[256,128]{1,0:T(8,128)(2,1)S(1)}, u32[]{:S(2)}, u32[]{:S(2)}) collective-permute-start(bf16[256,128]{1,0:T(8,128)(2,1)S(1)} %get-tuple-element.53), channel_id=1, source_target_pairs={{0,6},{2,8},{4,10},{6,12},{8,14},{10,16},{12,18},{14,20},{16,22},{... | collective-permute-start | bytes 196616 | tf_op jit(solution)/shard_map/ppermute | solution.py:778
  50.9 7.5 %collective-permute-start.3 = (bf16[256,128]{1,0:T(8,128)(2,1)S(1)}, bf16[256,128]{1,0:T(8,128)(2,1)S(1)}, u32[]{:S(2)}, u32[]{:S(2)}) collective-permute-start(bf16[256,128]{1,0:T(8,128)(2,1)S(1)} %get-tuple-element.54), channel_id=1, source_target_pairs={{0,4},{2,6},{4,8},{6,10},{8,12},{10,14},{12,16},{14,18},{16,20},{1... | collective-permute-start | bytes 196616 | tf_op jit(solution)/shard_map/ppermute | solution.py:778
  54.3 6.1 %collective-permute-start.2 = (bf16[256,128]{1,0:T(8,128)(2,1)S(1)}, bf16[256,128]{1,0:T(8,128)(2,1)S(1)}, u32[]{:S(2)}, u32[]{:S(2)}) collective-permute-start(bf16[256,128]{1,0:T(8,128)(2,1)S(1)} %get-tuple-element.55), channel_id=1, source_target_pairs={{0,2},{2,4},{4,6},{6,8},{8,10},{10,12},{12,14},{14,16},{16,18},{18... | collective-permute-start | bytes 196616 | tf_op jit(solution)/shard_map/ppermute | solution.py:778
  63.8 25.8 %all-to-all-start.2 = ((bf16[16,176,128]{2,1,0:T(8,128)(2,1)}), bf16[16,176,128]{2,1,0:T(8,128)(2,1)S(1)}, u32[]{:S(2)}, u32[]{:S(2)}) async-start(bf16[16,176,128]{2,1,0:T(8,128)(2,1)} %shard_map.97), calls=%async_computation.2 | async-start | bytes 1441792 | tf_op jit(solution)/shard_map/all_to_all | solution.py:786
  71.0 1.7 %collective-permute-start.7 = (bf16[4,256,128]{2,1,0:T(8,128)(2,1)S(1)}, bf16[4,256,128]{2,1,0:T(8,128)(2,1)S(1)}, u32[]{:S(2)}, u32[]{:S(2)}) collective-permute-start(bf16[4,256,128]{2,1,0:T(8,128)(2,1)S(1)} %pad_maximum_fusion.own_faces_ref), channel_id=1, source_target_pairs={{0,1},{1,0},{2,3},{3,2},{4,5},{5,4},{6,7},{7,6},{8,9},{9,8},{10,11... | collective-permute-start | bytes 786440 | tf_op jit(solution)/shard_map/ppermute | solution.py:782
  71.1 1.6 %collective-permute-start.6 = (bf16[16,16,128]{2,1,0:T(8,128)(2,1)S(1)}, bf16[16,16,128]{2,1,0:T(8,128)(2,1)S(1)}, u32[]{:S(2)}, u32[]{:S(2)}) collective-permute-start(bf16[16,16,128]{2,1,0:T(8,128)(2,1)S(1)} %slice.19), channel_id=1, source_target_pairs={{0,1},{1,0},{2,3},{3,2},{4,5},{5,4},{6,7},{7,6},{8,9},{9,8},{10,11... | collective-permute-start | bytes 196616 | tf_op jit(solution)/shard_map/ppermute | solution.py:782

commit v4 on v2

--- a/solution.py
+++ b/solution.py
@@ -14,6 +14,7 @@
 DIRECTIONS = [offset for offset in OFFSETS if offset != (0, 0, 0)]
 FILL_ORDER = sorted(range(26), key=lambda k: (abs(DIRECTIONS[k][2]), k))
 INACTIVE = -1e30
+EDGE = 8
 F32 = jnp.float32
 BF16 = jnp.bfloat16
 
@@ -126,10 +127,7 @@
         @pl.when(block >= 0)
         def _(dx=dx, dy=dy, dz=dz, x=x, y=y, z=z, block=block):
             if dx == 0:
-                line = rows_ref[pl.ds(y * 16 + z, 16, stride=256), :]
-                low, high = line[:8], swap_halves(line[8:])
-                line = jnp.where(low_lanes(low), low, high)
-                rows = jnp.concatenate([line, line])
+                rows = rows_ref[pl.ds(y * 16 + z, 16, stride=256), :]
             elif dz == 0:
                 rows = rows_ref[x * 256 + y * 16 : x * 256 + y * 16 + 16, :]
             elif dy == 0:
@@ -137,9 +135,9 @@
             else:
                 at = x * 256 + y * 16 + z
                 rows = jnp.broadcast_to(rows_ref[at : at + 1, :], (16, 128))
-            if dx == 1:
-                rows = swap_halves(rows)
-            slots_ref[block, start : start + 16, :] = rows.astype(BF16)
+            low, high = rows[:EDGE], swap_halves(rows[EDGE:])
+            rows = jnp.where(low_lanes(low), low, high)
+            slots_ref[block, start : start + EDGE, :] = rows.astype(BF16)
 
 
 def fill_faces(rows_ref, near_ref, place, faces_ref):
@@ -271,12 +269,12 @@
 
         @pl.when(block >= 0)
         def _(offset=offset, block=block, face=face):
-            height = 128 if face else 16
+            height = 128 if face else 16 if start == 0 else EDGE
             own = own_ref[block, start : start + height, :].astype(F32)
             other = other_ref[block, 0:height, :].astype(F32)
             first = jnp.where(low_lanes(own), own, swap_halves(other))
             second = jnp.where(low_lanes(own), swap_halves(own), other)
-            if face:
+            if face or start:
                 rows = jnp.concatenate([first, second])
             elif offset[0] == 0:
                 rows = jnp.concatenate([first[:8], second[:8]])
@@ -300,15 +298,15 @@
     for copy in copies + bricks:
         copy.start()
     copies[1].wait()
-    filled = filled_voxels(heights_ref)
+    filled = filled_voxels(heights_ref).astype(BF16)
     for oz in range(2):
         for oy in range(2):
             pair = []
             for ox in range(2):
                 brick = ox + 2 * oy + 4 * oz
                 bricks[brick].wait()
-                pair.append(features_ref[brick].astype(F32) * filled[brick : brick + 1])
-            turned = jnp.concatenate(pair).T
+                pair.append(features_ref[brick] * filled[brick : brick + 1])
+            turned = jnp.concatenate(pair).T.astype(F32)
             for vx in range(8):
                 for vy in range(8):
                     at = vx * 256 + (8 * oy + vy) * 16 + 8 * oz
@@ -365,7 +363,7 @@
     core_ref, conv_hbm, down_hbm, cot_hbm, heights_hbm, own_hbm, other_hbm,
     lanes_hbm, active_hbm, slope_hbm, inner_hbm, taps_hbm, down_out_hbm, cot_out_hbm,
     conv_in_ref, down_in_ref, cot_in_ref, heights_ref, own_ref, other_ref,
-    two_ref, down_ref, cot_ref, padded_ref, rows_ref, mask_ref, lanes_ref, active_ref,
+    two_ref, down_ref, cot_ref, own_cot_ref, padded_ref, rows_ref, mask_ref, lanes_ref, active_ref,
     slope_ref, inner_ref, arrived, left, left_inner
 ):
     came = start_all(
@@ -385,7 +383,7 @@
             [
                 (two_ref.at[0:3456, 0:128], taps_hbm),
                 (down_ref, down_out_hbm),
-                (cot_ref, cot_out_hbm),
+                (own_cot_ref, cot_out_hbm),
                 (lanes_ref, lanes_hbm),
                 (active_ref, active_hbm),
                 (slope_ref, slope_hbm),
@@ -397,6 +395,7 @@
     forward_weights(
         core_ref[0] * 64, conv_in_ref, down_in_ref, cot_in_ref, two_ref, down_ref, cot_ref
     )
+    own_cot_ref[...] = cot_ref[:, 0:128].T
     for copy in gone[:3]:
         copy.start()
     for copy in came[3:]:
@@ -592,8 +591,8 @@
 ):
     came = start_all(
         [
+            (lanes_hbm, lanes_ref),
             (slope_hbm, slope_ref),
-            (lanes_hbm, lanes_ref),
             (down_hbm, down_ref),
             (cot_hbm, cot_ref),
         ],
@@ -606,6 +605,9 @@
     fill_margin(margin, near_ref, own_ref, other_ref, z_faces=False)
     add_margin(planes_ref, lines_ref, near_ref, own_ref, other_ref, taps_ref, pre_ref)
     came[0].wait()
+    put_own_margin(planes_ref, lines_ref, near_ref, own_ref, other_ref, lanes_ref)
+    for copy in came[1:]:
+        copy.wait()
 
     turned_ref[:, 0:512] = jnp.zeros((128, 512), BF16)
     turned_ref[:, 4608:5120] = jnp.zeros((128, 512), BF16)
@@ -625,10 +627,7 @@
         pltpu.make_async_copy(coarse_ref, coarse_hbm, left.at[1]),
     ]
     gone[0].start()
-    fill_faces(grad_ref, near_ref, (core_ref[0], at_ref[0]), faces_ref)
-    share = slots_ref.shape[1] - 16
-    fill_edges(grad_ref, near_ref, slots_ref, share)
-
+    share = slots_ref.shape[1] - EDGE
     def put_terms(at, rows):
         while rows.shape[0]:
             owner, row = at // share, at % share
@@ -637,16 +636,8 @@
             rows = rows[count:]
             at += count
 
-    ends = [1024 // share] + [(1024 + 576 * i) // share for i in (1, 2)] + [slots_ref.shape[0]]
-    leaving = [
-        pltpu.make_async_copy(
-            slots_ref.at[first:last], slots_hbm.at[first:last], left_slots.at[i]
-        )
-        for i, (first, last) in enumerate(zip([0] + ends, ends))
-    ]
-
-    came[2].wait()
-    came[3].wait()
+    leaving = [pltpu.make_async_copy(slots_ref, slots_hbm, left_slots.at[0])]
+
     patches = []
     for tap in range(8):
         tx, ty, tz = tap // 4, tap // 2 % 2, tap % 2
@@ -660,15 +651,9 @@
     coarse = jnp.dot(patches, down_ref[...], preferred_element_type=F32)
     coarse_ref[...] = coarse[:, :128].astype(BF16)
     gone[1].start()
-    own_cot = cot_ref[:, 0:128].astype(F32).T.astype(BF16)
-    grad_down = jnp.dot(own_cot, patches, preferred_element_type=F32)
+    grad_down = jnp.dot(cot_ref[...], patches, preferred_element_type=F32).astype(BF16)
     for tap in range(8):
-        part = grad_down[:, tap * 128 : tap * 128 + 128].T
-        put_terms(tap * 128, part.astype(BF16))
-    leaving[0].start()
-
-    came[1].wait()
-    put_own_margin(planes_ref, lines_ref, near_ref, own_ref, other_ref, lanes_ref)
+        put_terms(tap * 128, grad_down[:, tap * 128 : tap * 128 + 128].T)
     lhs = jnp.concatenate(
         [turned_ref[:, (2 - ex) * 256 : (2 - ex) * 256 + 4608] for ex in range(3)]
     )
@@ -676,9 +661,12 @@
         rhs = lanes_ref[:, ey * 16 : ey * 16 + 256, :].reshape(4608, 256)
         summed = jnp.dot(lhs, rhs, preferred_element_type=F32)
         for ex in range(3):
-            part = summed[ex * 128 : ex * 128 + 128].T
-            put_terms(1024 + (ey * 3 + ex) * 192, part[0:192].astype(BF16))
-        leaving[ey + 1].start()
+            part = summed[ex * 128 : ex * 128 + 128].astype(BF16).T
+            put_terms(1024 + (ey * 3 + ex) * 192, part[0:192])
+    fill_edges(grad_ref, near_ref, slots_ref, share)
+    for copy in leaving:
+        copy.start()
+    fill_faces(grad_ref, near_ref, (core_ref[0], at_ref[0]), faces_ref)
     for copy in gone + leaving:
         copy.wait()
 
@@ -688,19 +676,14 @@
         copy.wait()
 
 
-def total(slots_ref, out_hbm, sum_ref, left):
-    devices, share, _ = out_hbm.shape
+def total(slots_ref, out_ref):
+    devices, share, _ = out_ref.shape
     summed = slots_ref[0, 0:share, :].astype(F32)
     for device in range(1, devices):
         summed = summed + slots_ref[device, 0:share, :].astype(F32)
-    sum_ref[...] = (summed / devices).astype(BF16)
-    copies = [
-        pltpu.make_async_copy(sum_ref, out_hbm.at[i], left.at[i]) for i in range(devices)
-    ]
-    for copy in copies:
-        copy.start()
-    for copy in copies:
-        copy.wait()
+    summed = (summed / devices).astype(BF16)
+    for device in range(devices):
+        out_ref[device] = summed
 
 
 def backward(
@@ -719,7 +702,7 @@
         rows = grad_pre_ref[x * 256 : x * 256 + 256, :].astype(F32)
         put_lines(Whole(padded_ref), [(x + 1, 16, 256)], rows)
     fill_margin(
-        Whole(padded_ref), near_ref, own_ref, other_ref, own_ref.shape[1] - 16,
+        Whole(padded_ref), near_ref, own_ref, other_ref, own_ref.shape[1] - EDGE,
         ((core_ref[0], at_ref[0]), own_faces_ref, other_faces_ref),
     )
     came[2].wait()
@@ -827,7 +810,7 @@
         held_out(4096, 128, dtype=F32),
         held_out(3456, 128),
         held_out(1024, 256),
-        held_out(512, 256),
+        held_out(128, 512),
     ]
     lanes, active, slope, inner, taps, down, cot = kernel_call(
         prepare,
@@ -844,6 +827,7 @@
             memory(4608, 256),
             memory(1024, 256),
             memory(512, 256),
+            memory(128, 512),
             memory(18, 288, 384),
             memory(4096, 128, dtype=F32),
             memory(4096, 128, dtype=F32),
@@ -872,7 +856,7 @@
     terms, faces, coarse, grad_pre = kernel_call(
         forward,
         [
-            held_out(devices, share + 16, 128),
+            held_out(devices, share + EDGE, 128),
             out(4, 256, 128),
             held_out(512, 128),
             held_out(4096, 128),
@@ -888,13 +872,13 @@
             memory(4096, 128, dtype=F32),
             memory(18, 288, 256),
             memory(1024, 256),
-            memory(512, 256),
+            memory(128, 512),
             memory(512, 128),
             memory(4096, 128),
-            memory(devices, share + 16, 128),
+            memory(devices, share + EDGE, 128),
             copies(4),
             copies(2),
-            copies(4),
+            copies(1),
         ],
         flops=5 << 30,
         mib=24,
@@ -908,13 +892,7 @@
     came_faces = jnp.stack(came_faces)
     other_faces = over_chan(came_faces)
     sums = to_all(
-        kernel_call(
-            total,
-            held_out(devices, share, 128),
-            [vmem()],
-            hbm(),
-            [memory(share, 128), copies(devices)],
-        )(arrived)
+        kernel_call(total, out(devices, share, 128), [vmem()], vmem())(arrived)
     )
     arrived_other = over_chan(arrived[:, share:])
     grad_features = kernel_call(

time: 90.8 us -> 89.7 us (0.988)
  transfers between devices with their start and end apart: 11 -> 11, of which waited for: 7 -> 6; matrix products, arithmetic and copies ran while one was open for 0% -> 0% of each run, Pallas kernels for 28% -> 28%
where the time goes in v4:
time: 89.7 us; the launch traced here: 89.1 us
  Pallas kernels  35.7 us (40%)
  starting transfers between devices  34.3 us (38%)
  waiting for transfers between devices  18.3 us (20%)
    pallas_call x7, Pallas kernels, run(): return call(*placed)  35.7 us
    all_to_all x3, starting transfers between devices, to_all(): return lax.all_to_all(slots, 'space', 0, 0, tiled=True)  19.2 us
    all_to_all x3, waiting for transfers between devices, to_all(): return lax.all_to_all(slots, 'space', 0, 0, tiled=True)  14 us
    ppermute x4, starting transfers between devices, over_space(): return lax.ppermute(block, ('space', 'chan'), route)  13.9 us
    ppermute x4, waiting for transfers between devices, over_space(): return lax.ppermute(block, ('space', 'chan'), route)  3.2 us
  transfers between devices with their start and end apart: 11, of which 6 were waited for; matrix products, arithmetic and copies ran while one was open for 0% of the time, Pallas kernels for 28%

profile of v4, /device:TPU:0, one launch (start us, length us, event | category | flops | bytes accessed | tf_op | source)
XLA Modules:
  0.0 89.1 jit_solution(4478602766680041513)
XLA Ops:
  0.6 0.5 collective-permute-start
  1.1 2.4 %shard_map.93 = bf16[16,128,128]{2,1,0:T(8,128)(2,1)} custom-call(s32[1,26]{1,0:T(1,128)} %near_ref.3, s32[8,64]{1,0:T(8,128)} %heights_hbm.3, bf16[8,64,512]{2,1,0:T(8,128)(2,1)} %bitcast.21), custom_call_target="tpu_custom_call" | custom-call | bytes 4194304 | tf_op jit(solution)/shard_map/pallas_call | solution.py:51
  3.5 8.0 %all-to-all-start = ((bf16[16,128,128]{2,1,0:T(8,128)(2,1)}), bf16[16,128,128]{2,1,0:T(8,128)(2,1)S(1)}, u32[]{:S(2)}, u32[]{:S(2)}) async-start(bf16[16,128,128]{2,1,0:T(8,128)(2,1)} %shard_map.93), calls=%async_computation | async-start | bytes 1048576 | tf_op jit(solution)/shard_map/all_to_all | solution.py:768
  11.5 0.0 collective-permute-done.other_hbm
  11.5 11.5 %shard_map.94 = (bf16[18,288,256]{2,1,0:T(8,128)(2,1)}, bf16[4096,128]{1,0:T(8,128)(2,1)}, f32[4096,128]{1,0:T(8,128)}, f32[4096,128]{1,0:T(8,128)}, bf16[3456,1...) custom-call(s32[1]{0:T(128)} %bitcast.core_ref, bf16[27,128,128]{2,1,0:T(8,128)(2,1)} %conv_hbm.3, ...), custom_call_target="tpu_custom_call" | custom-call | flops 5368709120 | bytes 4194304 | tf_op jit(solution)/shard_map/pallas_call | solution.py:51
  23.1 0.0 copy-start
  23.1 3.9 %all-to-all-done.own_ref = bf16[16,128,128]{2,1,0:T(8,128)(2,1)S(1)} async-done(((bf16[16,128,128]{2,1,0:T(8,128)(2,1)}), bf16[16,128,128]{2,1,0:T(8,128)(2,1)S(1)}, u32[]{:S(2)}, u32[]{:S(2)}) %all-to-all-start) | async-done | bytes 524320 | tf_op jit(solution)/shard_map/all_to_all | solution.py:768
  26.9 0.0 collective-permute-start.1
  27.0 1.9 %shard_map.95 = (bf16[3456,128]{1,0:T(8,128)(2,1)S(1)}, f32[4096,128]{1,0:T(8,128)S(1)}) custom-call(bf16[3456,128]{1,0:T(8,128)(2,1)} %get-tuple-element.30.taps_hbm, f32[4096,128]{1,0:T(8,128)} %get-tuple-element.31.inner_hbm), custom_call_target="tpu_custom_call" | custom-call | bytes 4194304 | tf_op jit(solution)/shard_map/pallas_call | solution.py:51
  28.8 0.0 collective-permute-done.1.other_ref
  28.9 0.0 copy-done
  28.9 8.6 %shard_map.96 = (bf16[16,184,128]{2,1,0:T(8,128)(2,1)}, bf16[4,256,128]{2,1,0:T(8,128)(2,1)S(1)}, bf16[512,128]{1,0:T(8,128)(2,1)}, bf16[4096,128]{1,0:T(8,128)(2,1)}) custom-call(s32[1,26]{1,0:T(1,128)S(1)} %copy-done, s32[1]{0:T(128)} %bitcast.core_ref, s32[1]{0:T(128)} %bitcast.1.at_ref, bf16[16,128,128]{2,1,0:T(8,128)(2,1)S(1)} %all-to-all-done.own_ref, ...), custom_call_target="tpu_custom_call" | custom-call | flops 5368709120 | bytes 4194304 | tf_op jit(solution)/shard_map/pallas_call | solution.py:51
  37.5 4.2 %all-to-all-start.1 = ((bf16[16,184,128]{2,1,0:T(8,128)(2,1)}), bf16[16,184,128]{2,1,0:T(8,128)(2,1)S(1)}, u32[]{:S(2)}, u32[]{:S(2)}) async-start(bf16[16,184,128]{2,1,0:T(8,128)(2,1)} %get-tuple-element.39), calls=%async_computation.1 | async-start | bytes 1507328 | tf_op jit(solution)/shard_map/all_to_all | solution.py:768
  41.8 3.8 %collective-permute-start.5 = (bf16[256,128]{1,0:T(8,128)(2,1)S(1)}, bf16[256,128]{1,0:T(8,128)(2,1)S(1)}, u32[]{:S(2)}, u32[]{:S(2)}) collective-permute-start(bf16[256,128]{1,0:T(8,128)(2,1)S(1)} %get-tuple-element.50), channel_id=1, source_target_pairs={{0,8},{2,10},{4,12},{6,14},{8,16},{10,18},{12,20},{14,22},{16,24},... | collective-permute-start | bytes 196616 | tf_op jit(solution)/shard_map/ppermute | solution.py:760
  45.6 4.3 %collective-permute-start.4 = (bf16[256,128]{1,0:T(8,128)(2,1)S(1)}, bf16[256,128]{1,0:T(8,128)(2,1)S(1)}, u32[]{:S(2)}, u32[]{:S(2)}) collective-permute-start(bf16[256,128]{1,0:T(8,128)(2,1)S(1)} %get-tuple-element.51), channel_id=1, source_target_pairs={{0,6},{2,8},{4,10},{6,12},{8,14},{10,16},{12,18},{14,20},{16,22},{... | collective-permute-start | bytes 196616 | tf_op jit(solution)/shard_map/ppermute | solution.py:760
  49.9 3.4 %collective-permute-start.3 = (bf16[256,128]{1,0:T(8,128)(2,1)S(1)}, bf16[256,128]{1,0:T(8,128)(2,1)S(1)}, u32[]{:S(2)}, u32[]{:S(2)}) collective-permute-start(bf16[256,128]{1,0:T(8,128)(2,1)S(1)} %get-tuple-element.52), channel_id=1, source_target_pairs={{0,4},{2,6},{4,8},{6,10},{8,12},{10,14},{12,16},{14,18},{16,20},{1... | collective-permute-start | bytes 196616 | tf_op jit(solution)/shard_map/ppermute | solution.py:760
  53.2 2.5 %collective-permute-start.2 = (bf16[256,128]{1,0:T(8,128)(2,1)S(1)}, bf16[256,128]{1,0:T(8,128)(2,1)S(1)}, u32[]{:S(2)}, u32[]{:S(2)}) collective-permute-start(bf16[256,128]{1,0:T(8,128)(2,1)S(1)} %get-tuple-element.53), channel_id=1, source_target_pairs={{0,2},{2,4},{4,6},{6,8},{8,10},{10,12},{12,14},{14,16},{16,18},{18... | collective-permute-start | bytes 196616 | tf_op jit(solution)/shard_map/ppermute | solution.py:760
  55.7 0.0 collective-permute-done.5
  55.7 0.0 collective-permute-done.4
  55.7 1.5 %collective-permute-done.3 = bf16[256,128]{1,0:T(8,128)(2,1)S(1)} collective-permute-done((bf16[256,128]{1,0:T(8,128)(2,1)S(1)}, bf16[256,128]{1,0:T(8,128)(2,1)S(1)}, u32[]{:S(2)}, u32[]{:S(2)}) %collective-permute-start.3) | collective-permute-done | bytes 65568 | tf_op jit(solution)/shard_map/ppermute | solution.py:760
  57.2 1.7 %collective-permute-done.2 = bf16[256,128]{1,0:T(8,128)(2,1)S(1)} collective-permute-done((bf16[256,128]{1,0:T(8,128)(2,1)S(1)}, bf16[256,128]{1,0:T(8,128)(2,1)S(1)}, u32[]{:S(2)}, u32[]{:S(2)}) %collective-permute-start.2) | collective-permute-done | bytes 65568 | tf_op jit(solution)/shard_map/ppermute | solution.py:760
  58.9 2.3 %all-to-all-done.1.slots_ref.own_ref = bf16[16,184,128]{2,1,0:T(8,128)(2,1)S(1)} async-done(((bf16[16,184,128]{2,1,0:T(8,128)(2,1)}), bf16[16,184,128]{2,1,0:T(8,128)(2,1)S(1)}, u32[]{:S(2)}, u32[]{:S(2)}) %all-to-all-start.1) | async-done | bytes 753696 | tf_op jit(solution)/shard_map/all_to_all | solution.py:768
  61.2 1.0 %shard_map.97 = bf16[16,176,128]{2,1,0:T(8,128)(2,1)} custom-call(bf16[16,184,128]{2,1,0:T(8,128)(2,1)S(1)} %all-to-all-done.1.slots_ref.own_ref), custom_call_target="tpu_custom_call" | custom-call | bytes 4194304 | tf_op jit(solution)/shard_map/pallas_call | solution.py:51
  62.2 7.0 %all-to-all-start.2 = ((bf16[16,176,128]{2,1,0:T(8,128)(2,1)}), bf16[16,176,128]{2,1,0:T(8,128)(2,1)S(1)}, u32[]{:S(2)}, u32[]{:S(2)}) async-start(bf16[16,176,128]{2,1,0:T(8,128)(2,1)} %shard_map.97), calls=%async_computation.2 | async-start | bytes 1441792 | tf_op jit(solution)/shard_map/all_to_all | solution.py:768
  69.3 0.1 collective-permute-start.7
  69.4 0.5 collective-permute-start.6
  69.8 1.1 %collective-permute-done.6.other_ref = bf16[16,8,128]{2,1,0:T(8,128)(2,1)S(1)} collective-permute-done((bf16[16,8,128]{2,1,0:T(8,128)(2,1)S(1)}, bf16[16,8,128]{2,1,0:T(8,128)(2,1)S(1)}, u32[]{:S(2)}, u32[]{:S(2)}) %collective-permute-start.6) | collective-permute-done | bytes 32800 | tf_op jit(solution)/shard_map/ppermute | solution.py:764
  70.9 0.0 collective-permute-done.7.other_faces_ref
  70.9 9.1 %shard_map.99 = bf16[8,64,512]{2,1,0:T(8,128)(2,1)} custom-call(s32[1,26]{1,0:T(1,128)S(1)} %copy-done, s32[1]{0:T(128)} %bitcast.core_ref, s32[1]{0:T(128)} %bitcast.1.at_ref, bf16[16,184,128]{2,1,0:T(8,128)(2,1)S(1)} %all-to-all-done.1.slots_ref.own_ref, bf16[16,8,128]{2,1,0:T(8,128)(2,1)S(1)} %collective-permute-done.6.other_ref, ...), custom_call_target="tpu_custom_call" | custom-call | flops 5368709120 | bytes 4194304 | tf_op jit(solution)/shard_map/pallas_call | solution.py:51
  80.0 7.8 %all-to-all-done.2 = bf16[16,176,128]{2,1,0:T(8,128)(2,1)S(1)} async-done(((bf16[16,176,128]{2,1,0:T(8,128)(2,1)}), bf16[16,176,128]{2,1,0:T(8,128)(2,1)S(1)}, u32[]{:S(2)}, u32[]{:S(2)}) %all-to-all-start.2) | async-done | bytes 720928 | tf_op jit(solution)/shard_map/all_to_all | solution.py:768
  87.9 1.2 %shard_map.98 = (f32[27,64,128]{2,1,0:T(8,128)}, f32[8,128,128]{2,1,0:T(8,128)}) custom-call(s32[1]{0:T(128)} %bitcast.core_ref, bf16[2816,128]{1,0:T(8,128)(2,1)S(1)} %bitcast.19), custom_call_target="tpu_custom_call" | custom-call | bytes 4194304 | tf_op jit(solution)/shard_map/pallas_call | solution.py:51
  (3 shorter events, 0.1 us)
Async XLA Ops:
  0.6 10.9 %collective-permute-start = (bf16[8,64,512]{2,1,0:T(8,128)(2,1)}, bf16[8,64,512]{2,1,0:T(8,128)(2,1)S(1)}, u32[]{:S(2)}, u32[]{:S(2)}) collective-permute-start(bf16[8,64,512]{2,1,0:T(8,128)(2,1)} %bitcast.20), channel_id=1, source_target_pairs={{0,1},{1,0},{2,3},{3,2},{4,5},{5,4},{6,7},{7,6},{8,9},{9,8},{10,11... | collective-permute-start | bytes 1572872 | tf_op jit(solution)/shard_map/ppermute | solution.py:764
  3.5 23.4 %all-to-all-start = ((bf16[16,128,128]{2,1,0:T(8,128)(2,1)}), bf16[16,128,128]{2,1,0:T(8,128)(2,1)S(1)}, u32[]{:S(2)}, u32[]{:S(2)}) async-start(bf16[16,128,128]{2,1,0:T(8,128)(2,1)} %shard_map.93), calls=%async_computation | async-start | bytes 1048576 | tf_op jit(solution)/shard_map/all_to_all | solution.py:768
  23.1 5.8 %copy-start = (s32[1,26]{1,0:T(1,128)S(1)}, s32[1,26]{1,0:T(1,128)}, u32[]{:S(2)}) copy-start(s32[1,26]{1,0:T(1,128)} %near_ref.3) | copy-start | bytes 316
  26.9 1.9 %collective-permute-start.1 = (bf16[16,128,128]{2,1,0:T(8,128)(2,1)S(1)}, bf16[16,128,128]{2,1,0:T(8,128)(2,1)S(1)}, u32[]{:S(2)}, u32[]{:S(2)}) collective-permute-start(bf16[16,128,128]{2,1,0:T(8,128)(2,1)S(1)} %all-to-all-done.own_ref), channel_id=1, source_target_pairs={{0,1},{1,0},{2,3},{3,2},{4,5},{5,4},{6,7},{7,6},{8,9},{9,8},{10,11... | collective-permute-start | bytes 1572872 | tf_op jit(solution)/shard_map/ppermute | solution.py:764
  37.5 23.7 %all-to-all-start.1 = ((bf16[16,184,128]{2,1,0:T(8,128)(2,1)}), bf16[16,184,128]{2,1,0:T(8,128)(2,1)S(1)}, u32[]{:S(2)}, u32[]{:S(2)}) async-start(bf16[16,184,128]{2,1,0:T(8,128)(2,1)} %get-tuple-element.39), calls=%async_computation.1 | async-start | bytes 1507328 | tf_op jit(solution)/shard_map/all_to_all | solution.py:768
  41.8 14.0 %collective-permute-start.5 = (bf16[256,128]{1,0:T(8,128)(2,1)S(1)}, bf16[256,128]{1,0:T(8,128)(2,1)S(1)}, u32[]{:S(2)}, u32[]{:S(2)}) collective-permute-start(bf16[256,128]{1,0:T(8,128)(2,1)S(1)} %get-tuple-element.50), channel_id=1, source_target_pairs={{0,8},{2,10},{4,12},{6,14},{8,16},{10,18},{12,20},{14,22},{16,24},... | collective-permute-start | bytes 196616 | tf_op jit(solution)/shard_map/ppermute | solution.py:760
  45.6 10.2 %collective-permute-start.4 = (bf16[256,128]{1,0:T(8,128)(2,1)S(1)}, bf16[256,128]{1,0:T(8,128)(2,1)S(1)}, u32[]{:S(2)}, u32[]{:S(2)}) collective-permute-start(bf16[256,128]{1,0:T(8,128)(2,1)S(1)} %get-tuple-element.51), channel_id=1, source_target_pairs={{0,6},{2,8},{4,10},{6,12},{8,14},{10,16},{12,18},{14,20},{16,22},{... | collective-permute-start | bytes 196616 | tf_op jit(solution)/shard_map/ppermute | solution.py:760
  49.9 7.3 %collective-permute-start.3 = (bf16[256,128]{1,0:T(8,128)(2,1)S(1)}, bf16[256,128]{1,0:T(8,128)(2,1)S(1)}, u32[]{:S(2)}, u32[]{:S(2)}) collective-permute-start(bf16[256,128]{1,0:T(8,128)(2,1)S(1)} %get-tuple-element.52), channel_id=1, source_target_pairs={{0,4},{2,6},{4,8},{6,10},{8,12},{10,14},{12,16},{14,18},{16,20},{1... | collective-permute-start | bytes 196616 | tf_op jit(solution)/shard_map/ppermute | solution.py:760
  53.2 5.7 %collective-permute-start.2 = (bf16[256,128]{1,0:T(8,128)(2,1)S(1)}, bf16[256,128]{1,0:T(8,128)(2,1)S(1)}, u32[]{:S(2)}, u32[]{:S(2)}) collective-permute-start(bf16[256,128]{1,0:T(8,128)(2,1)S(1)} %get-tuple-element.53), channel_id=1, source_target_pairs={{0,2},{2,4},{4,6},{6,8},{8,10},{10,12},{12,14},{14,16},{16,18},{18... | collective-permute-start | bytes 196616 | tf_op jit(solution)/shard_map/ppermute | solution.py:760
  62.2 25.7 %all-to-all-start.2 = ((bf16[16,176,128]{2,1,0:T(8,128)(2,1)}), bf16[16,176,128]{2,1,0:T(8,128)(2,1)S(1)}, u32[]{:S(2)}, u32[]{:S(2)}) async-start(bf16[16,176,128]{2,1,0:T(8,128)(2,1)} %shard_map.97), calls=%async_computation.2 | async-start | bytes 1441792 | tf_op jit(solution)/shard_map/all_to_all | solution.py:768
  69.3 1.7 %collective-permute-start.7 = (bf16[4,256,128]{2,1,0:T(8,128)(2,1)S(1)}, bf16[4,256,128]{2,1,0:T(8,128)(2,1)S(1)}, u32[]{:S(2)}, u32[]{:S(2)}) collective-permute-start(bf16[4,256,128]{2,1,0:T(8,128)(2,1)S(1)} %pad_maximum_fusion.own_faces_ref), channel_id=1, source_target_pairs={{0,1},{1,0},{2,3},{3,2},{4,5},{5,4},{6,7},{7,6},{8,9},{9,8},{10,11... | collective-permute-start | bytes 786440 | tf_op jit(solution)/shard_map/ppermute | solution.py:764
  69.4 1.6 %collective-permute-start.6 = (bf16[16,8,128]{2,1,0:T(8,128)(2,1)S(1)}, bf16[16,8,128]{2,1,0:T(8,128)(2,1)S(1)}, u32[]{:S(2)}, u32[]{:S(2)}) collective-permute-start(bf16[16,8,128]{2,1,0:T(8,128)(2,1)S(1)} %slice.19), channel_id=1, source_target_pairs={{0,1},{1,0},{2,3},{3,2},{4,5},{5,4},{6,7},{7,6},{8,9},{9,8},{10,11... | collective-permute-start | bytes 98312 | tf_op jit(solution)/shard_map/ppermute | solution.py:764

commit v5 on v4

--- a/solution.py
+++ b/solution.py
@@ -80,7 +80,14 @@
     return (level.astype(F32) < tall).astype(F32)
 
 
-def fill_slots(rows_ref, near_ref, slots_ref):
+def fill_slots(rows_ref, near_ref, slots_ref, slots_hbm, left):
+    def leave(k):
+        block = near_ref[0, k]
+        rows = slice(0, 128 if DIRECTIONS[k].count(0) == 2 else 16)
+        return pltpu.make_async_copy(
+            slots_ref.at[block, rows], slots_hbm.at[block, rows], left.at[k]
+        )
+
     for k, (dx, dy, dz) in enumerate(DIRECTIONS):
         block = near_ref[0, k]
         xh = 7 if dx == 1 else 0
@@ -88,7 +95,7 @@
         z = 15 if dz == 1 else 0
 
         @pl.when(block >= 0)
-        def _(dx=dx, dy=dy, dz=dz, xh=xh, y=y, z=z, block=block):
+        def _(k=k, dx=dx, dy=dy, dz=dz, xh=xh, y=y, z=z, block=block):
             zeros = [d == 0 for d in (dx, dy, dz)]
             if zeros == [False, True, True]:
                 plane = rows_ref[xh * 256 : xh * 256 + 256, :]
@@ -115,6 +122,13 @@
                 at = xh * 256 + y * 16 + z
                 region = jnp.broadcast_to(rows_ref[at : at + 1, :], (16, 128))
             slots_ref[block, 0 : region.shape[0], :] = region.astype(BF16)
+            leave(k).start()
+
+    for k in range(26):
+
+        @pl.when(near_ref[0, k] >= 0)
+        def _(k=k):
+            leave(k).wait()
 
 
 def fill_edges(rows_ref, near_ref, slots_ref, start):
@@ -284,8 +298,8 @@
 
 
 def send_features(
-    near_hbm, heights_hbm, features_hbm, slots_ref,
-    near_ref, heights_ref, features_ref, rows_ref, arrived
+    near_hbm, heights_hbm, features_hbm, slots_hbm,
+    near_ref, heights_ref, features_ref, rows_ref, slots_ref, arrived, left
 ):
     copies = [
         pltpu.make_async_copy(near_hbm, near_ref, arrived.at[8]),
@@ -313,7 +327,7 @@
                     source = (vx * 8 + vy) * 8
                     rows_ref[at : at + 8, :] = turned[source : source + 8]
     copies[0].wait()
-    fill_slots(rows_ref, near_ref, slots_ref)
+    fill_slots(rows_ref, near_ref, slots_ref, slots_hbm, left)
 
 
 def own_first_taps(shift, conv_ref, yz):
@@ -789,19 +803,22 @@
     turned = features.transpose(0, 2, 1)
     slots = kernel_call(
         send_features,
-        out(devices, 128, 128),
+        held_out(devices, 128, 128),
         [hbm()] * 3,
-        vmem(),
+        hbm(),
         [
             pltpu.SMEM(neighbours.shape, jnp.int32),
             memory(8, 64, dtype=jnp.int32),
             memory(8, 64, 512),
             memory(2048, 128, dtype=F32),
+            memory(devices, 128, 128),
             copies(10),
+            copies(26),
         ],
     )(neighbours, heights, turned)
+    slots, turned_after = lax.optimization_barrier((slots, turned))
     came = to_all(slots)
-    other_turned = over_chan(turned)
+    other_turned = over_chan(turned_after)
 
     held = [
         held_out(18, 288, 256),

time: 89.7 us -> 89.4 us (level)
  transfers between devices with their start and end apart: 11 -> 11, of which waited for: 6 -> 6; matrix products, arithmetic and copies ran while one was open for 0% -> 0% of each run, Pallas kernels for 28% -> 26%
where the time goes in v5:
time: 89.4 us; the launch traced here: 88.8 us
  Pallas kernels  36.3 us (41%)
  starting transfers between devices  33.8 us (38%)
  waiting for transfers between devices  17.8 us (20%)
    pallas_call x7, Pallas kernels, run(): return call(*placed)  36.3 us
    all_to_all x3, starting transfers between devices, to_all(): return lax.all_to_all(slots, 'space', 0, 0, tiled=True)  18.8 us
    ppermute x4, starting transfers between devices, over_space(): return lax.ppermute(block, ('space', 'chan'), route)  13.9 us
    all_to_all x3, waiting for transfers between devices, to_all(): return lax.all_to_all(slots, 'space', 0, 0, tiled=True)  13.5 us
    ppermute x4, waiting for transfers between devices, over_space(): return lax.ppermute(block, ('space', 'chan'), route)  3.21 us
  transfers between devices with their start and end apart: 11, of which 6 were waited for; matrix products, arithmetic and copies ran while one was open for 0% of the time, Pallas kernels for 26%

profile of v5, /device:TPU:0, one launch (start us, length us, event | category | flops | bytes accessed | tf_op | source)
XLA Modules:
  0.0 88.8 jit_solution(1579810153119138160)
XLA Ops:
  0.6 2.5 %shard_map.93 = bf16[16,128,128]{2,1,0:T(8,128)(2,1)} custom-call(s32[1,26]{1,0:T(1,128)} %near_ref.3, s32[8,64]{1,0:T(8,128)} %heights_hbm.3, bf16[8,64,512]{2,1,0:T(8,128)(2,1)} %bitcast.20), custom_call_target="tpu_custom_call" | custom-call | bytes 4194304 | tf_op jit(solution)/shard_map/pallas_call | solution.py:51
  3.1 0.5 collective-permute-start
  3.7 7.7 %all-to-all-start = ((bf16[16,128,128]{2,1,0:T(8,128)(2,1)}), bf16[16,128,128]{2,1,0:T(8,128)(2,1)S(1)}, u32[]{:S(2)}, u32[]{:S(2)}) async-start(bf16[16,128,128]{2,1,0:T(8,128)(2,1)} %shard_map.93), calls=%async_computation | async-start | bytes 1048576 | tf_op jit(solution)/shard_map/all_to_all | solution.py:782
  11.4 0.0 collective-permute-done.other_hbm
  11.4 11.5 %shard_map.94 = (bf16[18,288,256]{2,1,0:T(8,128)(2,1)}, bf16[4096,128]{1,0:T(8,128)(2,1)}, f32[4096,128]{1,0:T(8,128)}, f32[4096,128]{1,0:T(8,128)}, bf16[3456,1...) custom-call(s32[1]{0:T(128)} %bitcast.core_ref, bf16[27,128,128]{2,1,0:T(8,128)(2,1)} %conv_hbm.3, ...), custom_call_target="tpu_custom_call" | custom-call | flops 5368709120 | bytes 4194304 | tf_op jit(solution)/shard_map/pallas_call | solution.py:51
  22.9 0.0 copy-start
  22.9 3.9 %all-to-all-done.own_ref = bf16[16,128,128]{2,1,0:T(8,128)(2,1)S(1)} async-done(((bf16[16,128,128]{2,1,0:T(8,128)(2,1)}), bf16[16,128,128]{2,1,0:T(8,128)(2,1)S(1)}, u32[]{:S(2)}, u32[]{:S(2)}) %all-to-all-start) | async-done | bytes 524320 | tf_op jit(solution)/shard_map/all_to_all | solution.py:782
  26.8 0.0 collective-permute-start.1
  26.8 1.9 %shard_map.95 = (bf16[3456,128]{1,0:T(8,128)(2,1)S(1)}, f32[4096,128]{1,0:T(8,128)S(1)}) custom-call(bf16[3456,128]{1,0:T(8,128)(2,1)} %get-tuple-element.34.taps_hbm, f32[4096,128]{1,0:T(8,128)} %get-tuple-element.35.inner_hbm), custom_call_target="tpu_custom_call" | custom-call | bytes 4194304 | tf_op jit(solution)/shard_map/pallas_call | solution.py:51
  28.7 0.0 collective-permute-done.1.other_ref
  28.7 0.0 copy-done
  28.7 8.6 %shard_map.96 = (bf16[16,184,128]{2,1,0:T(8,128)(2,1)}, bf16[4,256,128]{2,1,0:T(8,128)(2,1)S(1)}, bf16[512,128]{1,0:T(8,128)(2,1)}, bf16[4096,128]{1,0:T(8,128)(2,1)}) custom-call(s32[1,26]{1,0:T(1,128)S(1)} %copy-done, s32[1]{0:T(128)} %bitcast.core_ref, s32[1]{0:T(128)} %bitcast.1.at_ref, bf16[16,128,128]{2,1,0:T(8,128)(2,1)S(1)} %all-to-all-done.own_ref, ...), custom_call_target="tpu_custom_call" | custom-call | flops 5368709120 | bytes 4194304 | tf_op jit(solution)/shard_map/pallas_call | solution.py:51
  37.4 4.1 %all-to-all-start.1 = ((bf16[16,184,128]{2,1,0:T(8,128)(2,1)}), bf16[16,184,128]{2,1,0:T(8,128)(2,1)S(1)}, u32[]{:S(2)}, u32[]{:S(2)}) async-start(bf16[16,184,128]{2,1,0:T(8,128)(2,1)} %get-tuple-element.43), calls=%async_computation.1 | async-start | bytes 1507328 | tf_op jit(solution)/shard_map/all_to_all | solution.py:782
  41.5 3.8 %collective-permute-start.5 = (bf16[256,128]{1,0:T(8,128)(2,1)S(1)}, bf16[256,128]{1,0:T(8,128)(2,1)S(1)}, u32[]{:S(2)}, u32[]{:S(2)}) collective-permute-start(bf16[256,128]{1,0:T(8,128)(2,1)S(1)} %get-tuple-element.54), channel_id=1, source_target_pairs={{0,8},{2,10},{4,12},{6,14},{8,16},{10,18},{12,20},{14,22},{16,24},... | collective-permute-start | bytes 196616 | tf_op jit(solution)/shard_map/ppermute | solution.py:774
  45.3 4.3 %collective-permute-start.4 = (bf16[256,128]{1,0:T(8,128)(2,1)S(1)}, bf16[256,128]{1,0:T(8,128)(2,1)S(1)}, u32[]{:S(2)}, u32[]{:S(2)}) collective-permute-start(bf16[256,128]{1,0:T(8,128)(2,1)S(1)} %get-tuple-element.55), channel_id=1, source_target_pairs={{0,6},{2,8},{4,10},{6,12},{8,14},{10,16},{12,18},{14,20},{16,22},{... | collective-permute-start | bytes 196616 | tf_op jit(solution)/shard_map/ppermute | solution.py:774
  49.6 3.4 %collective-permute-start.3 = (bf16[256,128]{1,0:T(8,128)(2,1)S(1)}, bf16[256,128]{1,0:T(8,128)(2,1)S(1)}, u32[]{:S(2)}, u32[]{:S(2)}) collective-permute-start(bf16[256,128]{1,0:T(8,128)(2,1)S(1)} %get-tuple-element.56), channel_id=1, source_target_pairs={{0,4},{2,6},{4,8},{6,10},{8,12},{10,14},{12,16},{14,18},{16,20},{1... | collective-permute-start | bytes 196616 | tf_op jit(solution)/shard_map/ppermute | solution.py:774
  52.9 2.5 %collective-permute-start.2 = (bf16[256,128]{1,0:T(8,128)(2,1)S(1)}, bf16[256,128]{1,0:T(8,128)(2,1)S(1)}, u32[]{:S(2)}, u32[]{:S(2)}) collective-permute-start(bf16[256,128]{1,0:T(8,128)(2,1)S(1)} %get-tuple-element.57), channel_id=1, source_target_pairs={{0,2},{2,4},{4,6},{6,8},{8,10},{10,12},{12,14},{14,16},{16,18},{18... | collective-permute-start | bytes 196616 | tf_op jit(solution)/shard_map/ppermute | solution.py:774
  55.4 0.0 collective-permute-done.5
  55.4 0.0 collective-permute-done.4
  55.5 1.5 %collective-permute-done.3 = bf16[256,128]{1,0:T(8,128)(2,1)S(1)} collective-permute-done((bf16[256,128]{1,0:T(8,128)(2,1)S(1)}, bf16[256,128]{1,0:T(8,128)(2,1)S(1)}, u32[]{:S(2)}, u32[]{:S(2)}) %collective-permute-start.3) | collective-permute-done | bytes 65568 | tf_op jit(solution)/shard_map/ppermute | solution.py:774
  56.9 1.7 %collective-permute-done.2 = bf16[256,128]{1,0:T(8,128)(2,1)S(1)} collective-permute-done((bf16[256,128]{1,0:T(8,128)(2,1)S(1)}, bf16[256,128]{1,0:T(8,128)(2,1)S(1)}, u32[]{:S(2)}, u32[]{:S(2)}) %collective-permute-start.2) | collective-permute-done | bytes 65568 | tf_op jit(solution)/shard_map/ppermute | solution.py:774
  58.7 2.3 %all-to-all-done.1.slots_ref.own_ref = bf16[16,184,128]{2,1,0:T(8,128)(2,1)S(1)} async-done(((bf16[16,184,128]{2,1,0:T(8,128)(2,1)}), bf16[16,184,128]{2,1,0:T(8,128)(2,1)S(1)}, u32[]{:S(2)}, u32[]{:S(2)}) %all-to-all-start.1) | async-done | bytes 753696 | tf_op jit(solution)/shard_map/all_to_all | solution.py:782
  60.9 1.0 %shard_map.97 = bf16[16,176,128]{2,1,0:T(8,128)(2,1)} custom-call(bf16[16,184,128]{2,1,0:T(8,128)(2,1)S(1)} %all-to-all-done.1.slots_ref.own_ref), custom_call_target="tpu_custom_call" | custom-call | bytes 4194304 | tf_op jit(solution)/shard_map/pallas_call | solution.py:51
  61.9 7.0 %all-to-all-start.2 = ((bf16[16,176,128]{2,1,0:T(8,128)(2,1)}), bf16[16,176,128]{2,1,0:T(8,128)(2,1)S(1)}, u32[]{:S(2)}, u32[]{:S(2)}) async-start(bf16[16,176,128]{2,1,0:T(8,128)(2,1)} %shard_map.97), calls=%async_computation.2 | async-start | bytes 1441792 | tf_op jit(solution)/shard_map/all_to_all | solution.py:782
  69.0 0.1 collective-permute-start.7
  69.1 0.5 collective-permute-start.6
  69.6 1.1 %collective-permute-done.6.other_ref = bf16[16,8,128]{2,1,0:T(8,128)(2,1)S(1)} collective-permute-done((bf16[16,8,128]{2,1,0:T(8,128)(2,1)S(1)}, bf16[16,8,128]{2,1,0:T(8,128)(2,1)S(1)}, u32[]{:S(2)}, u32[]{:S(2)}) %collective-permute-start.6) | collective-permute-done | bytes 32800 | tf_op jit(solution)/shard_map/ppermute | solution.py:778
  70.6 0.0 collective-permute-done.7.other_faces_ref
  70.6 9.6 %shard_map.99 = bf16[8,64,512]{2,1,0:T(8,128)(2,1)} custom-call(s32[1,26]{1,0:T(1,128)S(1)} %copy-done, s32[1]{0:T(128)} %bitcast.core_ref, s32[1]{0:T(128)} %bitcast.1.at_ref, bf16[16,184,128]{2,1,0:T(8,128)(2,1)S(1)} %all-to-all-done.1.slots_ref.own_ref, bf16[16,8,128]{2,1,0:T(8,128)(2,1)S(1)} %collective-permute-done.6.other_ref, ...), custom_call_target="tpu_custom_call" | custom-call | flops 5368709120 | bytes 4194304 | tf_op jit(solution)/shard_map/pallas_call | solution.py:51
  80.2 7.4 %all-to-all-done.2 = bf16[16,176,128]{2,1,0:T(8,128)(2,1)S(1)} async-done(((bf16[16,176,128]{2,1,0:T(8,128)(2,1)}), bf16[16,176,128]{2,1,0:T(8,128)(2,1)S(1)}, u32[]{:S(2)}, u32[]{:S(2)}) %all-to-all-start.2) | async-done | bytes 720928 | tf_op jit(solution)/shard_map/all_to_all | solution.py:782
  87.6 1.2 %shard_map.98 = (f32[27,64,128]{2,1,0:T(8,128)}, f32[8,128,128]{2,1,0:T(8,128)}) custom-call(s32[1]{0:T(128)} %bitcast.core_ref, bf16[2816,128]{1,0:T(8,128)(2,1)S(1)} %bitcast.19), custom_call_target="tpu_custom_call" | custom-call | bytes 4194304 | tf_op jit(solution)/shard_map/pallas_call | solution.py:51
  (3 shorter events, 0.1 us)
Async XLA Ops:
  3.1 8.2 %collective-permute-start = (bf16[8,64,512]{2,1,0:T(8,128)(2,1)}, bf16[8,64,512]{2,1,0:T(8,128)(2,1)S(1)}, u32[]{:S(2)}, u32[]{:S(2)}) collective-permute-start(bf16[8,64,512]{2,1,0:T(8,128)(2,1)} %bitcast.21), channel_id=1, source_target_pairs={{0,1},{1,0},{2,3},{3,2},{4,5},{5,4},{6,7},{7,6},{8,9},{9,8},{10,11... | collective-permute-start | bytes 1572872 | tf_op jit(solution)/shard_map/ppermute | solution.py:778
  3.7 23.2 %all-to-all-start = ((bf16[16,128,128]{2,1,0:T(8,128)(2,1)}), bf16[16,128,128]{2,1,0:T(8,128)(2,1)S(1)}, u32[]{:S(2)}, u32[]{:S(2)}) async-start(bf16[16,128,128]{2,1,0:T(8,128)(2,1)} %shard_map.93), calls=%async_computation | async-start | bytes 1048576 | tf_op jit(solution)/shard_map/all_to_all | solution.py:782
  22.9 5.8 %copy-start = (s32[1,26]{1,0:T(1,128)S(1)}, s32[1,26]{1,0:T(1,128)}, u32[]{:S(2)}) copy-start(s32[1,26]{1,0:T(1,128)} %near_ref.3) | copy-start | bytes 316
  26.8 1.9 %collective-permute-start.1 = (bf16[16,128,128]{2,1,0:T(8,128)(2,1)S(1)}, bf16[16,128,128]{2,1,0:T(8,128)(2,1)S(1)}, u32[]{:S(2)}, u32[]{:S(2)}) collective-permute-start(bf16[16,128,128]{2,1,0:T(8,128)(2,1)S(1)} %all-to-all-done.own_ref), channel_id=1, source_target_pairs={{0,1},{1,0},{2,3},{3,2},{4,5},{5,4},{6,7},{7,6},{8,9},{9,8},{10,11... | collective-permute-start | bytes 1572872 | tf_op jit(solution)/shard_map/ppermute | solution.py:778
  37.4 23.6 %all-to-all-start.1 = ((bf16[16,184,128]{2,1,0:T(8,128)(2,1)}), bf16[16,184,128]{2,1,0:T(8,128)(2,1)S(1)}, u32[]{:S(2)}, u32[]{:S(2)}) async-start(bf16[16,184,128]{2,1,0:T(8,128)(2,1)} %get-tuple-element.43), calls=%async_computation.1 | async-start | bytes 1507328 | tf_op jit(solution)/shard_map/all_to_all | solution.py:782
  41.5 14.0 %collective-permute-start.5 = (bf16[256,128]{1,0:T(8,128)(2,1)S(1)}, bf16[256,128]{1,0:T(8,128)(2,1)S(1)}, u32[]{:S(2)}, u32[]{:S(2)}) collective-permute-start(bf16[256,128]{1,0:T(8,128)(2,1)S(1)} %get-tuple-element.54), channel_id=1, source_target_pairs={{0,8},{2,10},{4,12},{6,14},{8,16},{10,18},{12,20},{14,22},{16,24},... | collective-permute-start | bytes 196616 | tf_op jit(solution)/shard_map/ppermute | solution.py:774
  45.3 10.2 %collective-permute-start.4 = (bf16[256,128]{1,0:T(8,128)(2,1)S(1)}, bf16[256,128]{1,0:T(8,128)(2,1)S(1)}, u32[]{:S(2)}, u32[]{:S(2)}) collective-permute-start(bf16[256,128]{1,0:T(8,128)(2,1)S(1)} %get-tuple-element.55), channel_id=1, source_target_pairs={{0,6},{2,8},{4,10},{6,12},{8,14},{10,16},{12,18},{14,20},{16,22},{... | collective-permute-start | bytes 196616 | tf_op jit(solution)/shard_map/ppermute | solution.py:774
  49.6 7.3 %collective-permute-start.3 = (bf16[256,128]{1,0:T(8,128)(2,1)S(1)}, bf16[256,128]{1,0:T(8,128)(2,1)S(1)}, u32[]{:S(2)}, u32[]{:S(2)}) collective-permute-start(bf16[256,128]{1,0:T(8,128)(2,1)S(1)} %get-tuple-element.56), channel_id=1, source_target_pairs={{0,4},{2,6},{4,8},{6,10},{8,12},{10,14},{12,16},{14,18},{16,20},{1... | collective-permute-start | bytes 196616 | tf_op jit(solution)/shard_map/ppermute | solution.py:774
  52.9 5.7 %collective-permute-start.2 = (bf16[256,128]{1,0:T(8,128)(2,1)S(1)}, bf16[256,128]{1,0:T(8,128)(2,1)S(1)}, u32[]{:S(2)}, u32[]{:S(2)}) collective-permute-start(bf16[256,128]{1,0:T(8,128)(2,1)S(1)} %get-tuple-element.57), channel_id=1, source_target_pairs={{0,2},{2,4},{4,6},{6,8},{8,10},{10,12},{12,14},{14,16},{16,18},{18... | collective-permute-start | bytes 196616 | tf_op jit(solution)/shard_map/ppermute | solution.py:774
  61.9 25.7 %all-to-all-start.2 = ((bf16[16,176,128]{2,1,0:T(8,128)(2,1)}), bf16[16,176,128]{2,1,0:T(8,128)(2,1)S(1)}, u32[]{:S(2)}, u32[]{:S(2)}) async-start(bf16[16,176,128]{2,1,0:T(8,128)(2,1)} %shard_map.97), calls=%async_computation.2 | async-start | bytes 1441792 | tf_op jit(solution)/shard_map/all_to_all | solution.py:782
  69.0 1.7 %collective-permute-start.7 = (bf16[4,256,128]{2,1,0:T(8,128)(2,1)S(1)}, bf16[4,256,128]{2,1,0:T(8,128)(2,1)S(1)}, u32[]{:S(2)}, u32[]{:S(2)}) collective-permute-start(bf16[4,256,128]{2,1,0:T(8,128)(2,1)S(1)} %pad_maximum_fusion.own_faces_ref), channel_id=1, source_target_pairs={{0,1},{1,0},{2,3},{3,2},{4,5},{5,4},{6,7},{7,6},{8,9},{9,8},{10,11... | collective-permute-start | bytes 786440 | tf_op jit(solution)/shard_map/ppermute | solution.py:778
  69.1 1.6 %collective-permute-start.6 = (bf16[16,8,128]{2,1,0:T(8,128)(2,1)S(1)}, bf16[16,8,128]{2,1,0:T(8,128)(2,1)S(1)}, u32[]{:S(2)}, u32[]{:S(2)}) collective-permute-start(bf16[16,8,128]{2,1,0:T(8,128)(2,1)S(1)} %slice.19), channel_id=1, source_target_pairs={{0,1},{1,0},{2,3},{3,2},{4,5},{5,4},{6,7},{7,6},{8,9},{9,8},{10,11... | collective-permute-start | bytes 98312 | tf_op jit(solution)/shard_map/ppermute | solution.py:778

commit v6 on v5

--- a/solution.py
+++ b/solution.py
@@ -15,6 +15,7 @@
 FILL_ORDER = sorted(range(26), key=lambda k: (abs(DIRECTIONS[k][2]), k))
 INACTIVE = -1e30
 EDGE = 8
+INNER = 4
 F32 = jnp.float32
 BF16 = jnp.bfloat16
 
@@ -80,12 +81,16 @@
     return (level.astype(F32) < tall).astype(F32)
 
 
+def slot_of(slots_ref, block):
+    return block % INNER * (slots_ref.shape[0] // INNER) + block // INNER
+
+
 def fill_slots(rows_ref, near_ref, slots_ref, slots_hbm, left):
     def leave(k):
-        block = near_ref[0, k]
+        slot = slot_of(slots_ref, near_ref[0, k])
         rows = slice(0, 128 if DIRECTIONS[k].count(0) == 2 else 16)
         return pltpu.make_async_copy(
-            slots_ref.at[block, rows], slots_hbm.at[block, rows], left.at[k]
+            slots_ref.at[slot, rows], slots_hbm.at[slot, rows], left.at[k]
         )
 
     for k, (dx, dy, dz) in enumerate(DIRECTIONS):
@@ -121,7 +126,7 @@
             else:
                 at = xh * 256 + y * 16 + z
                 region = jnp.broadcast_to(rows_ref[at : at + 1, :], (16, 128))
-            slots_ref[block, 0 : region.shape[0], :] = region.astype(BF16)
+            slots_ref[slot_of(slots_ref, block), 0 : region.shape[0], :] = region.astype(BF16)
             leave(k).start()
 
     for k in range(26):
@@ -151,7 +156,7 @@
                 rows = jnp.broadcast_to(rows_ref[at : at + 1, :], (16, 128))
             low, high = rows[:EDGE], swap_halves(rows[EDGE:])
             rows = jnp.where(low_lanes(low), low, high)
-            slots_ref[block, start : start + EDGE, :] = rows.astype(BF16)
+            slots_ref[slot_of(slots_ref, block), start : start + EDGE, :] = rows.astype(BF16)
 
 
 def fill_faces(rows_ref, near_ref, place, faces_ref):
@@ -284,8 +289,9 @@
         @pl.when(block >= 0)
         def _(offset=offset, block=block, face=face):
             height = 128 if face else 16 if start == 0 else EDGE
-            own = own_ref[block, start : start + height, :].astype(F32)
-            other = other_ref[block, 0:height, :].astype(F32)
+            slot = slot_of(own_ref, block)
+            own = own_ref[slot, start : start + height, :].astype(F32)
+            other = other_ref[slot, 0:height, :].astype(F32)
             first = jnp.where(low_lanes(own), own, swap_halves(other))
             second = jnp.where(low_lanes(own), swap_halves(own), other)
             if face or start:
@@ -543,8 +549,9 @@
 
 
 def joined_face(own_ref, other_ref, block):
-    own = own_ref[block].astype(F32)
-    other = other_ref[block].astype(F32)
+    slot = slot_of(own_ref, block)
+    own = own_ref[slot].astype(F32)
+    other = other_ref[slot].astype(F32)
     return jnp.concatenate(
         [
             jnp.where(low_lanes(own), own, swap_halves(other)),
@@ -779,7 +786,9 @@
 
 
 def to_all(slots):
-    return lax.all_to_all(slots, "space", 0, 0, tiled=True)
+    outer = lax.axis_size("space") // INNER
+    order = [plane * INNER + j for j in range(INNER) for plane in range(outer)]
+    return lax.all_to_all(slots, "space", 0, 0, axis_index_groups=[order], tiled=True)
 
 
 def local(features, heights, neighbours, w_conv, w_down, cotangent):

time: 89.4 us -> 92.4 us (1.034)
  waiting for transfers between devices: 17.8 us -> 24.7 us
  starting transfers between devices: 33.8 us -> 30.5 us
    all_to_all x3, waiting for transfers between devices: 13.5 us -> 21.2 us  [to_all(): lax.all_to_all(slots, 'space', 0, 0, axis_index_groups=[order], tiled=True)]
    all_to_all x3, starting transfers between devices: 18.8 us -> 15.5 us  [to_all(): lax.all_to_all(slots, 'space', 0, 0, axis_index_groups=[order], tiled=True)]
  transfers between devices with their start and end apart: 11 -> 11, of which waited for: 6 -> 5; matrix products, arithmetic and copies ran while one was open for 0% -> 0% of each run, Pallas kernels for 26% -> 25%
where the time goes in v6:
time: 92.4 us; the launch traced here: 91.9 us
  Pallas kernels  35.7 us (39%)
  starting transfers between devices  30.5 us (33%)
  waiting for transfers between devices  24.7 us (27%)
    pallas_call x7, Pallas kernels, run(): return call(*placed)  35.7 us
    all_to_all x3, waiting for transfers between devices, to_all(): lax.all_to_all(slots, 'space', 0, 0, axis_index_groups=[order], tiled=True)  21.2 us
    all_to_all x3, starting transfers between devices, to_all(): lax.all_to_all(slots, 'space', 0, 0, axis_index_groups=[order], tiled=True)  15.5 us
    ppermute x4, starting transfers between devices, over_space(): return lax.ppermute(block, ('space', 'chan'), route)  13.9 us
    ppermute x4, waiting for transfers between devices, over_space(): return lax.ppermute(block, ('space', 'chan'), route)  2.47 us
  transfers between devices with their start and end apart: 11, of which 5 were waited for; matrix products, arithmetic and copies ran while one was open for 0% of the time, Pallas kernels for 25%

profile of v6, /device:TPU:0, one launch (start us, length us, event | category | flops | bytes accessed | tf_op | source)
XLA Modules:
  0.0 91.9 jit_solution(2552284734660274730)
XLA Ops:
  0.6 2.5 %shard_map.93 = bf16[16,128,128]{2,1,0:T(8,128)(2,1)} custom-call(s32[1,26]{1,0:T(1,128)} %near_ref.3, s32[8,64]{1,0:T(8,128)} %heights_hbm.3, bf16[8,64,512]{2,1,0:T(8,128)(2,1)} %bitcast.20), custom_call_target="tpu_custom_call" | custom-call | bytes 4194304 | tf_op jit(solution)/shard_map/pallas_call | solution.py:52
  3.1 0.5 collective-permute-start
  3.6 7.8 %all-to-all-start = ((bf16[16,128,128]{2,1,0:T(8,128)(2,1)}), bf16[16,128,128]{2,1,0:T(8,128)(2,1)S(1)}, u32[]{:S(2)}, u32[]{:S(2)}) async-start(bf16[16,128,128]{2,1,0:T(8,128)(2,1)} %shard_map.93), calls=%async_computation | async-start | bytes 1048576 | tf_op jit(solution)/shard_map/all_to_all | solution.py:791
  11.4 0.0 collective-permute-done.other_hbm
  11.4 11.6 %shard_map.94 = (bf16[18,288,256]{2,1,0:T(8,128)(2,1)}, bf16[4096,128]{1,0:T(8,128)(2,1)}, f32[4096,128]{1,0:T(8,128)}, f32[4096,128]{1,0:T(8,128)}, bf16[3456,1...) custom-call(s32[1]{0:T(128)} %bitcast.core_ref, bf16[27,128,128]{2,1,0:T(8,128)(2,1)} %conv_hbm.3, ...), custom_call_target="tpu_custom_call" | custom-call | flops 5368709120 | bytes 4194304 | tf_op jit(solution)/shard_map/pallas_call | solution.py:52
  23.0 0.0 copy-start
  23.0 5.3 %all-to-all-done.own_ref = bf16[16,128,128]{2,1,0:T(8,128)(2,1)S(1)} async-done(((bf16[16,128,128]{2,1,0:T(8,128)(2,1)}), bf16[16,128,128]{2,1,0:T(8,128)(2,1)S(1)}, u32[]{:S(2)}, u32[]{:S(2)}) %all-to-all-start) | async-done | bytes 524320 | tf_op jit(solution)/shard_map/all_to_all | solution.py:791
  28.3 0.0 collective-permute-start.1
  28.3 1.9 %shard_map.95 = (bf16[3456,128]{1,0:T(8,128)(2,1)S(1)}, f32[4096,128]{1,0:T(8,128)S(1)}) custom-call(bf16[3456,128]{1,0:T(8,128)(2,1)} %get-tuple-element.34.taps_hbm, f32[4096,128]{1,0:T(8,128)} %get-tuple-element.35.inner_hbm), custom_call_target="tpu_custom_call" | custom-call | bytes 4194304 | tf_op jit(solution)/shard_map/pallas_call | solution.py:52
  30.2 0.0 collective-permute-done.1.other_ref
  30.2 0.0 copy-done
  30.2 8.5 %shard_map.96 = (bf16[16,184,128]{2,1,0:T(8,128)(2,1)}, bf16[4,256,128]{2,1,0:T(8,128)(2,1)S(1)}, bf16[512,128]{1,0:T(8,128)(2,1)}, bf16[4096,128]{1,0:T(8,128)(2,1)}) custom-call(s32[1,26]{1,0:T(1,128)S(1)} %copy-done, s32[1]{0:T(128)} %bitcast.core_ref, s32[1]{0:T(128)} %bitcast.1.at_ref, bf16[16,128,128]{2,1,0:T(8,128)(2,1)S(1)} %all-to-all-done.own_ref, ...), custom_call_target="tpu_custom_call" | custom-call | flops 5368709120 | bytes 4194304 | tf_op jit(solution)/shard_map/pallas_call | solution.py:52
  38.6 3.6 %all-to-all-start.1 = ((bf16[16,184,128]{2,1,0:T(8,128)(2,1)}), bf16[16,184,128]{2,1,0:T(8,128)(2,1)S(1)}, u32[]{:S(2)}, u32[]{:S(2)}) async-start(bf16[16,184,128]{2,1,0:T(8,128)(2,1)} %get-tuple-element.43), calls=%async_computation.1 | async-start | bytes 1507328 | tf_op jit(solution)/shard_map/all_to_all | solution.py:791
  42.3 3.7 %collective-permute-start.5 = (bf16[256,128]{1,0:T(8,128)(2,1)S(1)}, bf16[256,128]{1,0:T(8,128)(2,1)S(1)}, u32[]{:S(2)}, u32[]{:S(2)}) collective-permute-start(bf16[256,128]{1,0:T(8,128)(2,1)S(1)} %get-tuple-element.54), channel_id=1, source_target_pairs={{0,8},{2,10},{4,12},{6,14},{8,16},{10,18},{12,20},{14,22},{16,24},... | collective-permute-start | bytes 196616 | tf_op jit(solution)/shard_map/ppermute | solution.py:781
  46.0 4.4 %collective-permute-start.4 = (bf16[256,128]{1,0:T(8,128)(2,1)S(1)}, bf16[256,128]{1,0:T(8,128)(2,1)S(1)}, u32[]{:S(2)}, u32[]{:S(2)}) collective-permute-start(bf16[256,128]{1,0:T(8,128)(2,1)S(1)} %get-tuple-element.55), channel_id=1, source_target_pairs={{0,6},{2,8},{4,10},{6,12},{8,14},{10,16},{12,18},{14,20},{16,22},{... | collective-permute-start | bytes 196616 | tf_op jit(solution)/shard_map/ppermute | solution.py:781
  50.4 3.3 %collective-permute-start.3 = (bf16[256,128]{1,0:T(8,128)(2,1)S(1)}, bf16[256,128]{1,0:T(8,128)(2,1)S(1)}, u32[]{:S(2)}, u32[]{:S(2)}) collective-permute-start(bf16[256,128]{1,0:T(8,128)(2,1)S(1)} %get-tuple-element.56), channel_id=1, source_target_pairs={{0,4},{2,6},{4,8},{6,10},{8,12},{10,14},{12,16},{14,18},{16,20},{1... | collective-permute-start | bytes 196616 | tf_op jit(solution)/shard_map/ppermute | solution.py:781
  53.7 2.5 %collective-permute-start.2 = (bf16[256,128]{1,0:T(8,128)(2,1)S(1)}, bf16[256,128]{1,0:T(8,128)(2,1)S(1)}, u32[]{:S(2)}, u32[]{:S(2)}) collective-permute-start(bf16[256,128]{1,0:T(8,128)(2,1)S(1)} %get-tuple-element.57), channel_id=1, source_target_pairs={{0,2},{2,4},{4,6},{6,8},{8,10},{10,12},{12,14},{14,16},{16,18},{18... | collective-permute-start | bytes 196616 | tf_op jit(solution)/shard_map/ppermute | solution.py:781
  56.2 0.0 collective-permute-done.5
  56.2 0.0 collective-permute-done.4
  56.2 0.0 collective-permute-done.3
  56.2 2.5 %collective-permute-done.2 = bf16[256,128]{1,0:T(8,128)(2,1)S(1)} collective-permute-done((bf16[256,128]{1,0:T(8,128)(2,1)S(1)}, bf16[256,128]{1,0:T(8,128)(2,1)S(1)}, u32[]{:S(2)}, u32[]{:S(2)}) %collective-permute-start.2) | collective-permute-done | bytes 65568 | tf_op jit(solution)/shard_map/ppermute | solution.py:781
  58.7 6.2 %all-to-all-done.1.slots_ref.own_ref = bf16[16,184,128]{2,1,0:T(8,128)(2,1)S(1)} async-done(((bf16[16,184,128]{2,1,0:T(8,128)(2,1)}), bf16[16,184,128]{2,1,0:T(8,128)(2,1)S(1)}, u32[]{:S(2)}, u32[]{:S(2)}) %all-to-all-start.1) | async-done | bytes 753696 | tf_op jit(solution)/shard_map/all_to_all | solution.py:791
  64.9 1.0 %shard_map.97 = bf16[16,176,128]{2,1,0:T(8,128)(2,1)} custom-call(bf16[16,184,128]{2,1,0:T(8,128)(2,1)S(1)} %all-to-all-done.1.slots_ref.own_ref), custom_call_target="tpu_custom_call" | custom-call | bytes 4194304 | tf_op jit(solution)/shard_map/pallas_call | solution.py:52
  65.9 4.1 %all-to-all-start.2 = ((bf16[16,176,128]{2,1,0:T(8,128)(2,1)}), bf16[16,176,128]{2,1,0:T(8,128)(2,1)S(1)}, u32[]{:S(2)}, u32[]{:S(2)}) async-start(bf16[16,176,128]{2,1,0:T(8,128)(2,1)} %shard_map.97), calls=%async_computation.2 | async-start | bytes 1441792 | tf_op jit(solution)/shard_map/all_to_all | solution.py:791
  70.1 0.1 collective-permute-start.7
  70.2 0.5 collective-permute-start.6
  70.7 1.1 %collective-permute-done.6.other_ref = bf16[16,8,128]{2,1,0:T(8,128)(2,1)S(1)} collective-permute-done((bf16[16,8,128]{2,1,0:T(8,128)(2,1)S(1)}, bf16[16,8,128]{2,1,0:T(8,128)(2,1)S(1)}, u32[]{:S(2)}, u32[]{:S(2)}) %collective-permute-start.6) | collective-permute-done | bytes 32800 | tf_op jit(solution)/shard_map/ppermute | solution.py:785
  71.8 0.0 collective-permute-done.7.other_faces_ref
  71.8 9.2 %shard_map.99 = bf16[8,64,512]{2,1,0:T(8,128)(2,1)} custom-call(s32[1,26]{1,0:T(1,128)S(1)} %copy-done, s32[1]{0:T(128)} %bitcast.core_ref, s32[1]{0:T(128)} %bitcast.1.at_ref, bf16[16,184,128]{2,1,0:T(8,128)(2,1)S(1)} %all-to-all-done.1.slots_ref.own_ref, bf16[16,8,128]{2,1,0:T(8,128)(2,1)S(1)} %collective-permute-done.6.other_ref, ...), custom_call_target="tpu_custom_call" | custom-call | flops 5368709120 | bytes 4194304 | tf_op jit(solution)/shard_map/pallas_call | solution.py:52
  80.9 9.7 %all-to-all-done.2 = bf16[16,176,128]{2,1,0:T(8,128)(2,1)S(1)} async-done(((bf16[16,176,128]{2,1,0:T(8,128)(2,1)}), bf16[16,176,128]{2,1,0:T(8,128)(2,1)S(1)}, u32[]{:S(2)}, u32[]{:S(2)}) %all-to-all-start.2) | async-done | bytes 720928 | tf_op jit(solution)/shard_map/all_to_all | solution.py:791
  90.6 1.2 %shard_map.98 = (f32[27,64,128]{2,1,0:T(8,128)}, f32[8,128,128]{2,1,0:T(8,128)}) custom-call(s32[1]{0:T(128)} %bitcast.core_ref, bf16[2816,128]{1,0:T(8,128)(2,1)S(1)} %bitcast.19), custom_call_target="tpu_custom_call" | custom-call | bytes 4194304 | tf_op jit(solution)/shard_map/pallas_call | solution.py:52
  (3 shorter events, 0.1 us)
Async XLA Ops:
  3.1 8.3 %collective-permute-start = (bf16[8,64,512]{2,1,0:T(8,128)(2,1)}, bf16[8,64,512]{2,1,0:T(8,128)(2,1)S(1)}, u32[]{:S(2)}, u32[]{:S(2)}) collective-permute-start(bf16[8,64,512]{2,1,0:T(8,128)(2,1)} %bitcast.21), channel_id=1, source_target_pairs={{0,1},{1,0},{2,3},{3,2},{4,5},{5,4},{6,7},{7,6},{8,9},{9,8},{10,11... | collective-permute-start | bytes 1572872 | tf_op jit(solution)/shard_map/ppermute | solution.py:785
  3.6 24.6 %all-to-all-start = ((bf16[16,128,128]{2,1,0:T(8,128)(2,1)}), bf16[16,128,128]{2,1,0:T(8,128)(2,1)S(1)}, u32[]{:S(2)}, u32[]{:S(2)}) async-start(bf16[16,128,128]{2,1,0:T(8,128)(2,1)} %shard_map.93), calls=%async_computation | async-start | bytes 1048576 | tf_op jit(solution)/shard_map/all_to_all | solution.py:791
  23.0 7.2 %copy-start = (s32[1,26]{1,0:T(1,128)S(1)}, s32[1,26]{1,0:T(1,128)}, u32[]{:S(2)}) copy-start(s32[1,26]{1,0:T(1,128)} %near_ref.3) | copy-start | bytes 316
  28.3 1.9 %collective-permute-start.1 = (bf16[16,128,128]{2,1,0:T(8,128)(2,1)S(1)}, bf16[16,128,128]{2,1,0:T(8,128)(2,1)S(1)}, u32[]{:S(2)}, u32[]{:S(2)}) collective-permute-start(bf16[16,128,128]{2,1,0:T(8,128)(2,1)S(1)} %all-to-all-done.own_ref), channel_id=1, source_target_pairs={{0,1},{1,0},{2,3},{3,2},{4,5},{5,4},{6,7},{7,6},{8,9},{9,8},{10,11... | collective-permute-start | bytes 1572872 | tf_op jit(solution)/shard_map/ppermute | solution.py:785
  38.6 26.3 %all-to-all-start.1 = ((bf16[16,184,128]{2,1,0:T(8,128)(2,1)}), bf16[16,184,128]{2,1,0:T(8,128)(2,1)S(1)}, u32[]{:S(2)}, u32[]{:S(2)}) async-start(bf16[16,184,128]{2,1,0:T(8,128)(2,1)} %get-tuple-element.43), calls=%async_computation.1 | async-start | bytes 1507328 | tf_op jit(solution)/shard_map/all_to_all | solution.py:791
  42.3 13.9 %collective-permute-start.5 = (bf16[256,128]{1,0:T(8,128)(2,1)S(1)}, bf16[256,128]{1,0:T(8,128)(2,1)S(1)}, u32[]{:S(2)}, u32[]{:S(2)}) collective-permute-start(bf16[256,128]{1,0:T(8,128)(2,1)S(1)} %get-tuple-element.54), channel_id=1, source_target_pairs={{0,8},{2,10},{4,12},{6,14},{8,16},{10,18},{12,20},{14,22},{16,24},... | collective-permute-start | bytes 196616 | tf_op jit(solution)/shard_map/ppermute | solution.py:781
  46.0 10.2 %collective-permute-start.4 = (bf16[256,128]{1,0:T(8,128)(2,1)S(1)}, bf16[256,128]{1,0:T(8,128)(2,1)S(1)}, u32[]{:S(2)}, u32[]{:S(2)}) collective-permute-start(bf16[256,128]{1,0:T(8,128)(2,1)S(1)} %get-tuple-element.55), channel_id=1, source_target_pairs={{0,6},{2,8},{4,10},{6,12},{8,14},{10,16},{12,18},{14,20},{16,22},{... | collective-permute-start | bytes 196616 | tf_op jit(solution)/shard_map/ppermute | solution.py:781
  50.4 5.9 %collective-permute-start.3 = (bf16[256,128]{1,0:T(8,128)(2,1)S(1)}, bf16[256,128]{1,0:T(8,128)(2,1)S(1)}, u32[]{:S(2)}, u32[]{:S(2)}) collective-permute-start(bf16[256,128]{1,0:T(8,128)(2,1)S(1)} %get-tuple-element.56), channel_id=1, source_target_pairs={{0,4},{2,6},{4,8},{6,10},{8,12},{10,14},{12,16},{14,18},{16,20},{1... | collective-permute-start | bytes 196616 | tf_op jit(solution)/shard_map/ppermute | solution.py:781
  53.7 5.0 %collective-permute-start.2 = (bf16[256,128]{1,0:T(8,128)(2,1)S(1)}, bf16[256,128]{1,0:T(8,128)(2,1)S(1)}, u32[]{:S(2)}, u32[]{:S(2)}) collective-permute-start(bf16[256,128]{1,0:T(8,128)(2,1)S(1)} %get-tuple-element.57), channel_id=1, source_target_pairs={{0,2},{2,4},{4,6},{6,8},{8,10},{10,12},{12,14},{14,16},{16,18},{18... | collective-permute-start | bytes 196616 | tf_op jit(solution)/shard_map/ppermute | solution.py:781
  65.9 24.7 %all-to-all-start.2 = ((bf16[16,176,128]{2,1,0:T(8,128)(2,1)}), bf16[16,176,128]{2,1,0:T(8,128)(2,1)S(1)}, u32[]{:S(2)}, u32[]{:S(2)}) async-start(bf16[16,176,128]{2,1,0:T(8,128)(2,1)} %shard_map.97), calls=%async_computation.2 | async-start | bytes 1441792 | tf_op jit(solution)/shard_map/all_to_all | solution.py:791
  70.1 1.7 %collective-permute-start.7 = (bf16[4,256,128]{2,1,0:T(8,128)(2,1)S(1)}, bf16[4,256,128]{2,1,0:T(8,128)(2,1)S(1)}, u32[]{:S(2)}, u32[]{:S(2)}) collective-permute-start(bf16[4,256,128]{2,1,0:T(8,128)(2,1)S(1)} %pad_maximum_fusion.own_faces_ref), channel_id=1, source_target_pairs={{0,1},{1,0},{2,3},{3,2},{4,5},{5,4},{6,7},{7,6},{8,9},{9,8},{10,11... | collective-permute-start | bytes 786440 | tf_op jit(solution)/shard_map/ppermute | solution.py:785
  70.2 1.6 %collective-permute-start.6 = (bf16[16,8,128]{2,1,0:T(8,128)(2,1)S(1)}, bf16[16,8,128]{2,1,0:T(8,128)(2,1)S(1)}, u32[]{:S(2)}, u32[]{:S(2)}) collective-permute-start(bf16[16,8,128]{2,1,0:T(8,128)(2,1)S(1)} %slice.19), channel_id=1, source_target_pairs={{0,1},{1,0},{2,3},{3,2},{4,5},{5,4},{6,7},{7,6},{8,9},{9,8},{10,11... | collective-permute-start | bytes 98312 | tf_op jit(solution)/shard_map/ppermute | solution.py:785

commit v7 on v6

--- a/solution.py
+++ b/solution.py
@@ -82,7 +82,20 @@
 
 
 def slot_of(slots_ref, block):
-    return block % INNER * (slots_ref.shape[0] // INNER) + block // INNER
+    planes = slots_ref.shape[0] // INNER
+    column = block % INNER
+    column = column ^ (column >> 1)
+    plane = block // INNER
+    return column * planes + jnp.where(column % 2 == 0, plane, planes - 1 - plane)
+
+
+def block_order(devices):
+    planes = devices // INNER
+    order = []
+    for at, column in enumerate((0, 1, 3, 2)):
+        up = range(planes) if at % 2 == 0 else reversed(range(planes))
+        order += [plane * INNER + column for plane in up]
+    return order
 
 
 def fill_slots(rows_ref, near_ref, slots_ref, slots_hbm, left):
@@ -786,8 +799,7 @@
 
 
 def to_all(slots):
-    outer = lax.axis_size("space") // INNER
-    order = [plane * INNER + j for j in range(INNER) for plane in range(outer)]
+    order = block_order(lax.axis_size("space"))
     return lax.all_to_all(slots, "space", 0, 0, axis_index_groups=[order], tiled=True)
 
 

time: 92.4 us -> 89.7 us (0.971)
  waiting for transfers between devices: 24.7 us -> 19.5 us
  starting transfers between devices: 30.5 us -> 32.5 us
    all_to_all x3, waiting for transfers between devices: 21.2 us -> 16.5 us  [to_all(): lax.all_to_all(slots, 'space', 0, 0, axis_index_groups=[order], tiled=True)]
    all_to_all x3, starting transfers between devices: 15.5 us -> 17.5 us  [to_all(): lax.all_to_all(slots, 'space', 0, 0, axis_index_groups=[order], tiled=True)]
  transfers between devices with their start and end apart: 11 -> 11, of which waited for: 5 -> 5; matrix products, arithmetic and copies ran while one was open for 0% -> 0% of each run, Pallas kernels for 25% -> 26%
where the time goes in v7:
time: 89.7 us; the launch traced here: 89 us
  Pallas kernels  36.1 us (40%)
  starting transfers between devices  32.5 us (36%)
  waiting for transfers between devices  19.5 us (22%)
    pallas_call x7, Pallas kernels, run(): return call(*placed)  36.1 us
    all_to_all x3, starting transfers between devices, to_all(): lax.all_to_all(slots, 'space', 0, 0, axis_index_groups=[order], tiled=True)  17.5 us
    all_to_all x3, waiting for transfers between devices, to_all(): lax.all_to_all(slots, 'space', 0, 0, axis_index_groups=[order], tiled=True)  16.5 us
    ppermute x4, starting transfers between devices, over_space(): return lax.ppermute(block, ('space', 'chan'), route)  13.9 us
    ppermute x4, waiting for transfers between devices, over_space(): return lax.ppermute(block, ('space', 'chan'), route)  1.88 us
  transfers between devices with their start and end apart: 11, of which 5 were waited for; matrix products, arithmetic and copies ran while one was open for 0% of the time, Pallas kernels for 26%

profile of v7, /device:TPU:0, one launch (start us, length us, event | category | flops | bytes accessed | tf_op | source)
XLA Modules:
  0.0 89.0 jit_solution(4810636613875887325)
XLA Ops:
  0.6 2.6 %shard_map.93 = bf16[16,128,128]{2,1,0:T(8,128)(2,1)} custom-call(s32[1,26]{1,0:T(1,128)} %near_ref.3, s32[8,64]{1,0:T(8,128)} %heights_hbm.3, bf16[8,64,512]{2,1,0:T(8,128)(2,1)} %bitcast.20), custom_call_target="tpu_custom_call" | custom-call | bytes 4194304 | tf_op jit(solution)/shard_map/pallas_call | solution.py:52
  3.2 0.5 collective-permute-start
  3.7 7.6 %all-to-all-start = ((bf16[16,128,128]{2,1,0:T(8,128)(2,1)}), bf16[16,128,128]{2,1,0:T(8,128)(2,1)S(1)}, u32[]{:S(2)}, u32[]{:S(2)}) async-start(bf16[16,128,128]{2,1,0:T(8,128)(2,1)} %shard_map.93), calls=%async_computation | async-start | bytes 1048576 | tf_op jit(solution)/shard_map/all_to_all | solution.py:803
  11.3 0.0 collective-permute-done.other_hbm
  11.3 11.5 %shard_map.94 = (bf16[18,288,256]{2,1,0:T(8,128)(2,1)}, bf16[4096,128]{1,0:T(8,128)(2,1)}, f32[4096,128]{1,0:T(8,128)}, f32[4096,128]{1,0:T(8,128)}, bf16[3456,1...) custom-call(s32[1]{0:T(128)} %bitcast.core_ref, bf16[27,128,128]{2,1,0:T(8,128)(2,1)} %conv_hbm.3, ...), custom_call_target="tpu_custom_call" | custom-call | flops 5368709120 | bytes 4194304 | tf_op jit(solution)/shard_map/pallas_call | solution.py:52
  22.9 0.0 copy-start
  22.9 4.0 %all-to-all-done.own_ref = bf16[16,128,128]{2,1,0:T(8,128)(2,1)S(1)} async-done(((bf16[16,128,128]{2,1,0:T(8,128)(2,1)}), bf16[16,128,128]{2,1,0:T(8,128)(2,1)S(1)}, u32[]{:S(2)}, u32[]{:S(2)}) %all-to-all-start) | async-done | bytes 524320 | tf_op jit(solution)/shard_map/all_to_all | solution.py:803
  26.9 0.0 collective-permute-start.1
  26.9 1.9 %shard_map.95 = (bf16[3456,128]{1,0:T(8,128)(2,1)S(1)}, f32[4096,128]{1,0:T(8,128)S(1)}) custom-call(bf16[3456,128]{1,0:T(8,128)(2,1)} %get-tuple-element.34.taps_hbm, f32[4096,128]{1,0:T(8,128)} %get-tuple-element.35.inner_hbm), custom_call_target="tpu_custom_call" | custom-call | bytes 4194304 | tf_op jit(solution)/shard_map/pallas_call | solution.py:52
  28.8 0.0 collective-permute-done.1.other_ref
  28.8 0.0 copy-done
  28.8 8.5 %shard_map.96 = (bf16[16,184,128]{2,1,0:T(8,128)(2,1)}, bf16[4,256,128]{2,1,0:T(8,128)(2,1)S(1)}, bf16[512,128]{1,0:T(8,128)(2,1)}, bf16[4096,128]{1,0:T(8,128)(2,1)}) custom-call(s32[1,26]{1,0:T(1,128)S(1)} %copy-done, s32[1]{0:T(128)} %bitcast.core_ref, s32[1]{0:T(128)} %bitcast.1.at_ref, bf16[16,128,128]{2,1,0:T(8,128)(2,1)S(1)} %all-to-all-done.own_ref, ...), custom_call_target="tpu_custom_call" | custom-call | flops 5368709120 | bytes 4194304 | tf_op jit(solution)/shard_map/pallas_call | solution.py:52
  37.3 4.0 %all-to-all-start.1 = ((bf16[16,184,128]{2,1,0:T(8,128)(2,1)}), bf16[16,184,128]{2,1,0:T(8,128)(2,1)S(1)}, u32[]{:S(2)}, u32[]{:S(2)}) async-start(bf16[16,184,128]{2,1,0:T(8,128)(2,1)} %get-tuple-element.43), calls=%async_computation.1 | async-start | bytes 1507328 | tf_op jit(solution)/shard_map/all_to_all | solution.py:803
  41.3 3.8 %collective-permute-start.5 = (bf16[256,128]{1,0:T(8,128)(2,1)S(1)}, bf16[256,128]{1,0:T(8,128)(2,1)S(1)}, u32[]{:S(2)}, u32[]{:S(2)}) collective-permute-start(bf16[256,128]{1,0:T(8,128)(2,1)S(1)} %get-tuple-element.54), channel_id=1, source_target_pairs={{0,8},{2,10},{4,12},{6,14},{8,16},{10,18},{12,20},{14,22},{16,24},... | collective-permute-start | bytes 196616 | tf_op jit(solution)/shard_map/ppermute | solution.py:794
  45.1 4.3 %collective-permute-start.4 = (bf16[256,128]{1,0:T(8,128)(2,1)S(1)}, bf16[256,128]{1,0:T(8,128)(2,1)S(1)}, u32[]{:S(2)}, u32[]{:S(2)}) collective-permute-start(bf16[256,128]{1,0:T(8,128)(2,1)S(1)} %get-tuple-element.55), channel_id=1, source_target_pairs={{0,6},{2,8},{4,10},{6,12},{8,14},{10,16},{12,18},{14,20},{16,22},{... | collective-permute-start | bytes 196616 | tf_op jit(solution)/shard_map/ppermute | solution.py:794
  49.4 3.4 %collective-permute-start.3 = (bf16[256,128]{1,0:T(8,128)(2,1)S(1)}, bf16[256,128]{1,0:T(8,128)(2,1)S(1)}, u32[]{:S(2)}, u32[]{:S(2)}) collective-permute-start(bf16[256,128]{1,0:T(8,128)(2,1)S(1)} %get-tuple-element.56), channel_id=1, source_target_pairs={{0,4},{2,6},{4,8},{6,10},{8,12},{10,14},{12,16},{14,18},{16,20},{1... | collective-permute-start | bytes 196616 | tf_op jit(solution)/shard_map/ppermute | solution.py:794
  52.8 2.5 %collective-permute-start.2 = (bf16[256,128]{1,0:T(8,128)(2,1)S(1)}, bf16[256,128]{1,0:T(8,128)(2,1)S(1)}, u32[]{:S(2)}, u32[]{:S(2)}) collective-permute-start(bf16[256,128]{1,0:T(8,128)(2,1)S(1)} %get-tuple-element.57), channel_id=1, source_target_pairs={{0,2},{2,4},{4,6},{6,8},{8,10},{10,12},{12,14},{14,16},{16,18},{18... | collective-permute-start | bytes 196616 | tf_op jit(solution)/shard_map/ppermute | solution.py:794
  55.3 0.0 collective-permute-done.5
  55.3 0.0 collective-permute-done.4
  55.3 0.0 collective-permute-done.3
  55.3 1.9 %collective-permute-done.2 = bf16[256,128]{1,0:T(8,128)(2,1)S(1)} collective-permute-done((bf16[256,128]{1,0:T(8,128)(2,1)S(1)}, bf16[256,128]{1,0:T(8,128)(2,1)S(1)}, u32[]{:S(2)}, u32[]{:S(2)}) %collective-permute-start.2) | collective-permute-done | bytes 65568 | tf_op jit(solution)/shard_map/ppermute | solution.py:794
  57.2 4.7 %all-to-all-done.1.slots_ref.own_ref = bf16[16,184,128]{2,1,0:T(8,128)(2,1)S(1)} async-done(((bf16[16,184,128]{2,1,0:T(8,128)(2,1)}), bf16[16,184,128]{2,1,0:T(8,128)(2,1)S(1)}, u32[]{:S(2)}, u32[]{:S(2)}) %all-to-all-start.1) | async-done | bytes 753696 | tf_op jit(solution)/shard_map/all_to_all | solution.py:803
  61.9 1.0 %shard_map.97 = bf16[16,176,128]{2,1,0:T(8,128)(2,1)} custom-call(bf16[16,184,128]{2,1,0:T(8,128)(2,1)S(1)} %all-to-all-done.1.slots_ref.own_ref), custom_call_target="tpu_custom_call" | custom-call | bytes 4194304 | tf_op jit(solution)/shard_map/pallas_call | solution.py:52
  62.8 6.0 %all-to-all-start.2 = ((bf16[16,176,128]{2,1,0:T(8,128)(2,1)}), bf16[16,176,128]{2,1,0:T(8,128)(2,1)S(1)}, u32[]{:S(2)}, u32[]{:S(2)}) async-start(bf16[16,176,128]{2,1,0:T(8,128)(2,1)} %shard_map.97), calls=%async_computation.2 | async-start | bytes 1441792 | tf_op jit(solution)/shard_map/all_to_all | solution.py:803
  68.8 0.1 collective-permute-start.7
  68.9 0.5 collective-permute-start.6
  69.4 1.1 %collective-permute-done.6.other_ref = bf16[16,8,128]{2,1,0:T(8,128)(2,1)S(1)} collective-permute-done((bf16[16,8,128]{2,1,0:T(8,128)(2,1)S(1)}, bf16[16,8,128]{2,1,0:T(8,128)(2,1)S(1)}, u32[]{:S(2)}, u32[]{:S(2)}) %collective-permute-start.6) | collective-permute-done | bytes 32800 | tf_op jit(solution)/shard_map/ppermute | solution.py:798
  70.5 0.0 collective-permute-done.7.other_faces_ref
  70.5 9.4 %shard_map.99 = bf16[8,64,512]{2,1,0:T(8,128)(2,1)} custom-call(s32[1,26]{1,0:T(1,128)S(1)} %copy-done, s32[1]{0:T(128)} %bitcast.core_ref, s32[1]{0:T(128)} %bitcast.1.at_ref, bf16[16,184,128]{2,1,0:T(8,128)(2,1)S(1)} %all-to-all-done.1.slots_ref.own_ref, bf16[16,8,128]{2,1,0:T(8,128)(2,1)S(1)} %collective-permute-done.6.other_ref, ...), custom_call_target="tpu_custom_call" | custom-call | flops 5368709120 | bytes 4194304 | tf_op jit(solution)/shard_map/pallas_call | solution.py:52
  79.9 7.9 %all-to-all-done.2 = bf16[16,176,128]{2,1,0:T(8,128)(2,1)S(1)} async-done(((bf16[16,176,128]{2,1,0:T(8,128)(2,1)}), bf16[16,176,128]{2,1,0:T(8,128)(2,1)S(1)}, u32[]{:S(2)}, u32[]{:S(2)}) %all-to-all-start.2) | async-done | bytes 720928 | tf_op jit(solution)/shard_map/all_to_all | solution.py:803
  87.8 1.2 %shard_map.98 = (f32[27,64,128]{2,1,0:T(8,128)}, f32[8,128,128]{2,1,0:T(8,128)}) custom-call(s32[1]{0:T(128)} %bitcast.core_ref, bf16[2816,128]{1,0:T(8,128)(2,1)S(1)} %bitcast.19), custom_call_target="tpu_custom_call" | custom-call | bytes 4194304 | tf_op jit(solution)/shard_map/pallas_call | solution.py:52
  (3 shorter events, 0.1 us)
Async XLA Ops:
  3.2 8.1 %collective-permute-start = (bf16[8,64,512]{2,1,0:T(8,128)(2,1)}, bf16[8,64,512]{2,1,0:T(8,128)(2,1)S(1)}, u32[]{:S(2)}, u32[]{:S(2)}) collective-permute-start(bf16[8,64,512]{2,1,0:T(8,128)(2,1)} %bitcast.21), channel_id=1, source_target_pairs={{0,1},{1,0},{2,3},{3,2},{4,5},{5,4},{6,7},{7,6},{8,9},{9,8},{10,11... | collective-permute-start | bytes 1572872 | tf_op jit(solution)/shard_map/ppermute | solution.py:798
  3.7 23.2 %all-to-all-start = ((bf16[16,128,128]{2,1,0:T(8,128)(2,1)}), bf16[16,128,128]{2,1,0:T(8,128)(2,1)S(1)}, u32[]{:S(2)}, u32[]{:S(2)}) async-start(bf16[16,128,128]{2,1,0:T(8,128)(2,1)} %shard_map.93), calls=%async_computation | async-start | bytes 1048576 | tf_op jit(solution)/shard_map/all_to_all | solution.py:803
  22.9 5.9 %copy-start = (s32[1,26]{1,0:T(1,128)S(1)}, s32[1,26]{1,0:T(1,128)}, u32[]{:S(2)}) copy-start(s32[1,26]{1,0:T(1,128)} %near_ref.3) | copy-start | bytes 316
  26.9 1.9 %collective-permute-start.1 = (bf16[16,128,128]{2,1,0:T(8,128)(2,1)S(1)}, bf16[16,128,128]{2,1,0:T(8,128)(2,1)S(1)}, u32[]{:S(2)}, u32[]{:S(2)}) collective-permute-start(bf16[16,128,128]{2,1,0:T(8,128)(2,1)S(1)} %all-to-all-done.own_ref), channel_id=1, source_target_pairs={{0,1},{1,0},{2,3},{3,2},{4,5},{5,4},{6,7},{7,6},{8,9},{9,8},{10,11... | collective-permute-start | bytes 1572872 | tf_op jit(solution)/shard_map/ppermute | solution.py:798
  37.3 24.6 %all-to-all-start.1 = ((bf16[16,184,128]{2,1,0:T(8,128)(2,1)}), bf16[16,184,128]{2,1,0:T(8,128)(2,1)S(1)}, u32[]{:S(2)}, u32[]{:S(2)}) async-start(bf16[16,184,128]{2,1,0:T(8,128)(2,1)} %get-tuple-element.43), calls=%async_computation.1 | async-start | bytes 1507328 | tf_op jit(solution)/shard_map/all_to_all | solution.py:803
  41.3 14.0 %collective-permute-start.5 = (bf16[256,128]{1,0:T(8,128)(2,1)S(1)}, bf16[256,128]{1,0:T(8,128)(2,1)S(1)}, u32[]{:S(2)}, u32[]{:S(2)}) collective-permute-start(bf16[256,128]{1,0:T(8,128)(2,1)S(1)} %get-tuple-element.54), channel_id=1, source_target_pairs={{0,8},{2,10},{4,12},{6,14},{8,16},{10,18},{12,20},{14,22},{16,24},... | collective-permute-start | bytes 196616 | tf_op jit(solution)/shard_map/ppermute | solution.py:794
  45.1 10.2 %collective-permute-start.4 = (bf16[256,128]{1,0:T(8,128)(2,1)S(1)}, bf16[256,128]{1,0:T(8,128)(2,1)S(1)}, u32[]{:S(2)}, u32[]{:S(2)}) collective-permute-start(bf16[256,128]{1,0:T(8,128)(2,1)S(1)} %get-tuple-element.55), channel_id=1, source_target_pairs={{0,6},{2,8},{4,10},{6,12},{8,14},{10,16},{12,18},{14,20},{16,22},{... | collective-permute-start | bytes 196616 | tf_op jit(solution)/shard_map/ppermute | solution.py:794
  49.4 5.9 %collective-permute-start.3 = (bf16[256,128]{1,0:T(8,128)(2,1)S(1)}, bf16[256,128]{1,0:T(8,128)(2,1)S(1)}, u32[]{:S(2)}, u32[]{:S(2)}) collective-permute-start(bf16[256,128]{1,0:T(8,128)(2,1)S(1)} %get-tuple-element.56), channel_id=1, source_target_pairs={{0,4},{2,6},{4,8},{6,10},{8,12},{10,14},{12,16},{14,18},{16,20},{1... | collective-permute-start | bytes 196616 | tf_op jit(solution)/shard_map/ppermute | solution.py:794
  52.8 4.4 %collective-permute-start.2 = (bf16[256,128]{1,0:T(8,128)(2,1)S(1)}, bf16[256,128]{1,0:T(8,128)(2,1)S(1)}, u32[]{:S(2)}, u32[]{:S(2)}) collective-permute-start(bf16[256,128]{1,0:T(8,128)(2,1)S(1)} %get-tuple-element.57), channel_id=1, source_target_pairs={{0,2},{2,4},{4,6},{6,8},{8,10},{10,12},{12,14},{14,16},{16,18},{18... | collective-permute-start | bytes 196616 | tf_op jit(solution)/shard_map/ppermute | solution.py:794
  62.8 25.0 %all-to-all-start.2 = ((bf16[16,176,128]{2,1,0:T(8,128)(2,1)}), bf16[16,176,128]{2,1,0:T(8,128)(2,1)S(1)}, u32[]{:S(2)}, u32[]{:S(2)}) async-start(bf16[16,176,128]{2,1,0:T(8,128)(2,1)} %shard_map.97), calls=%async_computation.2 | async-start | bytes 1441792 | tf_op jit(solution)/shard_map/all_to_all | solution.py:803
  68.8 1.7 %collective-permute-start.7 = (bf16[4,256,128]{2,1,0:T(8,128)(2,1)S(1)}, bf16[4,256,128]{2,1,0:T(8,128)(2,1)S(1)}, u32[]{:S(2)}, u32[]{:S(2)}) collective-permute-start(bf16[4,256,128]{2,1,0:T(8,128)(2,1)S(1)} %pad_maximum_fusion.own_faces_ref), channel_id=1, source_target_pairs={{0,1},{1,0},{2,3},{3,2},{4,5},{5,4},{6,7},{7,6},{8,9},{9,8},{10,11... | collective-permute-start | bytes 786440 | tf_op jit(solution)/shard_map/ppermute | solution.py:798
  68.9 1.6 %collective-permute-start.6 = (bf16[16,8,128]{2,1,0:T(8,128)(2,1)S(1)}, bf16[16,8,128]{2,1,0:T(8,128)(2,1)S(1)}, u32[]{:S(2)}, u32[]{:S(2)}) collective-permute-start(bf16[16,8,128]{2,1,0:T(8,128)(2,1)S(1)} %slice.19), channel_id=1, source_target_pairs={{0,1},{1,0},{2,3},{3,2},{4,5},{5,4},{6,7},{7,6},{8,9},{9,8},{10,11... | collective-permute-start | bytes 98312 | tf_op jit(solution)/shard_map/ppermute | solution.py:798

commit v8 on v7

--- a/solution.py
+++ b/solution.py
@@ -86,14 +86,14 @@
     column = block % INNER
     column = column ^ (column >> 1)
     plane = block // INNER
-    return column * planes + jnp.where(column % 2 == 0, plane, planes - 1 - plane)
+    return column * planes + jnp.where(column % 2 == 0, planes - 1 - plane, plane)
 
 
 def block_order(devices):
     planes = devices // INNER
     order = []
     for at, column in enumerate((0, 1, 3, 2)):
-        up = range(planes) if at % 2 == 0 else reversed(range(planes))
+        up = range(planes) if at % 2 else reversed(range(planes))
         order += [plane * INNER + column for plane in up]
     return order
 

time: 89.7 us -> 88.3 us (0.984)
  waiting for transfers between devices: 19.5 us -> 14.5 us
  starting transfers between devices: 32.5 us -> 36.6 us
    all_to_all x3, starting transfers between devices: 17.5 us -> 23.9 us  [to_all(): lax.all_to_all(slots, 'space', 0, 0, axis_index_groups=[order], tiled=True)]
    all_to_all x3, waiting for transfers between devices: 16.5 us -> 11 us  [to_all(): lax.all_to_all(slots, 'space', 0, 0, axis_index_groups=[order], tiled=True)]
    ppermute x4, starting transfers between devices: 13.9 us -> 11.7 us  [over_space(): return lax.ppermute(block, ('space', 'chan'), route)]
  transfers between devices with their start and end apart: 11 -> 11, of which waited for: 5 -> 6; matrix products, arithmetic and copies ran while one was open for 0% -> 0% of each run, Pallas kernels for 26% -> 26%
where the time goes in v8:
time: 88.3 us; the launch traced here: 87.5 us
  starting transfers between devices  36.6 us (41%)
  Pallas kernels  35.6 us (40%)
  waiting for transfers between devices  14.5 us (16%)
    pallas_call x7, Pallas kernels, run(): return call(*placed)  35.6 us
    all_to_all x3, starting transfers between devices, to_all(): lax.all_to_all(slots, 'space', 0, 0, axis_index_groups=[order], tiled=True)  23.9 us
    ppermute x4, starting transfers between devices, over_space(): return lax.ppermute(block, ('space', 'chan'), route)  11.7 us
    all_to_all x3, waiting for transfers between devices, to_all(): lax.all_to_all(slots, 'space', 0, 0, axis_index_groups=[order], tiled=True)  11 us
    ppermute x4, waiting for transfers between devices, over_space(): return lax.ppermute(block, ('space', 'chan'), route)  2.37 us
  transfers between devices with their start and end apart: 11, of which 6 were waited for; matrix products, arithmetic and copies ran while one was open for 0% of the time, Pallas kernels for 26%

profile of v8, /device:TPU:0, one launch (start us, length us, event | category | flops | bytes accessed | tf_op | source)
XLA Modules:
  0.0 87.5 jit_solution(10818252844958076828)
XLA Ops:
  0.6 2.5 %shard_map.93 = bf16[16,128,128]{2,1,0:T(8,128)(2,1)} custom-call(s32[1,26]{1,0:T(1,128)} %near_ref.3, s32[8,64]{1,0:T(8,128)} %heights_hbm.3, bf16[8,64,512]{2,1,0:T(8,128)(2,1)} %bitcast.20), custom_call_target="tpu_custom_call" | custom-call | bytes 4194304 | tf_op jit(solution)/shard_map/pallas_call | solution.py:52
  3.1 0.5 collective-permute-start
  3.6 8.3 %all-to-all-start = ((bf16[16,128,128]{2,1,0:T(8,128)(2,1)}), bf16[16,128,128]{2,1,0:T(8,128)(2,1)S(1)}, u32[]{:S(2)}, u32[]{:S(2)}) async-start(bf16[16,128,128]{2,1,0:T(8,128)(2,1)} %shard_map.93), calls=%async_computation | async-start | bytes 1048576 | tf_op jit(solution)/shard_map/all_to_all | solution.py:803
  12.0 0.0 collective-permute-done.other_hbm
  12.0 11.5 %shard_map.94 = (bf16[18,288,256]{2,1,0:T(8,128)(2,1)}, bf16[4096,128]{1,0:T(8,128)(2,1)}, f32[4096,128]{1,0:T(8,128)}, f32[4096,128]{1,0:T(8,128)}, bf16[3456,1...) custom-call(s32[1]{0:T(128)} %bitcast.core_ref, bf16[27,128,128]{2,1,0:T(8,128)(2,1)} %conv_hbm.3, ...), custom_call_target="tpu_custom_call" | custom-call | flops 5368709120 | bytes 4194304 | tf_op jit(solution)/shard_map/pallas_call | solution.py:52
  23.5 0.0 copy-start
  23.5 1.6 %all-to-all-done.own_ref = bf16[16,128,128]{2,1,0:T(8,128)(2,1)S(1)} async-done(((bf16[16,128,128]{2,1,0:T(8,128)(2,1)}), bf16[16,128,128]{2,1,0:T(8,128)(2,1)S(1)}, u32[]{:S(2)}, u32[]{:S(2)}) %all-to-all-start) | async-done | bytes 524320 | tf_op jit(solution)/shard_map/all_to_all | solution.py:803
  25.1 0.0 collective-permute-start.1
  25.1 1.9 %shard_map.95 = (bf16[3456,128]{1,0:T(8,128)(2,1)S(1)}, f32[4096,128]{1,0:T(8,128)S(1)}) custom-call(bf16[3456,128]{1,0:T(8,128)(2,1)} %get-tuple-element.34.taps_hbm, f32[4096,128]{1,0:T(8,128)} %get-tuple-element.35.inner_hbm), custom_call_target="tpu_custom_call" | custom-call | bytes 4194304 | tf_op jit(solution)/shard_map/pallas_call | solution.py:52
  27.0 0.0 collective-permute-done.1.other_ref
  27.0 0.0 copy-done
  27.0 8.4 %shard_map.96 = (bf16[16,184,128]{2,1,0:T(8,128)(2,1)}, bf16[4,256,128]{2,1,0:T(8,128)(2,1)S(1)}, bf16[512,128]{1,0:T(8,128)(2,1)}, bf16[4096,128]{1,0:T(8,128)(2,1)}) custom-call(s32[1,26]{1,0:T(1,128)S(1)} %copy-done, s32[1]{0:T(128)} %bitcast.core_ref, s32[1]{0:T(128)} %bitcast.1.at_ref, bf16[16,128,128]{2,1,0:T(8,128)(2,1)S(1)} %all-to-all-done.own_ref, ...), custom_call_target="tpu_custom_call" | custom-call | flops 5368709120 | bytes 4194304 | tf_op jit(solution)/shard_map/pallas_call | solution.py:52
  35.4 6.7 %all-to-all-start.1 = ((bf16[16,184,128]{2,1,0:T(8,128)(2,1)}), bf16[16,184,128]{2,1,0:T(8,128)(2,1)S(1)}, u32[]{:S(2)}, u32[]{:S(2)}) async-start(bf16[16,184,128]{2,1,0:T(8,128)(2,1)} %get-tuple-element.43), calls=%async_computation.1 | async-start | bytes 1507328 | tf_op jit(solution)/shard_map/all_to_all | solution.py:803
  42.1 2.5 %collective-permute-start.5 = (bf16[256,128]{1,0:T(8,128)(2,1)S(1)}, bf16[256,128]{1,0:T(8,128)(2,1)S(1)}, u32[]{:S(2)}, u32[]{:S(2)}) collective-permute-start(bf16[256,128]{1,0:T(8,128)(2,1)S(1)} %get-tuple-element.54), channel_id=1, source_target_pairs={{0,8},{2,10},{4,12},{6,14},{8,16},{10,18},{12,20},{14,22},{16,24},... | collective-permute-start | bytes 196616 | tf_op jit(solution)/shard_map/ppermute | solution.py:794
  44.5 4.3 %collective-permute-start.4 = (bf16[256,128]{1,0:T(8,128)(2,1)S(1)}, bf16[256,128]{1,0:T(8,128)(2,1)S(1)}, u32[]{:S(2)}, u32[]{:S(2)}) collective-permute-start(bf16[256,128]{1,0:T(8,128)(2,1)S(1)} %get-tuple-element.55), channel_id=1, source_target_pairs={{0,6},{2,8},{4,10},{6,12},{8,14},{10,16},{12,18},{14,20},{16,22},{... | collective-permute-start | bytes 196616 | tf_op jit(solution)/shard_map/ppermute | solution.py:794
  48.8 2.5 %collective-permute-start.3 = (bf16[256,128]{1,0:T(8,128)(2,1)S(1)}, bf16[256,128]{1,0:T(8,128)(2,1)S(1)}, u32[]{:S(2)}, u32[]{:S(2)}) collective-permute-start(bf16[256,128]{1,0:T(8,128)(2,1)S(1)} %get-tuple-element.56), channel_id=1, source_target_pairs={{0,4},{2,6},{4,8},{6,10},{8,12},{10,14},{12,16},{14,18},{16,20},{1... | collective-permute-start | bytes 196616 | tf_op jit(solution)/shard_map/ppermute | solution.py:794
  51.3 2.5 %collective-permute-start.2 = (bf16[256,128]{1,0:T(8,128)(2,1)S(1)}, bf16[256,128]{1,0:T(8,128)(2,1)S(1)}, u32[]{:S(2)}, u32[]{:S(2)}) collective-permute-start(bf16[256,128]{1,0:T(8,128)(2,1)S(1)} %get-tuple-element.57), channel_id=1, source_target_pairs={{0,2},{2,4},{4,6},{6,8},{8,10},{10,12},{12,14},{14,16},{16,18},{18... | collective-permute-start | bytes 196616 | tf_op jit(solution)/shard_map/ppermute | solution.py:794
  53.8 1.6 %collective-permute-done.5 = bf16[256,128]{1,0:T(8,128)(2,1)S(1)} collective-permute-done((bf16[256,128]{1,0:T(8,128)(2,1)S(1)}, bf16[256,128]{1,0:T(8,128)(2,1)S(1)}, u32[]{:S(2)}, u32[]{:S(2)}) %collective-permute-start.5) | collective-permute-done | bytes 65568 | tf_op jit(solution)/shard_map/ppermute | solution.py:794
  55.4 0.0 collective-permute-done.4
  55.4 0.0 collective-permute-done.3
  55.4 0.7 collective-permute-done.2
  56.2 3.5 %all-to-all-done.1.slots_ref.own_ref = bf16[16,184,128]{2,1,0:T(8,128)(2,1)S(1)} async-done(((bf16[16,184,128]{2,1,0:T(8,128)(2,1)}), bf16[16,184,128]{2,1,0:T(8,128)(2,1)S(1)}, u32[]{:S(2)}, u32[]{:S(2)}) %all-to-all-start.1) | async-done | bytes 753696 | tf_op jit(solution)/shard_map/all_to_all | solution.py:803
  59.7 1.0 %shard_map.97 = bf16[16,176,128]{2,1,0:T(8,128)(2,1)} custom-call(bf16[16,184,128]{2,1,0:T(8,128)(2,1)S(1)} %all-to-all-done.1.slots_ref.own_ref), custom_call_target="tpu_custom_call" | custom-call | bytes 4194304 | tf_op jit(solution)/shard_map/pallas_call | solution.py:52
  60.7 8.9 %all-to-all-start.2 = ((bf16[16,176,128]{2,1,0:T(8,128)(2,1)}), bf16[16,176,128]{2,1,0:T(8,128)(2,1)S(1)}, u32[]{:S(2)}, u32[]{:S(2)}) async-start(bf16[16,176,128]{2,1,0:T(8,128)(2,1)} %shard_map.97), calls=%async_computation.2 | async-start | bytes 1441792 | tf_op jit(solution)/shard_map/all_to_all | solution.py:803
  69.6 0.1 collective-permute-start.7
  69.7 0.5 collective-permute-start.6
  70.2 1.1 %collective-permute-done.6.other_ref = bf16[16,8,128]{2,1,0:T(8,128)(2,1)S(1)} collective-permute-done((bf16[16,8,128]{2,1,0:T(8,128)(2,1)S(1)}, bf16[16,8,128]{2,1,0:T(8,128)(2,1)S(1)}, u32[]{:S(2)}, u32[]{:S(2)}) %collective-permute-start.6) | collective-permute-done | bytes 32800 | tf_op jit(solution)/shard_map/ppermute | solution.py:798
  71.2 0.0 collective-permute-done.7.other_faces_ref
  71.2 9.1 %shard_map.99 = bf16[8,64,512]{2,1,0:T(8,128)(2,1)} custom-call(s32[1,26]{1,0:T(1,128)S(1)} %copy-done, s32[1]{0:T(128)} %bitcast.core_ref, s32[1]{0:T(128)} %bitcast.1.at_ref, bf16[16,184,128]{2,1,0:T(8,128)(2,1)S(1)} %all-to-all-done.1.slots_ref.own_ref, bf16[16,8,128]{2,1,0:T(8,128)(2,1)S(1)} %collective-permute-done.6.other_ref, ...), custom_call_target="tpu_custom_call" | custom-call | flops 5368709120 | bytes 4194304 | tf_op jit(solution)/shard_map/pallas_call | solution.py:52
  80.4 5.9 %all-to-all-done.2 = bf16[16,176,128]{2,1,0:T(8,128)(2,1)S(1)} async-done(((bf16[16,176,128]{2,1,0:T(8,128)(2,1)}), bf16[16,176,128]{2,1,0:T(8,128)(2,1)S(1)}, u32[]{:S(2)}, u32[]{:S(2)}) %all-to-all-start.2) | async-done | bytes 720928 | tf_op jit(solution)/shard_map/all_to_all | solution.py:803
  86.3 1.2 %shard_map.98 = (f32[27,64,128]{2,1,0:T(8,128)}, f32[8,128,128]{2,1,0:T(8,128)}) custom-call(s32[1]{0:T(128)} %bitcast.core_ref, bf16[2816,128]{1,0:T(8,128)(2,1)S(1)} %bitcast.19), custom_call_target="tpu_custom_call" | custom-call | bytes 4194304 | tf_op jit(solution)/shard_map/pallas_call | solution.py:52
  (3 shorter events, 0.1 us)
Async XLA Ops:
  3.1 8.8 %collective-permute-start = (bf16[8,64,512]{2,1,0:T(8,128)(2,1)}, bf16[8,64,512]{2,1,0:T(8,128)(2,1)S(1)}, u32[]{:S(2)}, u32[]{:S(2)}) collective-permute-start(bf16[8,64,512]{2,1,0:T(8,128)(2,1)} %bitcast.21), channel_id=1, source_target_pairs={{0,1},{1,0},{2,3},{3,2},{4,5},{5,4},{6,7},{7,6},{8,9},{9,8},{10,11... | collective-permute-start | bytes 1572872 | tf_op jit(solution)/shard_map/ppermute | solution.py:798
  3.6 21.5 %all-to-all-start = ((bf16[16,128,128]{2,1,0:T(8,128)(2,1)}), bf16[16,128,128]{2,1,0:T(8,128)(2,1)S(1)}, u32[]{:S(2)}, u32[]{:S(2)}) async-start(bf16[16,128,128]{2,1,0:T(8,128)(2,1)} %shard_map.93), calls=%async_computation | async-start | bytes 1048576 | tf_op jit(solution)/shard_map/all_to_all | solution.py:803
  23.5 3.5 %copy-start = (s32[1,26]{1,0:T(1,128)S(1)}, s32[1,26]{1,0:T(1,128)}, u32[]{:S(2)}) copy-start(s32[1,26]{1,0:T(1,128)} %near_ref.3) | copy-start | bytes 316
  25.1 1.9 %collective-permute-start.1 = (bf16[16,128,128]{2,1,0:T(8,128)(2,1)S(1)}, bf16[16,128,128]{2,1,0:T(8,128)(2,1)S(1)}, u32[]{:S(2)}, u32[]{:S(2)}) collective-permute-start(bf16[16,128,128]{2,1,0:T(8,128)(2,1)S(1)} %all-to-all-done.own_ref), channel_id=1, source_target_pairs={{0,1},{1,0},{2,3},{3,2},{4,5},{5,4},{6,7},{7,6},{8,9},{9,8},{10,11... | collective-permute-start | bytes 1572872 | tf_op jit(solution)/shard_map/ppermute | solution.py:798
  35.4 24.3 %all-to-all-start.1 = ((bf16[16,184,128]{2,1,0:T(8,128)(2,1)}), bf16[16,184,128]{2,1,0:T(8,128)(2,1)S(1)}, u32[]{:S(2)}, u32[]{:S(2)}) async-start(bf16[16,184,128]{2,1,0:T(8,128)(2,1)} %get-tuple-element.43), calls=%async_computation.1 | async-start | bytes 1507328 | tf_op jit(solution)/shard_map/all_to_all | solution.py:803
  42.1 13.4 %collective-permute-start.5 = (bf16[256,128]{1,0:T(8,128)(2,1)S(1)}, bf16[256,128]{1,0:T(8,128)(2,1)S(1)}, u32[]{:S(2)}, u32[]{:S(2)}) collective-permute-start(bf16[256,128]{1,0:T(8,128)(2,1)S(1)} %get-tuple-element.54), channel_id=1, source_target_pairs={{0,8},{2,10},{4,12},{6,14},{8,16},{10,18},{12,20},{14,22},{16,24},... | collective-permute-start | bytes 196616 | tf_op jit(solution)/shard_map/ppermute | solution.py:794
  44.5 10.9 %collective-permute-start.4 = (bf16[256,128]{1,0:T(8,128)(2,1)S(1)}, bf16[256,128]{1,0:T(8,128)(2,1)S(1)}, u32[]{:S(2)}, u32[]{:S(2)}) collective-permute-start(bf16[256,128]{1,0:T(8,128)(2,1)S(1)} %get-tuple-element.55), channel_id=1, source_target_pairs={{0,6},{2,8},{4,10},{6,12},{8,14},{10,16},{12,18},{14,20},{16,22},{... | collective-permute-start | bytes 196616 | tf_op jit(solution)/shard_map/ppermute | solution.py:794
  48.8 6.6 %collective-permute-start.3 = (bf16[256,128]{1,0:T(8,128)(2,1)S(1)}, bf16[256,128]{1,0:T(8,128)(2,1)S(1)}, u32[]{:S(2)}, u32[]{:S(2)}) collective-permute-start(bf16[256,128]{1,0:T(8,128)(2,1)S(1)} %get-tuple-element.56), channel_id=1, source_target_pairs={{0,4},{2,6},{4,8},{6,10},{8,12},{10,14},{12,16},{14,18},{16,20},{1... | collective-permute-start | bytes 196616 | tf_op jit(solution)/shard_map/ppermute | solution.py:794
  51.3 4.9 %collective-permute-start.2 = (bf16[256,128]{1,0:T(8,128)(2,1)S(1)}, bf16[256,128]{1,0:T(8,128)(2,1)S(1)}, u32[]{:S(2)}, u32[]{:S(2)}) collective-permute-start(bf16[256,128]{1,0:T(8,128)(2,1)S(1)} %get-tuple-element.57), channel_id=1, source_target_pairs={{0,2},{2,4},{4,6},{6,8},{8,10},{10,12},{12,14},{14,16},{16,18},{18... | collective-permute-start | bytes 196616 | tf_op jit(solution)/shard_map/ppermute | solution.py:794
  60.7 25.6 %all-to-all-start.2 = ((bf16[16,176,128]{2,1,0:T(8,128)(2,1)}), bf16[16,176,128]{2,1,0:T(8,128)(2,1)S(1)}, u32[]{:S(2)}, u32[]{:S(2)}) async-start(bf16[16,176,128]{2,1,0:T(8,128)(2,1)} %shard_map.97), calls=%async_computation.2 | async-start | bytes 1441792 | tf_op jit(solution)/shard_map/all_to_all | solution.py:803
  69.6 1.7 %collective-permute-start.7 = (bf16[4,256,128]{2,1,0:T(8,128)(2,1)S(1)}, bf16[4,256,128]{2,1,0:T(8,128)(2,1)S(1)}, u32[]{:S(2)}, u32[]{:S(2)}) collective-permute-start(bf16[4,256,128]{2,1,0:T(8,128)(2,1)S(1)} %pad_maximum_fusion.own_faces_ref), channel_id=1, source_target_pairs={{0,1},{1,0},{2,3},{3,2},{4,5},{5,4},{6,7},{7,6},{8,9},{9,8},{10,11... | collective-permute-start | bytes 786440 | tf_op jit(solution)/shard_map/ppermute | solution.py:798
  69.7 1.6 %collective-permute-start.6 = (bf16[16,8,128]{2,1,0:T(8,128)(2,1)S(1)}, bf16[16,8,128]{2,1,0:T(8,128)(2,1)S(1)}, u32[]{:S(2)}, u32[]{:S(2)}) collective-permute-start(bf16[16,8,128]{2,1,0:T(8,128)(2,1)S(1)} %slice.19), channel_id=1, source_target_pairs={{0,1},{1,0},{2,3},{3,2},{4,5},{5,4},{6,7},{7,6},{8,9},{9,8},{10,11... | collective-permute-start | bytes 98312 | tf_op jit(solution)/shard_map/ppermute | solution.py:798

commit v9 on v8

--- a/solution.py
+++ b/solution.py
@@ -84,7 +84,7 @@
 def slot_of(slots_ref, block):
     planes = slots_ref.shape[0] // INNER
     column = block % INNER
-    column = column ^ (column >> 1)
+    column = ((column ^ (column >> 1)) + 2) % INNER
     plane = block // INNER
     return column * planes + jnp.where(column % 2 == 0, planes - 1 - plane, plane)
 
@@ -92,7 +92,7 @@
 def block_order(devices):
     planes = devices // INNER
     order = []
-    for at, column in enumerate((0, 1, 3, 2)):
+    for at, column in enumerate((3, 2, 0, 1)):
         up = range(planes) if at % 2 else reversed(range(planes))
         order += [plane * INNER + column for plane in up]
     return order

time: 88.3 us -> 89.5 us (1.014)
    all_to_all x3, starting transfers between devices: 23.9 us -> 25.3 us  [to_all(): lax.all_to_all(slots, 'space', 0, 0, axis_index_groups=[order], tiled=True)]
    ppermute x4, waiting for transfers between devices: 2.37 us -> 3.34 us  [over_space(): return lax.ppermute(block, ('space', 'chan'), route)]
    ppermute x4, starting transfers between devices: 11.7 us -> 10.8 us  [over_space(): return lax.ppermute(block, ('space', 'chan'), route)]
  transfers between devices with their start and end apart: 11 -> 11, of which waited for: 6 -> 6; matrix products, arithmetic and copies ran while one was open for 0% -> 0% of each run, Pallas kernels for 26% -> 25%
where the time goes in v9:
time: 89.5 us; the launch traced here: 88.9 us
  starting transfers between devices  37.2 us (42%)
  Pallas kernels  35.7 us (40%)
  waiting for transfers between devices  15.2 us (17%)
    pallas_call x7, Pallas kernels, run(): return call(*placed)  35.7 us
    all_to_all x3, starting transfers between devices, to_all(): lax.all_to_all(slots, 'space', 0, 0, axis_index_groups=[order], tiled=True)  25.3 us
    ppermute x4, starting transfers between devices, over_space(): return lax.ppermute(block, ('space', 'chan'), route)  10.8 us
    all_to_all x3, waiting for transfers between devices, to_all(): lax.all_to_all(slots, 'space', 0, 0, axis_index_groups=[order], tiled=True)  10.7 us
    ppermute x4, waiting for transfers between devices, over_space(): return lax.ppermute(block, ('space', 'chan'), route)  3.34 us
  transfers between devices with their start and end apart: 11, of which 6 were waited for; matrix products, arithmetic and copies ran while one was open for 0% of the time, Pallas kernels for 25%

profile of v9, /device:TPU:0, one launch (start us, length us, event | category | flops | bytes accessed | tf_op | source)
XLA Modules:
  0.0 88.9 jit_solution(13079639866431042019)
XLA Ops:
  0.6 2.4 %shard_map.93 = bf16[16,128,128]{2,1,0:T(8,128)(2,1)} custom-call(s32[1,26]{1,0:T(1,128)} %near_ref.3, s32[8,64]{1,0:T(8,128)} %heights_hbm.3, bf16[8,64,512]{2,1,0:T(8,128)(2,1)} %bitcast.20), custom_call_target="tpu_custom_call" | custom-call | bytes 4194304 | tf_op jit(solution)/shard_map/pallas_call | solution.py:52
  3.1 0.5 collective-permute-start
  3.6 9.8 %all-to-all-start = ((bf16[16,128,128]{2,1,0:T(8,128)(2,1)}), bf16[16,128,128]{2,1,0:T(8,128)(2,1)S(1)}, u32[]{:S(2)}, u32[]{:S(2)}) async-start(bf16[16,128,128]{2,1,0:T(8,128)(2,1)} %shard_map.93), calls=%async_computation | async-start | bytes 1048576 | tf_op jit(solution)/shard_map/all_to_all | solution.py:803
  13.4 0.0 collective-permute-done.other_hbm
  13.4 11.5 %shard_map.94 = (bf16[18,288,256]{2,1,0:T(8,128)(2,1)}, bf16[4096,128]{1,0:T(8,128)(2,1)}, f32[4096,128]{1,0:T(8,128)}, f32[4096,128]{1,0:T(8,128)}, bf16[3456,1...) custom-call(s32[1]{0:T(128)} %bitcast.core_ref, bf16[27,128,128]{2,1,0:T(8,128)(2,1)} %conv_hbm.3, ...), custom_call_target="tpu_custom_call" | custom-call | flops 5368709120 | bytes 4194304 | tf_op jit(solution)/shard_map/pallas_call | solution.py:52
  25.0 0.0 copy-start
  25.0 1.5 %all-to-all-done.own_ref = bf16[16,128,128]{2,1,0:T(8,128)(2,1)S(1)} async-done(((bf16[16,128,128]{2,1,0:T(8,128)(2,1)}), bf16[16,128,128]{2,1,0:T(8,128)(2,1)S(1)}, u32[]{:S(2)}, u32[]{:S(2)}) %all-to-all-start) | async-done | bytes 524320 | tf_op jit(solution)/shard_map/all_to_all | solution.py:803
  26.4 0.0 collective-permute-start.1
  26.4 1.9 %shard_map.95 = (bf16[3456,128]{1,0:T(8,128)(2,1)S(1)}, f32[4096,128]{1,0:T(8,128)S(1)}) custom-call(bf16[3456,128]{1,0:T(8,128)(2,1)} %get-tuple-element.34.taps_hbm, f32[4096,128]{1,0:T(8,128)} %get-tuple-element.35.inner_hbm), custom_call_target="tpu_custom_call" | custom-call | bytes 4194304 | tf_op jit(solution)/shard_map/pallas_call | solution.py:52
  28.3 0.0 collective-permute-done.1.other_ref
  28.3 0.0 copy-done
  28.3 8.5 %shard_map.96 = (bf16[16,184,128]{2,1,0:T(8,128)(2,1)}, bf16[4,256,128]{2,1,0:T(8,128)(2,1)S(1)}, bf16[512,128]{1,0:T(8,128)(2,1)}, bf16[4096,128]{1,0:T(8,128)(2,1)}) custom-call(s32[1,26]{1,0:T(1,128)S(1)} %copy-done, s32[1]{0:T(128)} %bitcast.core_ref, s32[1]{0:T(128)} %bitcast.1.at_ref, bf16[16,128,128]{2,1,0:T(8,128)(2,1)S(1)} %all-to-all-done.own_ref, ...), custom_call_target="tpu_custom_call" | custom-call | flops 5368709120 | bytes 4194304 | tf_op jit(solution)/shard_map/pallas_call | solution.py:52
  36.8 6.9 %all-to-all-start.1 = ((bf16[16,184,128]{2,1,0:T(8,128)(2,1)}), bf16[16,184,128]{2,1,0:T(8,128)(2,1)S(1)}, u32[]{:S(2)}, u32[]{:S(2)}) async-start(bf16[16,184,128]{2,1,0:T(8,128)(2,1)} %get-tuple-element.43), calls=%async_computation.1 | async-start | bytes 1507328 | tf_op jit(solution)/shard_map/all_to_all | solution.py:803
  43.8 2.5 %collective-permute-start.5 = (bf16[256,128]{1,0:T(8,128)(2,1)S(1)}, bf16[256,128]{1,0:T(8,128)(2,1)S(1)}, u32[]{:S(2)}, u32[]{:S(2)}) collective-permute-start(bf16[256,128]{1,0:T(8,128)(2,1)S(1)} %get-tuple-element.54), channel_id=1, source_target_pairs={{0,8},{2,10},{4,12},{6,14},{8,16},{10,18},{12,20},{14,22},{16,24},... | collective-permute-start | bytes 196616 | tf_op jit(solution)/shard_map/ppermute | solution.py:794
  46.3 2.5 %collective-permute-start.4 = (bf16[256,128]{1,0:T(8,128)(2,1)S(1)}, bf16[256,128]{1,0:T(8,128)(2,1)S(1)}, u32[]{:S(2)}, u32[]{:S(2)}) collective-permute-start(bf16[256,128]{1,0:T(8,128)(2,1)S(1)} %get-tuple-element.55), channel_id=1, source_target_pairs={{0,6},{2,8},{4,10},{6,12},{8,14},{10,16},{12,18},{14,20},{16,22},{... | collective-permute-start | bytes 196616 | tf_op jit(solution)/shard_map/ppermute | solution.py:794
  48.7 3.4 %collective-permute-start.3 = (bf16[256,128]{1,0:T(8,128)(2,1)S(1)}, bf16[256,128]{1,0:T(8,128)(2,1)S(1)}, u32[]{:S(2)}, u32[]{:S(2)}) collective-permute-start(bf16[256,128]{1,0:T(8,128)(2,1)S(1)} %get-tuple-element.56), channel_id=1, source_target_pairs={{0,4},{2,6},{4,8},{6,10},{8,12},{10,14},{12,16},{14,18},{16,20},{1... | collective-permute-start | bytes 196616 | tf_op jit(solution)/shard_map/ppermute | solution.py:794
  52.1 2.5 %collective-permute-start.2 = (bf16[256,128]{1,0:T(8,128)(2,1)S(1)}, bf16[256,128]{1,0:T(8,128)(2,1)S(1)}, u32[]{:S(2)}, u32[]{:S(2)}) collective-permute-start(bf16[256,128]{1,0:T(8,128)(2,1)S(1)} %get-tuple-element.57), channel_id=1, source_target_pairs={{0,2},{2,4},{4,6},{6,8},{8,10},{10,12},{12,14},{14,16},{16,18},{18... | collective-permute-start | bytes 196616 | tf_op jit(solution)/shard_map/ppermute | solution.py:794
  54.6 2.6 %collective-permute-done.5 = bf16[256,128]{1,0:T(8,128)(2,1)S(1)} collective-permute-done((bf16[256,128]{1,0:T(8,128)(2,1)S(1)}, bf16[256,128]{1,0:T(8,128)(2,1)S(1)}, u32[]{:S(2)}, u32[]{:S(2)}) %collective-permute-start.5) | collective-permute-done | bytes 65568 | tf_op jit(solution)/shard_map/ppermute | solution.py:794
  57.2 0.0 collective-permute-done.4
  57.2 0.0 collective-permute-done.3
  57.2 0.8 collective-permute-done.2
  57.9 3.8 %all-to-all-done.1.slots_ref.own_ref = bf16[16,184,128]{2,1,0:T(8,128)(2,1)S(1)} async-done(((bf16[16,184,128]{2,1,0:T(8,128)(2,1)}), bf16[16,184,128]{2,1,0:T(8,128)(2,1)S(1)}, u32[]{:S(2)}, u32[]{:S(2)}) %all-to-all-start.1) | async-done | bytes 753696 | tf_op jit(solution)/shard_map/all_to_all | solution.py:803
  61.7 1.0 %shard_map.97 = bf16[16,176,128]{2,1,0:T(8,128)(2,1)} custom-call(bf16[16,184,128]{2,1,0:T(8,128)(2,1)S(1)} %all-to-all-done.1.slots_ref.own_ref), custom_call_target="tpu_custom_call" | custom-call | bytes 4194304 | tf_op jit(solution)/shard_map/pallas_call | solution.py:52
  62.7 8.6 %all-to-all-start.2 = ((bf16[16,176,128]{2,1,0:T(8,128)(2,1)}), bf16[16,176,128]{2,1,0:T(8,128)(2,1)S(1)}, u32[]{:S(2)}, u32[]{:S(2)}) async-start(bf16[16,176,128]{2,1,0:T(8,128)(2,1)} %shard_map.97), calls=%async_computation.2 | async-start | bytes 1441792 | tf_op jit(solution)/shard_map/all_to_all | solution.py:803
  71.3 0.1 collective-permute-start.7
  71.4 0.5 collective-permute-start.6
  71.9 1.1 %collective-permute-done.6.other_ref = bf16[16,8,128]{2,1,0:T(8,128)(2,1)S(1)} collective-permute-done((bf16[16,8,128]{2,1,0:T(8,128)(2,1)S(1)}, bf16[16,8,128]{2,1,0:T(8,128)(2,1)S(1)}, u32[]{:S(2)}, u32[]{:S(2)}) %collective-permute-start.6) | collective-permute-done | bytes 32800 | tf_op jit(solution)/shard_map/ppermute | solution.py:798
  73.0 0.0 collective-permute-done.7.other_faces_ref
  73.0 9.2 %shard_map.99 = bf16[8,64,512]{2,1,0:T(8,128)(2,1)} custom-call(s32[1,26]{1,0:T(1,128)S(1)} %copy-done, s32[1]{0:T(128)} %bitcast.core_ref, s32[1]{0:T(128)} %bitcast.1.at_ref, bf16[16,184,128]{2,1,0:T(8,128)(2,1)S(1)} %all-to-all-done.1.slots_ref.own_ref, bf16[16,8,128]{2,1,0:T(8,128)(2,1)S(1)} %collective-permute-done.6.other_ref, ...), custom_call_target="tpu_custom_call" | custom-call | flops 5368709120 | bytes 4194304 | tf_op jit(solution)/shard_map/pallas_call | solution.py:52
  82.1 5.5 %all-to-all-done.2 = bf16[16,176,128]{2,1,0:T(8,128)(2,1)S(1)} async-done(((bf16[16,176,128]{2,1,0:T(8,128)(2,1)}), bf16[16,176,128]{2,1,0:T(8,128)(2,1)S(1)}, u32[]{:S(2)}, u32[]{:S(2)}) %all-to-all-start.2) | async-done | bytes 720928 | tf_op jit(solution)/shard_map/all_to_all | solution.py:803
  87.6 1.2 %shard_map.98 = (f32[27,64,128]{2,1,0:T(8,128)}, f32[8,128,128]{2,1,0:T(8,128)}) custom-call(s32[1]{0:T(128)} %bitcast.core_ref, bf16[2816,128]{1,0:T(8,128)(2,1)S(1)} %bitcast.19), custom_call_target="tpu_custom_call" | custom-call | bytes 4194304 | tf_op jit(solution)/shard_map/pallas_call | solution.py:52
  (3 shorter events, 0.1 us)
Async XLA Ops:
  3.1 10.3 %collective-permute-start = (bf16[8,64,512]{2,1,0:T(8,128)(2,1)}, bf16[8,64,512]{2,1,0:T(8,128)(2,1)S(1)}, u32[]{:S(2)}, u32[]{:S(2)}) collective-permute-start(bf16[8,64,512]{2,1,0:T(8,128)(2,1)} %bitcast.21), channel_id=1, source_target_pairs={{0,1},{1,0},{2,3},{3,2},{4,5},{5,4},{6,7},{7,6},{8,9},{9,8},{10,11... | collective-permute-start | bytes 1572872 | tf_op jit(solution)/shard_map/ppermute | solution.py:798
  3.6 22.8 %all-to-all-start = ((bf16[16,128,128]{2,1,0:T(8,128)(2,1)}), bf16[16,128,128]{2,1,0:T(8,128)(2,1)S(1)}, u32[]{:S(2)}, u32[]{:S(2)}) async-start(bf16[16,128,128]{2,1,0:T(8,128)(2,1)} %shard_map.93), calls=%async_computation | async-start | bytes 1048576 | tf_op jit(solution)/shard_map/all_to_all | solution.py:803
  25.0 3.4 %copy-start = (s32[1,26]{1,0:T(1,128)S(1)}, s32[1,26]{1,0:T(1,128)}, u32[]{:S(2)}) copy-start(s32[1,26]{1,0:T(1,128)} %near_ref.3) | copy-start | bytes 316
  26.4 1.9 %collective-permute-start.1 = (bf16[16,128,128]{2,1,0:T(8,128)(2,1)S(1)}, bf16[16,128,128]{2,1,0:T(8,128)(2,1)S(1)}, u32[]{:S(2)}, u32[]{:S(2)}) collective-permute-start(bf16[16,128,128]{2,1,0:T(8,128)(2,1)S(1)} %all-to-all-done.own_ref), channel_id=1, source_target_pairs={{0,1},{1,0},{2,3},{3,2},{4,5},{5,4},{6,7},{7,6},{8,9},{9,8},{10,11... | collective-permute-start | bytes 1572872 | tf_op jit(solution)/shard_map/ppermute | solution.py:798
  36.8 24.9 %all-to-all-start.1 = ((bf16[16,184,128]{2,1,0:T(8,128)(2,1)}), bf16[16,184,128]{2,1,0:T(8,128)(2,1)S(1)}, u32[]{:S(2)}, u32[]{:S(2)}) async-start(bf16[16,184,128]{2,1,0:T(8,128)(2,1)} %get-tuple-element.43), calls=%async_computation.1 | async-start | bytes 1507328 | tf_op jit(solution)/shard_map/all_to_all | solution.py:803
  43.8 13.4 %collective-permute-start.5 = (bf16[256,128]{1,0:T(8,128)(2,1)S(1)}, bf16[256,128]{1,0:T(8,128)(2,1)S(1)}, u32[]{:S(2)}, u32[]{:S(2)}) collective-permute-start(bf16[256,128]{1,0:T(8,128)(2,1)S(1)} %get-tuple-element.54), channel_id=1, source_target_pairs={{0,8},{2,10},{4,12},{6,14},{8,16},{10,18},{12,20},{14,22},{16,24},... | collective-permute-start | bytes 196616 | tf_op jit(solution)/shard_map/ppermute | solution.py:794
  46.3 10.9 %collective-permute-start.4 = (bf16[256,128]{1,0:T(8,128)(2,1)S(1)}, bf16[256,128]{1,0:T(8,128)(2,1)S(1)}, u32[]{:S(2)}, u32[]{:S(2)}) collective-permute-start(bf16[256,128]{1,0:T(8,128)(2,1)S(1)} %get-tuple-element.55), channel_id=1, source_target_pairs={{0,6},{2,8},{4,10},{6,12},{8,14},{10,16},{12,18},{14,20},{16,22},{... | collective-permute-start | bytes 196616 | tf_op jit(solution)/shard_map/ppermute | solution.py:794
  48.7 8.4 %collective-permute-start.3 = (bf16[256,128]{1,0:T(8,128)(2,1)S(1)}, bf16[256,128]{1,0:T(8,128)(2,1)S(1)}, u32[]{:S(2)}, u32[]{:S(2)}) collective-permute-start(bf16[256,128]{1,0:T(8,128)(2,1)S(1)} %get-tuple-element.56), channel_id=1, source_target_pairs={{0,4},{2,6},{4,8},{6,10},{8,12},{10,14},{12,16},{14,18},{16,20},{1... | collective-permute-start | bytes 196616 | tf_op jit(solution)/shard_map/ppermute | solution.py:794
  52.1 5.8 %collective-permute-start.2 = (bf16[256,128]{1,0:T(8,128)(2,1)S(1)}, bf16[256,128]{1,0:T(8,128)(2,1)S(1)}, u32[]{:S(2)}, u32[]{:S(2)}) collective-permute-start(bf16[256,128]{1,0:T(8,128)(2,1)S(1)} %get-tuple-element.57), channel_id=1, source_target_pairs={{0,2},{2,4},{4,6},{6,8},{8,10},{10,12},{12,14},{14,16},{16,18},{18... | collective-permute-start | bytes 196616 | tf_op jit(solution)/shard_map/ppermute | solution.py:794
  62.7 25.0 %all-to-all-start.2 = ((bf16[16,176,128]{2,1,0:T(8,128)(2,1)}), bf16[16,176,128]{2,1,0:T(8,128)(2,1)S(1)}, u32[]{:S(2)}, u32[]{:S(2)}) async-start(bf16[16,176,128]{2,1,0:T(8,128)(2,1)} %shard_map.97), calls=%async_computation.2 | async-start | bytes 1441792 | tf_op jit(solution)/shard_map/all_to_all | solution.py:803
  71.3 1.7 %collective-permute-start.7 = (bf16[4,256,128]{2,1,0:T(8,128)(2,1)S(1)}, bf16[4,256,128]{2,1,0:T(8,128)(2,1)S(1)}, u32[]{:S(2)}, u32[]{:S(2)}) collective-permute-start(bf16[4,256,128]{2,1,0:T(8,128)(2,1)S(1)} %pad_maximum_fusion.own_faces_ref), channel_id=1, source_target_pairs={{0,1},{1,0},{2,3},{3,2},{4,5},{5,4},{6,7},{7,6},{8,9},{9,8},{10,11... | collective-permute-start | bytes 786440 | tf_op jit(solution)/shard_map/ppermute | solution.py:798
  71.4 1.6 %collective-permute-start.6 = (bf16[16,8,128]{2,1,0:T(8,128)(2,1)S(1)}, bf16[16,8,128]{2,1,0:T(8,128)(2,1)S(1)}, u32[]{:S(2)}, u32[]{:S(2)}) collective-permute-start(bf16[16,8,128]{2,1,0:T(8,128)(2,1)S(1)} %slice.19), channel_id=1, source_target_pairs={{0,1},{1,0},{2,3},{3,2},{4,5},{5,4},{6,7},{7,6},{8,9},{9,8},{10,11... | collective-permute-start | bytes 98312 | tf_op jit(solution)/shard_map/ppermute | solution.py:798
